TPU v7x, 32 devices: a whole 2x2x4 slice. The times are simulated.
32 devices in a mesh: fibre: 8 (over y, x, core), group: 4 (over z).
Axes of the slice: x: 2, y: 2, z: 4, core: 2. Of those that a mesh axis runs over, the one named last changes fastest.
Arguments:
- tensor: float32 [512, 49152], P('fibre', 'group'), as said below
Outputs:
- basis: float32 [512, 49152], P('fibre', 'group')
- factor: float32 [512, 512], replicated
Inputs may be any that keep to these rules, and one draw needn't show every extreme that they name: `tensor`: entries are real-valued and the unfolding has full row rank.
All inputs are finite; a program needn't handle non-finite values.
Results may differ from a plain program's by a relative error of at most 0.00018.
Values sent between devices are 32-bit elements; how exact they have to be, the bound alone decides.
No kernel may reach another device: no remote copies, remote signals or barrier semaphores. Data moves between devices by JAX's collectives and lax.ppermute only.
A program may use at most 64 MiB of HBM per device.

v0:
```python
import functools

import jax
import jax.numpy as jnp
from jax import lax
from jax.experimental import pallas as pl
from jax.experimental.pallas import tpu as pltpu
from jax.sharding import PartitionSpec as P

LANES = 128
SUB = 8
PART = 32
MIB = 1024 * 1024


def split(x):
    high = x.astype(jnp.bfloat16)
    return high, (x - high.astype(jnp.float32)).astype(jnp.bfloat16)


def dot3(a, b, dims):
    (ah, al), (bh, bl) = a, b
    one = functools.partial(
        lax.dot_general, dimension_numbers=(dims, ((), ())), preferred_element_type=jnp.float32
    )
    return one(ah, bh) + (one(ah, bl) + one(al, bh))


def dot_full(a, b, dims):
    return lax.dot_general(
        a, b, (dims, ((), ())), precision=lax.Precision.HIGHEST, preferred_element_type=jnp.float32
    )


def packed_blocks(m):
    return [
        (r, c)
        for r in range(0, m, PART)
        for c in range(0, r + PART, LANES)
    ]


def gram_kernel(scale, x_ref, out_ref, high, low):
    m = x_ref.shape[0]
    half = m // 2
    high[...], low[...] = split(x_ref[...])
    blocks = packed_blocks(m)
    for start in (0, half):
        rows, upto = slice(start, start + half), slice(0, start + half)
        g = dot3((high[rows, :], low[rows, :]), (high[upto, :], low[upto, :]), ((1,), (1,))) * scale
        for i, (r, c) in enumerate(blocks):
            if start <= r < start + half:
                out_ref[i * PART : (i + 1) * PART, :] = g[r - start : r - start + PART, c : c + LANES]


def gram_packed(x, scale):
    m, n = x.shape
    return pl.pallas_call(
        functools.partial(gram_kernel, scale),
        out_shape=jax.ShapeDtypeStruct((len(packed_blocks(m)) * PART, LANES), jnp.float32),
        scratch_shapes=[pltpu.VMEM((m, n), jnp.bfloat16)] * 2,
        compiler_params=pltpu.CompilerParams(vmem_limit_bytes=32 * MIB),
        cost_estimate=pl.CostEstimate(
            flops=6 * m * m * n * 3 // 4, bytes_accessed=4 * m * n, transcendentals=0
        ),
        name="gram",
    )(x)


def along_lanes(v, j):
    return jnp.broadcast_to(v[:, j : j + 1], (SUB, LANES))


def along_sublanes(v, s):
    return jnp.broadcast_to(v[s : s + 1, :], (SUB, LANES))


def factor_block(x, z):
    sub = lax.broadcasted_iota(jnp.int32, (SUB, LANES), 0)
    for g in range(len(x)):
        cols = [along_lanes(x[g], SUB * g + t) for t in range(SUB)]
        x_rows, z_rows, inverses, r = [], [], [], {}
        xg, zg = x[g], z[g]
        for t in range(SUB):
            inverse = lax.rsqrt(along_sublanes(cols[t], t))
            m = jnp.where(sub > t, cols[t] * inverse, 0.0)
            x_row, z_row = along_sublanes(xg, t) * inverse, along_sublanes(zg, t) * inverse
            xg = jnp.where(sub == t, x_row, xg - m * x_row)
            zg = jnp.where(sub == t, z_row, zg - m * z_row)
            for u in range(t + 1, SUB):
                r[t, u] = along_sublanes(cols[u], t) * inverse
                cols[u] = cols[u] - m * r[t, u]
            x_rows.append(x_row)
            z_rows.append(z_row)
            inverses.append(inverse)
        x[g], z[g] = xg, zg
        for h in range(g + 1, len(x)):
            cols = [along_lanes(x[h], SUB * g + t) for t in range(SUB)]
            for t in range(SUB):
                cols[t] = cols[t] * inverses[t]
                for u in range(t + 1, SUB):
                    cols[u] = cols[u] - cols[t] * r[t, u]
                x[h] = x[h] - cols[t] * x_rows[t]
                z[h] = z[h] - cols[t] * z_rows[t]
    return jnp.concatenate(x, 0), jnp.concatenate(z, 0)


def factor_kernel(m, g_ref, l_ref, w_ref, a_ref):
    for i, (r, c) in enumerate(packed_blocks(m)):
        a_ref[r : r + PART, c : c + LANES] = g_ref[i * PART : (i + 1) * PART, :]
    l_ref[...] = jnp.zeros((m, m), jnp.float32)
    w_ref[...] = jnp.zeros((m, m), jnp.float32)
    row = lax.broadcasted_iota(jnp.int32, (LANES, LANES), 0)
    lane = lax.broadcasted_iota(jnp.int32, (LANES, LANES), 1)
    groups = range(0, LANES, SUB)
    for k in range(0, m, LANES):
        ks = slice(k, k + LANES)
        x = [a_ref[k + s : k + s + SUB, ks] for s in groups]
        z = [(lane[s : s + SUB] == row[s : s + SUB]).astype(jnp.float32) for s in groups]
        upper, inverse = factor_block(x, z)
        l_ref[ks, ks] = jnp.where(row >= lane, upper.T, 0.0)
        w_ref[ks, ks] = inverse
        if k + LANES < m:
            rest = slice(k + LANES, m)
            panel = dot_full(a_ref[rest, ks], inverse, ((1,), (1,)))
            l_ref[rest, ks] = panel
            a_ref[rest, rest] = a_ref[rest, rest] - dot_full(panel, panel, ((1,), (1,)))
    for i in range(LANES, m, LANES):
        rows = slice(i, i + LANES)
        acc = dot_full(l_ref[rows, 0:i], w_ref[0:i, 0:i], ((1,), (0,)))
        w_ref[rows, 0:i] = -dot_full(w_ref[rows, rows], acc, ((1,), (0,)))


def factor_and_inverse(packed, m):
    return pl.pallas_call(
        functools.partial(factor_kernel, m),
        out_shape=[jax.ShapeDtypeStruct((m, m), jnp.float32)] * 2,
        scratch_shapes=[pltpu.VMEM((m, m), jnp.float32)],
        compiler_params=pltpu.CompilerParams(vmem_limit_bytes=32 * MIB),
        cost_estimate=pl.CostEstimate(flops=12 * m * m * m, bytes_accessed=12 * m * m, transcendentals=m),
        name="factor",
    )(packed)


def apply_kernel(w_ref, x_ref, out_ref):
    m = w_ref.shape[0]
    half = m // 2
    x = split(x_ref[...])
    w = split(w_ref[...])
    for start in (0, half):
        rows, upto = slice(start, start + half), slice(0, start + half)
        out_ref[rows, :] = dot3([v[rows, upto] for v in w], [v[upto, :] for v in x], ((1,), (0,)))


def apply_inverse(w, x):
    m, n = x.shape
    tile = n // 3
    return pl.pallas_call(
        apply_kernel,
        grid=(n // tile,),
        in_specs=[
            pl.BlockSpec((m, m), lambda i: (0, 0)),
            pl.BlockSpec((m, tile), lambda i: (0, i)),
        ],
        out_specs=pl.BlockSpec((m, tile), lambda i: (0, i)),
        out_shape=jax.ShapeDtypeStruct((m, n), jnp.float32),
        compiler_params=pltpu.CompilerParams(vmem_limit_bytes=32 * MIB),
        cost_estimate=pl.CostEstimate(
            flops=6 * m * m * n * 3 // 4, bytes_accessed=8 * m * n, transcendentals=0
        ),
        name="apply",
    )(w, x)


def permute(x, axis, bits):
    return lax.ppermute(x, axis, [(i, i ^ bits) for i in range(lax.axis_size(axis))])


def tree_sum(terms):
    while len(terms) > 1:
        terms = [a + b for a, b in zip(terms[::2], terms[1::2], strict=True)]
    return terms[0]


def sum_everywhere(packed):
    chips = lax.axis_size("fibre") // 2
    me = lax.axis_index("fibre")
    core, chip = lax.rem(me, 2), lax.div(me, 2)
    pieces = packed.reshape(2, chips, -1, LANES)
    mine = lax.dynamic_index_in_dim(pieces, core, 0, keepdims=False)
    theirs = lax.dynamic_index_in_dim(pieces, 1 - core, 0, keepdims=False)
    mine = mine + permute(theirs, "fibre", 1)
    piece = tree_sum(
        [
            lax.dynamic_index_in_dim(mine, chip, 0, keepdims=False)
            if k == 0
            else permute(lax.dynamic_index_in_dim(mine, chip ^ k, 0, keepdims=False), "fibre", 2 * k)
            for k in range(chips)
        ]
    )
    piece = tree_sum(
        [piece if k == 0 else permute(piece, "group", k) for k in range(lax.axis_size("group"))]
    )
    gathered = jnp.zeros((chips, *piece.shape), piece.dtype)
    for k in range(chips):
        part = piece if k == 0 else permute(piece, "fibre", 2 * k)
        gathered = lax.dynamic_update_index_in_dim(gathered, part, chip ^ k, 0)
    other = permute(gathered, "fibre", 1)
    low = jnp.where(core == 0, gathered, other)
    high = jnp.where(core == 0, other, gathered)
    return jnp.stack([low, high]).reshape(packed.shape)


def local(tensor):
    columns = lax.all_to_all(tensor, "fibre", split_axis=1, concat_axis=0, tiled=True)
    m, n = columns.shape
    total_cols = n * lax.axis_size("fibre") * lax.axis_size("group")
    total = sum_everywhere(gram_packed(columns, 1.0 / total_cols))
    factor, inverse = factor_and_inverse(total, m)
    solved = apply_inverse(inverse, columns)
    basis = lax.all_to_all(solved, "fibre", split_axis=0, concat_axis=1, tiled=True)
    return (basis, factor)


def solution(mesh):
    return jax.shard_map(
        local,
        mesh=mesh,
        in_specs=(P("fibre", "group"),),
        out_specs=(P("fibre", "group"), P()),
        check_vma=False,
    )
```

profile of v0, /device:TPU:0, one launch (start us, length us, event | category | flops | bytes accessed | tf_op | source)
XLA Modules:
  0.0 148.3 jit_solution(8776993981055892907)
XLA Ops:
  0.6 3.8 %copy.8 = f32[8,8,8,1536]{3,2,0,1:T(8,128)} copy(f32[8,8,8,1536]{3,2,1,0:T(8,128)} %bitcast.47) | data formatting | bytes 6291456 | tf_op jit(solution)/shard_map/all_to_all | solution.py:215
  4.5 5.2 %all-to-all-start = ((f32[64,8,1536]{2,0,1:T(8,128)}), f32[64,8,1536]{2,0,1:T(8,128)S(1)}, u32[]{:S(2)}, u32[]{:S(2)}) async-start(f32[64,8,1536]{2,0,1:T(8,128)} %bitcast.45), calls=%async_computation | async-start | bytes 6291456 | tf_op jit(solution)/shard_map/all_to_all | solution.py:215
  9.6 37.9 %all-to-all-done = f32[64,8,1536]{2,0,1:T(8,128)S(1)} async-done(((f32[64,8,1536]{2,0,1:T(8,128)}), f32[64,8,1536]{2,0,1:T(8,128)S(1)}, u32[]{:S(2)}, u32[]{:S(2)}) %all-to-all-start) | async-done | bytes 3145760 | tf_op jit(solution)/shard_map/all_to_all | solution.py:215
  47.5 2.0 %gram.1 = f32[1280,128]{1,0:T(8,128)S(1)} custom-call(f32[512,1536]{1,0:T(8,128)S(1)} %bitcast.39), custom_call_target="tpu_custom_call" | custom-call | flops 1811939328 | bytes 3145728 | tf_op jit(solution)/shard_map/gram/pallas_call | solution.py:58
  49.6 0.8 copy-done
  50.5 1.7 %collective-permute-done = f32[4,160,128]{2,1,0:T(8,128)} collective-permute-done((f32[4,160,128]{2,1,0:T(8,128)S(1)}, f32[4,160,128]{2,1,0:T(8,128)}, u32[]{:S(2)}, u32[]{:S(2)}) %collective-permute-start) | collective-permute-done | bytes 327712 | tf_op jit(solution)/shard_map/ppermute | solution.py:176
  52.2 1.1 bitcast_add_fusion
  54.7 1.4 collective-permute-start.2
  56.0 1.5 %collective-permute-start.1 = (f32[160,128]{1,0:T(8,128)}, f32[160,128]{1,0:T(8,128)}, u32[]{:S(2)}, u32[]{:S(2)}) collective-permute-start(f32[160,128]{1,0:T(8,128)} %get-tuple-element.12), channel_id=1, source_target_pairs={{0,8},{4,12},{8,0},{12,4},{16,24},{20,28},{24,16},{28,20},{1,9},{5... | collective-permute-start | bytes 245768 | tf_op jit(solution)/shard_map/ppermute | solution.py:176
  57.5 2.9 %collective-permute-done.3 = f32[160,128]{1,0:T(8,128)S(1)} collective-permute-done((f32[160,128]{1,0:T(8,128)}, f32[160,128]{1,0:T(8,128)S(1)}, u32[]{:S(2)}, u32[]{:S(2)}) %collective-permute-start.3) | collective-permute-done | bytes 81952 | tf_op jit(solution)/shard_map/ppermute | solution.py:176
  60.9 0.9 fusion
  61.9 3.7 %collective-permute-start.6 = (f32[160,128]{1,0:T(8,128)S(1)}, f32[160,128]{1,0:T(8,128)S(1)}, u32[]{:S(2)}, u32[]{:S(2)}) collective-permute-start(f32[160,128]{1,0:T(8,128)S(1)} %fusion), channel_id=1, source_target_pairs={{0,3},{1,2},{2,1},{3,0},{4,7},{5,6},{6,5},{7,4},{8,11},{9,10},{10,... | collective-permute-start | bytes 245768 | tf_op jit(solution)/shard_map/ppermute | solution.py:176
  66.3 2.4 %collective-permute-done.6 = f32[160,128]{1,0:T(8,128)S(1)} collective-permute-done((f32[160,128]{1,0:T(8,128)S(1)}, f32[160,128]{1,0:T(8,128)S(1)}, u32[]{:S(2)}, u32[]{:S(2)}) %collective-permute-start.6) | collective-permute-done | bytes 81952 | tf_op jit(solution)/shard_map/ppermute | solution.py:176
  68.7 3.1 %collective-permute-done.5 = f32[160,128]{1,0:T(8,128)S(1)} collective-permute-done((f32[160,128]{1,0:T(8,128)S(1)}, f32[160,128]{1,0:T(8,128)S(1)}, u32[]{:S(2)}, u32[]{:S(2)}) %collective-permute-start.5) | collective-permute-done | bytes 81952 | tf_op jit(solution)/shard_map/ppermute | solution.py:176
  71.9 2.0 %collective-permute-start.7 = (f32[160,128]{1,0:T(8,128)S(1)}, f32[160,128]{1,0:T(8,128)S(1)}, u32[]{:S(2)}, u32[]{:S(2)}) collective-permute-start(f32[160,128]{1,0:T(8,128)S(1)} %get-tuple-element.7), channel_id=1, source_target_pairs={{0,8},{4,12},{8,0},{12,4},{16,24},{20,28},{24,16},{28,20},{1,9},{5... | collective-permute-start | bytes 245768 | tf_op jit(solution)/shard_map/ppermute | solution.py:176
  74.1 1.4 collective-permute-start.9
  75.4 1.1 collective-permute-done.7
  76.5 3.2 %collective-permute-done.8 = f32[160,128]{1,0:T(8,128)S(1)} collective-permute-done((f32[160,128]{1,0:T(8,128)S(1)}, f32[160,128]{1,0:T(8,128)S(1)}, u32[]{:S(2)}, u32[]{:S(2)}) %collective-permute-start.8) | collective-permute-done | bytes 81952 | tf_op jit(solution)/shard_map/ppermute | solution.py:176
  79.8 1.7 %collective-permute-done.10 = f32[4,160,128]{2,1,0:T(8,128)} collective-permute-done((f32[4,160,128]{2,1,0:T(8,128)S(1)}, f32[4,160,128]{2,1,0:T(8,128)}, u32[]{:S(2)}, u32[]{:S(2)}) %collective-permute-start.10) | collective-permute-done | bytes 327712 | tf_op jit(solution)/shard_map/ppermute | solution.py:176
  81.5 1.0 select_bitcast_fusion.1
  82.6 20.4 %factor.1 = (f32[512,512]{1,0:T(8,128)}, f32[512,512]{1,0:T(8,128)S(1)}) custom-call(f32[1280,128]{1,0:T(8,128)S(1)} %bitcast.44), custom_call_target="tpu_custom_call" | custom-call | flops 1610612736 | bytes 3145728 | tf_op jit(solution)/shard_map/factor/pallas_call | solution.py:135
  103.1 2.8 %apply.1 = f32[512,1536]{1,0:T(8,128)S(1)} custom-call(f32[512,512]{1,0:T(8,128)S(1)} %get-tuple-element.4.w_ref, f32[512,1536]{1,0:T(8,128)S(1)} %bitcast.40), custom_call_target="tpu_custom_call" | custom-call | flops 1811939328 | bytes 6291456 | tf_op jit(solution)/shard_map/apply/pallas_call | solution.py:158
  105.9 40.4 %all_to_all.38 = f32[8,64,1536]{2,1,0:T(8,128)S(1)} all-to-all(f32[8,64,1536]{2,1,0:T(8,128)S(1)} %bitcast.41), channel_id=1, replica_groups=mesh['fibre'=8,'group'=4] {'fibre'}, dimensions={0} | all-to-all | bytes 6291456 | tf_op jit(solution)/shard_map/all_to_all | solution.py:221
  146.3 1.9 %copy.6 = f32[8,8,8,1536]{3,2,0,1:T(8,128)} copy(f32[8,8,8,1536]{3,2,1,0:T(8,128)S(1)} %bitcast.46) | data formatting | bytes 6291456 | tf_op jit(solution)/shard_map/all_to_all | solution.py:221
  (19 shorter events, 3.1 us)
Async XLA Ops:
  4.5 43.1 %all-to-all-start = ((f32[64,8,1536]{2,0,1:T(8,128)}), f32[64,8,1536]{2,0,1:T(8,128)S(1)}, u32[]{:S(2)}, u32[]{:S(2)}) async-start(f32[64,8,1536]{2,0,1:T(8,128)} %bitcast.45), calls=%async_computation | async-start | bytes 6291456 | tf_op jit(solution)/shard_map/all_to_all | solution.py:215
  49.5 0.8 copy-start
  50.4 1.8 %collective-permute-start = (f32[4,160,128]{2,1,0:T(8,128)S(1)}, f32[4,160,128]{2,1,0:T(8,128)}, u32[]{:S(2)}, u32[]{:S(2)}) collective-permute-start(f32[4,160,128]{2,1,0:T(8,128)S(1)} %dynamic-slice_bitcast_fusion), channel_id=1, source_target_pairs={{0,4},{4,0},{8,12},{12,8},{16,20},{20,16},{24,28},{28,24},{1,5},{5... | collective-permute-start | bytes 983048 | tf_op jit(solution)/shard_map/ppermute | solution.py:176
  54.1 6.4 %collective-permute-start.3 = (f32[160,128]{1,0:T(8,128)}, f32[160,128]{1,0:T(8,128)S(1)}, u32[]{:S(2)}, u32[]{:S(2)}) collective-permute-start(f32[160,128]{1,0:T(8,128)} %get-tuple-element.10), channel_id=1, source_target_pairs={{0,24},{4,28},{8,16},{12,20},{16,8},{20,12},{24,0},{28,4},{1,25},{... | collective-permute-start | bytes 245768 | tf_op jit(solution)/shard_map/ppermute | solution.py:176
  54.7 6.3 %collective-permute-start.2 = (f32[160,128]{1,0:T(8,128)}, f32[160,128]{1,0:T(8,128)}, u32[]{:S(2)}, u32[]{:S(2)}) collective-permute-start(f32[160,128]{1,0:T(8,128)} %get-tuple-element.11), channel_id=1, source_target_pairs={{0,16},{4,20},{8,24},{12,28},{16,0},{20,4},{24,8},{28,12},{1,17},{... | collective-permute-start | bytes 245768 | tf_op jit(solution)/shard_map/ppermute | solution.py:176
  56.0 4.9 %collective-permute-start.1 = (f32[160,128]{1,0:T(8,128)}, f32[160,128]{1,0:T(8,128)}, u32[]{:S(2)}, u32[]{:S(2)}) collective-permute-start(f32[160,128]{1,0:T(8,128)} %get-tuple-element.12), channel_id=1, source_target_pairs={{0,8},{4,12},{8,0},{12,4},{16,24},{20,28},{24,16},{28,20},{1,9},{5... | collective-permute-start | bytes 245768 | tf_op jit(solution)/shard_map/ppermute | solution.py:176
  61.9 6.8 %collective-permute-start.6 = (f32[160,128]{1,0:T(8,128)S(1)}, f32[160,128]{1,0:T(8,128)S(1)}, u32[]{:S(2)}, u32[]{:S(2)}) collective-permute-start(f32[160,128]{1,0:T(8,128)S(1)} %fusion), channel_id=1, source_target_pairs={{0,3},{1,2},{2,1},{3,0},{4,7},{5,6},{6,5},{7,4},{8,11},{9,10},{10,... | collective-permute-start | bytes 245768 | tf_op jit(solution)/shard_map/ppermute | solution.py:176
  65.6 6.2 %collective-permute-start.5 = (f32[160,128]{1,0:T(8,128)S(1)}, f32[160,128]{1,0:T(8,128)S(1)}, u32[]{:S(2)}, u32[]{:S(2)}) collective-permute-start(f32[160,128]{1,0:T(8,128)S(1)} %fusion), channel_id=1, source_target_pairs={{0,2},{1,3},{2,0},{3,1},{4,6},{5,7},{6,4},{7,5},{8,10},{9,11},{10,... | collective-permute-start | bytes 245768 | tf_op jit(solution)/shard_map/ppermute | solution.py:176
  65.6 6.2 %collective-permute-start.4 = (f32[160,128]{1,0:T(8,128)S(1)}, f32[160,128]{1,0:T(8,128)S(1)}, u32[]{:S(2)}, u32[]{:S(2)}) collective-permute-start(f32[160,128]{1,0:T(8,128)S(1)} %fusion), channel_id=1, source_target_pairs={{0,1},{1,0},{2,3},{3,2},{4,5},{5,4},{6,7},{7,6},{8,9},{9,8},{10,11... | collective-permute-start | bytes 245768 | tf_op jit(solution)/shard_map/ppermute | solution.py:176
  71.9 4.6 %collective-permute-start.7 = (f32[160,128]{1,0:T(8,128)S(1)}, f32[160,128]{1,0:T(8,128)S(1)}, u32[]{:S(2)}, u32[]{:S(2)}) collective-permute-start(f32[160,128]{1,0:T(8,128)S(1)} %get-tuple-element.7), channel_id=1, source_target_pairs={{0,8},{4,12},{8,0},{12,4},{16,24},{20,28},{24,16},{28,20},{1,9},{5... | collective-permute-start | bytes 245768 | tf_op jit(solution)/shard_map/ppermute | solution.py:176
  73.8 5.9 %collective-permute-start.8 = (f32[160,128]{1,0:T(8,128)S(1)}, f32[160,128]{1,0:T(8,128)S(1)}, u32[]{:S(2)}, u32[]{:S(2)}) collective-permute-start(f32[160,128]{1,0:T(8,128)S(1)} %get-tuple-element.7), channel_id=1, source_target_pairs={{0,16},{4,20},{8,24},{12,28},{16,0},{20,4},{24,8},{28,12},{1,17},{... | collective-permute-start | bytes 245768 | tf_op jit(solution)/shard_map/ppermute | solution.py:176
  74.1 5.6 %collective-permute-start.9 = (f32[160,128]{1,0:T(8,128)S(1)}, f32[160,128]{1,0:T(8,128)S(1)}, u32[]{:S(2)}, u32[]{:S(2)}) collective-permute-start(f32[160,128]{1,0:T(8,128)S(1)} %get-tuple-element.7), channel_id=1, source_target_pairs={{0,24},{4,28},{8,16},{12,20},{16,8},{20,12},{24,0},{28,4},{1,25},{... | collective-permute-start | bytes 245768 | tf_op jit(solution)/shard_map/ppermute | solution.py:176
  79.7 1.8 %collective-permute-start.10 = (f32[4,160,128]{2,1,0:T(8,128)S(1)}, f32[4,160,128]{2,1,0:T(8,128)}, u32[]{:S(2)}, u32[]{:S(2)}) collective-permute-start(f32[4,160,128]{2,1,0:T(8,128)S(1)} %bitcast_dynamic-update-slice_fusion), channel_id=1, source_target_pairs={{0,4},{4,0},{8,12},{12,8},{16,20},{20,16},{24,28},{28,24},{1,5},{5... | collective-permute-start | bytes 983048 | tf_op jit(solution)/shard_map/ppermute | solution.py:176
where the time goes:
time: 149 us; the launch traced here: 148 us
  waiting for transfers between devices  54.4 us (37%)
  blocking collectives  40.4 us (27%)
  Pallas kernels  25.3 us (17%)
  starting transfers between devices  16.8 us (11%)
  local copies, waits for them, and re-layouts  7.38 us (5%)
  other arithmetic  3.14 us (2%)
    all_to_all x1, blocking collectives, local(): lax.all_to_all(solved, 'fibre', split_axis=0, concat_axis=1, tiled=True)  40.4 us
    all_to_all x1, waiting for transfers between devices, local(): lax.all_to_all(tensor, 'fibre', split_axis=1, concat_axis=0, tiled=True)  37.9 us
    pallas_call x1, Pallas kernels, factor_and_inverse(): pl.pallas_call(functools.partial(factor_kernel, m), out_shape=[jax.ShapeD...  20.4 us
    ppermute x11, waiting for transfers between devices, permute(): lax.ppermute(x, axis, [(i, i ^ bits) for i in range(lax.axis_size(axis))])  16.5 us
    ppermute x11, starting transfers between devices, permute(): lax.ppermute(x, axis, [(i, i ^ bits) for i in range(lax.axis_size(axis))])  11.6 us
    all_to_all x1, starting transfers between devices, local(): lax.all_to_all(tensor, 'fibre', split_axis=1, concat_axis=0, tiled=True)  5.17 us
    all_to_all x1, local copies, waits for them, and re-layouts, local(): lax.all_to_all(tensor, 'fibre', split_axis=1, concat_axis=0, tiled=True)  3.83 us
  transfers between devices with their start and end apart: 12, of which 9 were waited for; matrix products, arithmetic and copies ran while one was open for 0% of the time, Pallas kernels for 0%

commit v1 on v0

v1 whole, which is shorter than its diff:
```python
import functools

import jax
import jax.numpy as jnp
from jax import lax
from jax.experimental import pallas as pl
from jax.experimental.pallas import tpu as pltpu
from jax.sharding import PartitionSpec as P

LANES = 128
SUB = 8
PART = 32
MIB = 1024 * 1024


def split(x):
    high = x.astype(jnp.bfloat16)
    return high, (x - high.astype(jnp.float32)).astype(jnp.bfloat16)


def dot3(a, b, dims):
    (ah, al), (bh, bl) = a, b
    one = functools.partial(
        lax.dot_general, dimension_numbers=(dims, ((), ())), preferred_element_type=jnp.float32
    )
    return one(ah, bh) + (one(ah, bl) + one(al, bh))


def dot_full(a, b, dims):
    return lax.dot_general(
        a, b, (dims, ((), ())), precision=lax.Precision.HIGHEST, preferred_element_type=jnp.float32
    )


def packed_blocks(m):
    return [
        (r, c)
        for r in range(0, m, PART)
        for c in range(0, r + PART, LANES)
    ]


def fibre_index():
    return lax.axis_index("fibre")


def place_rows(parts, high, low):
    rows = parts[0].shape[0]
    me = fibre_index()
    for k, part in enumerate(parts):
        at = pl.ds(pl.multiple_of((me ^ k) * rows, rows), rows)
        high[at, :], low[at, :] = split(part[...])


def gram_kernel(scale, n, *refs):
    parts, (mine, theirs, high, low, packed) = refs[:n], refs[n:]
    m = high.shape[0]
    half = m // 2
    place_rows(parts, high, low)
    blocks = packed_blocks(m)
    for start in (0, half):
        rows, upto = slice(start, start + half), slice(0, start + half)
        g = dot3((high[rows, :], low[rows, :]), (high[upto, :], low[upto, :]), ((1,), (1,))) * scale
        for i, (r, c) in enumerate(blocks):
            if start <= r < start + half:
                packed[i * PART : (i + 1) * PART, :] = g[r - start : r - start + PART, c : c + LANES]
    me = fibre_index()
    piece = packed.shape[0] // n
    for k in range(0, n, 2):
        to = slice(k // 2 * piece, (k // 2 + 1) * piece)
        mine[to, :] = packed[pl.ds(pl.multiple_of(piece_of(me ^ k, n) * piece, SUB), piece), :]
        theirs[to, :] = packed[pl.ds(pl.multiple_of(piece_of(me ^ k ^ 1, n) * piece, SUB), piece), :]


def piece_of(device, n):
    return device


def gram_packed(parts, scale):
    rows, w = parts[0].shape
    n = len(parts)
    m = rows * n
    size = len(packed_blocks(m)) * PART
    half = jax.ShapeDtypeStruct((size // 2, LANES), jnp.float32)
    wide = jax.ShapeDtypeStruct((m, w), jnp.bfloat16)
    return pl.pallas_call(
        functools.partial(gram_kernel, scale, n),
        out_shape=[half, half, wide, wide],
        scratch_shapes=[pltpu.VMEM((size, LANES), jnp.float32)],
        compiler_params=pltpu.CompilerParams(vmem_limit_bytes=24 * MIB),
        cost_estimate=pl.CostEstimate(
            flops=6 * m * m * w * 3 // 4, bytes_accessed=4 * m * w, transcendentals=0
        ),
        name="gram",
    )(*parts)


def along_lanes(v, j):
    return jnp.broadcast_to(v[:, j : j + 1], (SUB, LANES))


def along_sublanes(v, s):
    return jnp.broadcast_to(v[s : s + 1, :], (SUB, LANES))


def factor_block(x, z):
    sub = lax.broadcasted_iota(jnp.int32, (SUB, LANES), 0)
    for g in range(len(x)):
        cols = [along_lanes(x[g], SUB * g + t) for t in range(SUB)]
        x_rows, z_rows, inverses, r = [], [], [], {}
        xg, zg = x[g], z[g]
        for t in range(SUB):
            inverse = lax.rsqrt(along_sublanes(cols[t], t))
            m = jnp.where(sub > t, cols[t] * inverse, 0.0)
            x_row, z_row = along_sublanes(xg, t) * inverse, along_sublanes(zg, t) * inverse
            xg = jnp.where(sub == t, x_row, xg - m * x_row)
            zg = jnp.where(sub == t, z_row, zg - m * z_row)
            for u in range(t + 1, SUB):
                r[t, u] = along_sublanes(cols[u], t) * inverse
                cols[u] = cols[u] - m * r[t, u]
            x_rows.append(x_row)
            z_rows.append(z_row)
            inverses.append(inverse)
        x[g], z[g] = xg, zg
        for h in range(g + 1, len(x)):
            cols = [along_lanes(x[h], SUB * g + t) for t in range(SUB)]
            for t in range(SUB):
                cols[t] = cols[t] * inverses[t]
                for u in range(t + 1, SUB):
                    cols[u] = cols[u] - cols[t] * r[t, u]
                x[h] = x[h] - cols[t] * x_rows[t]
                z[h] = z[h] - cols[t] * z_rows[t]
    return jnp.concatenate(x, 0), jnp.concatenate(z, 0)


def factor_kernel(m, n, *refs):
    pieces, (l_ref, w_ref, a_ref, packed) = refs[:n], refs[n:]
    piece = pieces[0].shape[0]
    me = fibre_index()
    for k, part in enumerate(pieces):
        packed[pl.ds(pl.multiple_of(piece_of(me ^ k, n) * piece, SUB), piece), :] = part[...]
    for i, (r, c) in enumerate(packed_blocks(m)):
        a_ref[r : r + PART, c : c + LANES] = packed[i * PART : (i + 1) * PART, :]
    l_ref[...] = jnp.zeros((m, m), jnp.float32)
    w_ref[...] = jnp.zeros((m, m), jnp.float32)
    row = lax.broadcasted_iota(jnp.int32, (LANES, LANES), 0)
    lane = lax.broadcasted_iota(jnp.int32, (LANES, LANES), 1)
    groups = range(0, LANES, SUB)
    for k in range(0, m, LANES):
        ks = slice(k, k + LANES)
        x = [a_ref[k + s : k + s + SUB, ks] for s in groups]
        z = [(lane[s : s + SUB] == row[s : s + SUB]).astype(jnp.float32) for s in groups]
        upper, inverse = factor_block(x, z)
        l_ref[ks, ks] = jnp.where(row >= lane, upper.T, 0.0)
        w_ref[ks, ks] = inverse
        if k + LANES < m:
            rest = slice(k + LANES, m)
            panel = dot_full(a_ref[rest, ks], inverse, ((1,), (1,)))
            l_ref[rest, ks] = panel
            a_ref[rest, rest] = a_ref[rest, rest] - dot_full(panel, panel, ((1,), (1,)))
    for i in range(LANES, m, LANES):
        rows = slice(i, i + LANES)
        acc = dot_full(l_ref[rows, 0:i], w_ref[0:i, 0:i], ((1,), (0,)))
        w_ref[rows, 0:i] = -dot_full(w_ref[rows, rows], acc, ((1,), (0,)))


def factor_and_inverse(pieces, m):
    n = len(pieces)
    return pl.pallas_call(
        functools.partial(factor_kernel, m, n),
        out_shape=[jax.ShapeDtypeStruct((m, m), jnp.float32)] * 2,
        scratch_shapes=[
            pltpu.VMEM((m, m), jnp.float32),
            pltpu.VMEM((n * pieces[0].shape[0], LANES), jnp.float32),
        ],
        compiler_params=pltpu.CompilerParams(vmem_limit_bytes=24 * MIB),
        cost_estimate=pl.CostEstimate(
            flops=160 * m * m * m, bytes_accessed=12 * m * m, transcendentals=m
        ),
        name="factor",
    )(*pieces)


def rows_of(w_ref, wide, ks, rows):
    me = fibre_index()
    for i, k in enumerate(ks):
        piece = w_ref[pl.ds(pl.multiple_of((me ^ k) * rows, rows), rows), :]
        high, low = split(piece)
        for half, value in zip(wide, (high, low), strict=True):
            half[i * rows : (i + 1) * rows, :] = value


def send_kernel(ks, w_ref, high, low, *refs):
    outs, wide = refs[: len(ks)], refs[len(ks) :]
    rows, width = outs[0].shape
    rows_of(w_ref, wide, ks, rows)
    for start in range(0, width, width // 2):
        cols = slice(start, start + width // 2)
        solved = dot3((wide[0][...], wide[1][...]), (high[:, cols], low[:, cols]), ((1,), (0,)))
        for i, out in enumerate(outs):
            out[:, cols] = solved[i * rows : (i + 1) * rows]


def rows_to_send(w, high, low, ks, rows):
    m, width = high.shape
    return pl.pallas_call(
        functools.partial(send_kernel, ks),
        out_shape=[jax.ShapeDtypeStruct((rows, width), jnp.float32)] * len(ks),
        scratch_shapes=[pltpu.VMEM((len(ks) * rows, m), jnp.bfloat16)] * 2,
        compiler_params=pltpu.CompilerParams(vmem_limit_bytes=24 * MIB),
        cost_estimate=pl.CostEstimate(
            flops=6 * len(ks) * rows * m * width, bytes_accessed=8 * m * width, transcendentals=0
        ),
        name="send_rows",
    )(w, high, low)


def keep_kernel(n, w_ref, high, low, *refs):
    parts, outs, (twin_high, twin_low), wide = refs[:n], refs[n : n + 4], refs[n + 4 : n + 6], refs[n + 6 :]
    rows, width = outs[0].shape
    rows_of(w_ref, wide, (0, 1), rows)
    place_rows(parts, twin_high, twin_low)
    for first, (h, l) in ((0, (high, low)), (2, (twin_high, twin_low))):
        for start in range(0, width, width // 2):
            cols = slice(start, start + width // 2)
            solved = dot3((wide[0][...], wide[1][...]), (h[:, cols], l[:, cols]), ((1,), (0,)))
            outs[first][:, cols] = solved[:rows]
            outs[first + 1][:, cols] = solved[rows:]


def rows_to_keep(w, high, low, twin):
    m, width = high.shape
    n = len(twin)
    rows = m // n
    return pl.pallas_call(
        functools.partial(keep_kernel, n),
        out_shape=[jax.ShapeDtypeStruct((rows, width), jnp.float32)] * 4,
        scratch_shapes=[pltpu.VMEM((m, width), jnp.bfloat16)] * 2 + [pltpu.VMEM((2 * rows, m), jnp.bfloat16)] * 2,
        compiler_params=pltpu.CompilerParams(vmem_limit_bytes=24 * MIB),
        cost_estimate=pl.CostEstimate(
            flops=24 * rows * m * width, bytes_accessed=8 * m * width, transcendentals=0
        ),
        name="keep_rows",
    )(w, high, low, *twin)


def permute(x, axis, bits):
    return lax.ppermute(x, axis, [(i, i ^ bits) for i in range(lax.axis_size(axis))])


def tree_sum(terms):
    while len(terms) > 1:
        terms = [a + b for a, b in zip(terms[::2], terms[1::2], strict=True)]
    return terms[0]


def after(x, *earlier):
    return lax.optimization_barrier((x, *earlier))[0]


def local(tensor):
    n = lax.axis_size("fibre")
    groups = lax.axis_size("group")
    chips = n // 2
    me = lax.axis_index("fibre")
    rows, wide = tensor.shape
    m, width = rows * n, wide // n
    opposite = n - 2

    def block(x, j):
        return lax.dynamic_slice(x, (0, j * width), (rows, width))

    far_first = sorted(range(1, n), key=lambda k: -k)
    parts = [block(tensor, me)] + [None] * (n - 1)
    for k in far_first:
        parts[k] = permute(block(tensor, me ^ k), "fibre", k)
    twin = [block(tensor, me ^ opposite)] + [None] * (n - 1)

    def send_twin(ks, *earlier):
        for k in ks:
            x = block(tensor, me ^ k ^ opposite)
            twin[k] = permute(after(x, *earlier) if earlier else x, "fibre", k)

    odd = [k for k in range(3, n - 2, 2)]
    even = [k for k in range(2, n - 2, 2)]
    send_twin(odd)
    mine, theirs, high, low = gram_packed(parts, 1.0 / (width * n * groups))
    mine = (mine + permute(theirs, "fibre", 1)).reshape(chips, -1, LANES)
    piece = tree_sum([mine[k] if k == 0 else permute(mine[k], "fibre", 2 * k) for k in range(chips)])
    send_twin(even, piece)
    piece = tree_sum([piece if k == 0 else permute(piece, "group", k) for k in range(groups)])
    pieces = [None] * n
    for k in range(chips):
        pieces[2 * k] = piece if k == 0 else permute(piece, "fibre", 2 * k)
        pieces[2 * k + 1] = permute(pieces[2 * k], "fibre", 1)
    send_twin((n - 1, n - 2, 1), pieces[2])
    factor, inverse = factor_and_inverse(pieces, m)
    ks = tuple(range(2, n - 2))
    solved = rows_to_send(inverse, high, low, ks, rows)
    out = {k: permute(x, "fibre", k) for k, x in zip(ks, solved, strict=True)}
    out[0], near, out[opposite], twin_near = rows_to_keep(inverse, high, low, twin)
    out[1] = permute(near, "fibre", 1)
    out[opposite + 1] = permute(twin_near, "fibre", 1)
    basis = jnp.zeros((rows, wide), jnp.float32)
    for k in (0, opposite, 1, opposite + 1, *ks):
        basis = lax.dynamic_update_slice(basis, out[k], (0, (me ^ k) * width))
    return (basis, factor)


def solution(mesh):
    return jax.shard_map(
        local,
        mesh=mesh,
        in_specs=(P("fibre", "group"),),
        out_specs=(P("fibre", "group"), P()),
        check_vma=False,
    )
```

time: 149 us -> 126 us (0.85)
  blocking collectives: 40.4 us -> 0 us
  starting transfers between devices: 16.8 us -> 32.9 us
  waiting for transfers between devices: 54.4 us -> 60.2 us
  other arithmetic: 3.14 us -> 0.07 us
  local copies, waits for them, and re-layouts: 7.38 us -> 5.48 us
    ppermute x11 -> x34, waiting for transfers between devices: 16.5 us -> 60.2 us  [permute(): lax.ppermute(x, axis, [(i, i ^ bits) for i in range(lax.axis_size(axis))])]
    all_to_all x1 -> x0, blocking collectives: 40.4 us -> none  [local(): lax.all_to_all(solved, 'fibre', split_axis=0, concat_axis=1, tiled=True)]
    all_to_all x1 -> x0, waiting for transfers between devices: 37.9 us -> none  [local(): lax.all_to_all(tensor, 'fibre', split_axis=1, concat_axis=0, tiled=True)]
    ppermute x11 -> x34, starting transfers between devices: 11.6 us -> 32.9 us  [permute(): lax.ppermute(x, axis, [(i, i ^ bits) for i in range(lax.axis_size(axis))])]
    all_to_all x2 -> x0, local copies, waits for them, and re-layouts: 5.76 us -> none  [the longest x1 3.83 us: local(): lax.all_to_all(tensor, 'fibre', split_axis=1, concat_axis=0, tiled=True)]
    all_to_all x1 -> x0, starting transfers between devices: 5.17 us -> none  [local(): lax.all_to_all(tensor, 'fibre', split_axis=1, concat_axis=0, tiled=True)]
    dynamic_slice x0 -> x1, local copies, waits for them, and re-layouts: none -> 3.34 us  [block(): return lax.dynamic_slice(x, (0, j * width), (rows, width))]
    pallas_call x3 -> x4, Pallas kernels: 25.3 us -> 26.7 us  [the longest x1 20.5 us: factor_and_inverse(): pl.pallas_call(functools.partial(factor_kernel, m, n), out_shape=[jax.Sha...]
  transfers between devices with their start and end apart: 12 -> 34, of which waited for: 9 -> 17; matrix products, arithmetic and copies ran while one was open for 0% -> 0% of each run, Pallas kernels for 0% -> 19%
where the time goes in v1:
time: 126 us
  waiting for transfers between devices  60.2 us (48%)
  starting transfers between devices  32.9 us (26%)
  Pallas kernels  26.7 us (21%)
  local copies, waits for them, and re-layouts  5.48 us (4%)
    ppermute x34, waiting for transfers between devices, permute(): lax.ppermute(x, axis, [(i, i ^ bits) for i in range(lax.axis_size(axis))])  60.2 us
    ppermute x34, starting transfers between devices, permute(): lax.ppermute(x, axis, [(i, i ^ bits) for i in range(lax.axis_size(axis))])  32.9 us
    pallas_call x1, Pallas kernels, factor_and_inverse(): pl.pallas_call(functools.partial(factor_kernel, m, n), out_shape=[jax.Sha...  20.5 us
    dynamic_slice x1, local copies, waits for them, and re-layouts, block(): return lax.dynamic_slice(x, (0, j * width), (rows, width))  3.34 us
    pallas_call x1, Pallas kernels, gram_packed(): pl.pallas_call(functools.partial(gram_kernel, scale, n), out_shape=[half,...  2.69 us
  transfers between devices with their start and end apart: 34, of which 17 were waited for; matrix products, arithmetic and copies ran while one was open for 0% of the time, Pallas kernels for 19%

profile of v1, /device:TPU:0, one launch (start us, length us, event | category | flops | bytes accessed | tf_op | source)
XLA Modules:
  0.0 126.2 jit_solution(4314197573103281763)
XLA Ops:
  0.7 3.3 %constant_dynamic-slice_fusion = (f32[64,1536]{1,0:T(8,128)S(1)}, f32[64,1536]{1,0:T(8,128)S(1)}, f32[64,1536]{1,0:T(8,128)S(1)}, f32[64,1536]{1,0:T(8,128)S(1)}...) fusion(f32[64,12288]{1,0:T(8,128)} %param.1, ...), kind=kLoop, calls=%fused_computation.11 | loop fusion | bytes 11796540 | tf_op jit(solution)/shard_map/dynamic_slice | solution.py:271
  4.6 2.6 %collective-permute-start.1 = (f32[64,1536]{1,0:T(8,128)S(1)}, f32[64,1536]{1,0:T(8,128)S(1)}, u32[]{:S(2)}, u32[]{:S(2)}) collective-permute-start(f32[64,1536]{1,0:T(8,128)S(1)} %get-tuple-element.51), channel_id=1, source_target_pairs={{0,8},{4,12},{8,0},{12,4},{16,24},{20,28},{24,16},{28,20},{1,9},{5... | collective-permute-start | bytes 1179656 | tf_op jit(solution)/shard_map/ppermute | solution.py:248
  7.2 1.8 %collective-permute-start.3 = (f32[64,1536]{1,0:T(8,128)S(1)}, f32[64,1536]{1,0:T(8,128)S(1)}, u32[]{:S(2)}, u32[]{:S(2)}) collective-permute-start(f32[64,1536]{1,0:T(8,128)S(1)} %get-tuple-element.49), channel_id=1, source_target_pairs={{0,16},{4,20},{8,24},{12,28},{16,0},{20,4},{24,8},{28,12},{1,17},{... | collective-permute-start | bytes 1179656 | tf_op jit(solution)/shard_map/ppermute | solution.py:248
  9.0 2.6 %collective-permute-start.5 = (f32[64,1536]{1,0:T(8,128)S(1)}, f32[64,1536]{1,0:T(8,128)S(1)}, u32[]{:S(2)}, u32[]{:S(2)}) collective-permute-start(f32[64,1536]{1,0:T(8,128)S(1)} %get-tuple-element.47.refs_0_), channel_id=1, source_target_pairs={{0,24},{4,28},{8,16},{12,20},{16,8},{20,12},{24,0},{28,4},{1,25},{... | collective-permute-start | bytes 1179656 | tf_op jit(solution)/shard_map/ppermute | solution.py:248
  11.6 5.5 %collective-permute-done.1.refs_2_ = f32[64,1536]{1,0:T(8,128)S(1)} collective-permute-done((f32[64,1536]{1,0:T(8,128)S(1)}, f32[64,1536]{1,0:T(8,128)S(1)}, u32[]{:S(2)}, u32[]{:S(2)}) %collective-permute-start.1) | collective-permute-done | bytes 393248 | tf_op jit(solution)/shard_map/ppermute | solution.py:248
  17.1 1.7 %collective-permute-start.6 = (f32[64,1536]{1,0:T(8,128)S(1)}, f32[64,1536]{1,0:T(8,128)S(1)}, u32[]{:S(2)}, u32[]{:S(2)}) collective-permute-start(f32[64,1536]{1,0:T(8,128)S(1)} %get-tuple-element.46), channel_id=1, source_target_pairs={{0,28},{4,24},{8,20},{12,16},{16,12},{20,8},{24,4},{28,0},{1,29},{... | collective-permute-start | bytes 1179656 | tf_op jit(solution)/shard_map/ppermute | solution.py:248
  18.8 6.2 %collective-permute-done.2.refs_3_ = f32[64,1536]{1,0:T(8,128)S(1)} collective-permute-done((f32[64,1536]{1,0:T(8,128)S(1)}, f32[64,1536]{1,0:T(8,128)S(1)}, u32[]{:S(2)}, u32[]{:S(2)}) %collective-permute-start.2) | collective-permute-done | bytes 393248 | tf_op jit(solution)/shard_map/ppermute | solution.py:248
  25.0 18.1 %collective-permute-done.4.refs_5_ = f32[64,1536]{1,0:T(8,128)S(1)} collective-permute-done((f32[64,1536]{1,0:T(8,128)S(1)}, f32[64,1536]{1,0:T(8,128)S(1)}, u32[]{:S(2)}, u32[]{:S(2)}) %collective-permute-start.4) | collective-permute-done | bytes 393248 | tf_op jit(solution)/shard_map/ppermute | solution.py:248
  43.1 2.7 %gram.1 = (f32[640,128]{1,0:T(8,128)S(1)}, f32[640,128]{1,0:T(8,128)S(1)}, bf16[512,1536]{1,0:T(8,128)(2,1)S(1)}, bf16[512,1536]{1,0:T(8,128)(2,1)S(1)}) custom-call(f32[64,1536]{1,0:T(8,128)S(1)} %get-tuple-element.53.refs_0_, f32[64,1536]{1,0:T(8,128)S(1)} %collective-permute-done.refs_1_, f32[64,1536]{1,0:T(8,128)S(1)} %collective-permute-done.1.refs_2_, ...), custom_call_target="tpu_custom_call" | custom-call | flops 1811939328 | bytes 3145728 | tf_op jit(solution)/shard_map/gram/pallas_call | solution.py:86
  47.8 2.7 %collective-permute-start.10 = (f32[160,128]{1,0:T(8,128)S(1)}, f32[160,128]{1,0:T(8,128)S(1)}, u32[]{:S(2)}, u32[]{:S(2)}) collective-permute-start(f32[160,128]{1,0:T(8,128)S(1)} %get-tuple-element.55), channel_id=1, source_target_pairs={{0,24},{4,28},{8,16},{12,20},{16,8},{20,12},{24,0},{28,4},{1,25},{... | collective-permute-start | bytes 245768 | tf_op jit(solution)/shard_map/ppermute | solution.py:248
  51.4 2.5 %collective-permute-done.10 = f32[160,128]{1,0:T(8,128)S(1)} collective-permute-done((f32[160,128]{1,0:T(8,128)S(1)}, f32[160,128]{1,0:T(8,128)S(1)}, u32[]{:S(2)}, u32[]{:S(2)}) %collective-permute-start.10) | collective-permute-done | bytes 81952 | tf_op jit(solution)/shard_map/ppermute | solution.py:248
  53.8 1.7 %collective-permute-done.8 = f32[160,128]{1,0:T(8,128)S(1)} collective-permute-done((f32[160,128]{1,0:T(8,128)S(1)}, f32[160,128]{1,0:T(8,128)S(1)}, u32[]{:S(2)}, u32[]{:S(2)}) %collective-permute-start.8) | collective-permute-done | bytes 81952 | tf_op jit(solution)/shard_map/ppermute | solution.py:248
  55.6 1.7 %collective-permute-start.11 = (f32[160,128]{1,0:T(8,128)S(1)}, f32[160,128]{1,0:T(8,128)S(1)}, u32[]{:S(2)}, u32[]{:S(2)}) collective-permute-start(f32[160,128]{1,0:T(8,128)S(1)} %fusion), channel_id=1, source_target_pairs={{0,1},{1,0},{2,3},{3,2},{4,5},{5,4},{6,7},{7,6},{8,9},{9,8},{10,11... | collective-permute-start | bytes 245768 | tf_op jit(solution)/shard_map/ppermute | solution.py:248
  57.3 2.6 %collective-permute-start.12 = (f32[160,128]{1,0:T(8,128)S(1)}, f32[160,128]{1,0:T(8,128)S(1)}, u32[]{:S(2)}, u32[]{:S(2)}) collective-permute-start(f32[160,128]{1,0:T(8,128)S(1)} %fusion), channel_id=1, source_target_pairs={{0,2},{1,3},{2,0},{3,1},{4,6},{5,7},{6,4},{7,5},{8,10},{9,11},{10,... | collective-permute-start | bytes 245768 | tf_op jit(solution)/shard_map/ppermute | solution.py:248
  60.0 2.6 %collective-permute-start.25 = (f32[64,1536]{1,0:T(8,128)S(1)}, f32[64,1536]{1,0:T(8,128)S(1)}, u32[]{:S(2)}, u32[]{:S(2)}) collective-permute-start(f32[64,1536]{1,0:T(8,128)S(1)} %get-tuple-element.41), channel_id=1, source_target_pairs={{0,20},{4,16},{8,28},{12,24},{16,4},{20,0},{24,12},{28,8},{1,21},{... | collective-permute-start | bytes 1179656 | tf_op jit(solution)/shard_map/ppermute | solution.py:248
  62.6 2.6 %collective-permute-done.12 = f32[160,128]{1,0:T(8,128)S(1)} collective-permute-done((f32[160,128]{1,0:T(8,128)S(1)}, f32[160,128]{1,0:T(8,128)S(1)}, u32[]{:S(2)}, u32[]{:S(2)}) %collective-permute-start.12) | collective-permute-done | bytes 81952 | tf_op jit(solution)/shard_map/ppermute | solution.py:248
  71.5 1.8 %collective-permute-done.15.refs_2_ = f32[160,128]{1,0:T(8,128)S(1)} collective-permute-done((f32[160,128]{1,0:T(8,128)S(1)}, f32[160,128]{1,0:T(8,128)S(1)}, u32[]{:S(2)}, u32[]{:S(2)}) %collective-permute-start.15) | collective-permute-done | bytes 81952 | tf_op jit(solution)/shard_map/ppermute | solution.py:248
  74.1 1.8 %collective-permute-done.19.refs_6_ = f32[160,128]{1,0:T(8,128)S(1)} collective-permute-done((f32[160,128]{1,0:T(8,128)S(1)}, f32[160,128]{1,0:T(8,128)S(1)}, u32[]{:S(2)}, u32[]{:S(2)}) %collective-permute-start.19) | collective-permute-done | bytes 81952 | tf_op jit(solution)/shard_map/ppermute | solution.py:248
  81.1 20.5 %factor.1 = (f32[512,512]{1,0:T(8,128)}, f32[512,512]{1,0:T(8,128)S(1)}) custom-call(f32[160,128]{1,0:T(8,128)S(1)} %add_add_fusion.refs_0_, f32[160,128]{1,0:T(8,128)S(1)} %collective-permute-done.14.refs_1_, f32[160,128]{1,0:T(8,128)S(1)} %collective-permute-done.15.refs_2_, f32[160,128]{1,0:T(8,128)S(1)} %collective-permute-done.16.refs_3_, ...), custom_call_target="tpu_custom_call" | custom-call | flops 21474836480 | bytes 3145728 | tf_op jit(solution)/shard_map/factor/pallas_call | solution.py:169
  105.5 2.1 %keep_rows.1 = (f32[64,1536]{1,0:T(8,128)S(1)}, f32[64,1536]{1,0:T(8,128)S(1)}, f32[64,1536]{1,0:T(8,128)S(1)}, f32[64,1536]{1,0:T(8,128)S(1)}) custom-call(f32[512,512]{1,0:T(8,128)S(1)} %get-tuple-element.23.w_ref, bf16[512,1536]{1,0:T(8,128)(2,1)S(1)} %get-tuple-element.24.high, bf16[512,1536]{1,0:T(8,128)(2,1)S(1)} %get-tuple-element.25.low, ...), custom_call_target="tpu_custom_call" | custom-call | flops 1207959552 | bytes 6291456 | tf_op jit(solution)/shard_map/keep_rows/pallas_call | solution.py:235
  110.6 4.5 %collective-permute-done.30 = f32[64,1536]{1,0:T(8,128)S(1)} collective-permute-done((f32[64,1536]{1,0:T(8,128)S(1)}, f32[64,1536]{1,0:T(8,128)S(1)}, u32[]{:S(2)}, u32[]{:S(2)}) %collective-permute-start.30) | collective-permute-done | bytes 393248 | tf_op jit(solution)/shard_map/ppermute | solution.py:248
  115.1 6.5 %collective-permute-done.31 = f32[64,1536]{1,0:T(8,128)S(1)} collective-permute-done((f32[64,1536]{1,0:T(8,128)S(1)}, f32[64,1536]{1,0:T(8,128)S(1)}, u32[]{:S(2)}, u32[]{:S(2)}) %collective-permute-start.31) | collective-permute-done | bytes 393248 | tf_op jit(solution)/shard_map/ppermute | solution.py:248
  121.7 2.8 %collective-permute-done.33 = f32[64,1536]{1,0:T(8,128)S(1)} collective-permute-done((f32[64,1536]{1,0:T(8,128)S(1)}, f32[64,1536]{1,0:T(8,128)S(1)}, u32[]{:S(2)}, u32[]{:S(2)}) %collective-permute-start.33) | collective-permute-done | bytes 393248 | tf_op jit(solution)/shard_map/ppermute | solution.py:248
  124.5 1.7 %copy-done = f32[64,12288]{1,0:T(8,128)} copy-done((f32[64,12288]{1,0:T(8,128)}, f32[64,12288]{1,0:T(8,128)S(1)}, u32[]{:S(2)}) %copy-start) | copy-done | bytes 3145752
  (64 shorter events, 22.8 us)
Async XLA Ops:
  4.6 12.5 %collective-permute-start.1 = (f32[64,1536]{1,0:T(8,128)S(1)}, f32[64,1536]{1,0:T(8,128)S(1)}, u32[]{:S(2)}, u32[]{:S(2)}) collective-permute-start(f32[64,1536]{1,0:T(8,128)S(1)} %get-tuple-element.51), channel_id=1, source_target_pairs={{0,8},{4,12},{8,0},{12,4},{16,24},{20,28},{24,16},{28,20},{1,9},{5... | collective-permute-start | bytes 1179656 | tf_op jit(solution)/shard_map/ppermute | solution.py:248
  7.2 17.9 %collective-permute-start.2 = (f32[64,1536]{1,0:T(8,128)S(1)}, f32[64,1536]{1,0:T(8,128)S(1)}, u32[]{:S(2)}, u32[]{:S(2)}) collective-permute-start(f32[64,1536]{1,0:T(8,128)S(1)} %get-tuple-element.50), channel_id=1, source_target_pairs={{0,12},{4,8},{8,4},{12,0},{16,28},{20,24},{24,20},{28,16},{1,13},{... | collective-permute-start | bytes 1179656 | tf_op jit(solution)/shard_map/ppermute | solution.py:248
  7.2 17.8 %collective-permute-start.3 = (f32[64,1536]{1,0:T(8,128)S(1)}, f32[64,1536]{1,0:T(8,128)S(1)}, u32[]{:S(2)}, u32[]{:S(2)}) collective-permute-start(f32[64,1536]{1,0:T(8,128)S(1)} %get-tuple-element.49), channel_id=1, source_target_pairs={{0,16},{4,20},{8,24},{12,28},{16,0},{20,4},{24,8},{28,12},{1,17},{... | collective-permute-start | bytes 1179656 | tf_op jit(solution)/shard_map/ppermute | solution.py:248
  9.0 34.1 %collective-permute-start.4 = (f32[64,1536]{1,0:T(8,128)S(1)}, f32[64,1536]{1,0:T(8,128)S(1)}, u32[]{:S(2)}, u32[]{:S(2)}) collective-permute-start(f32[64,1536]{1,0:T(8,128)S(1)} %get-tuple-element.48), channel_id=1, source_target_pairs={{0,20},{4,16},{8,28},{12,24},{16,4},{20,0},{24,12},{28,8},{1,21},{... | collective-permute-start | bytes 1179656 | tf_op jit(solution)/shard_map/ppermute | solution.py:248
  9.0 34.1 %collective-permute-start.5 = (f32[64,1536]{1,0:T(8,128)S(1)}, f32[64,1536]{1,0:T(8,128)S(1)}, u32[]{:S(2)}, u32[]{:S(2)}) collective-permute-start(f32[64,1536]{1,0:T(8,128)S(1)} %get-tuple-element.47.refs_0_), channel_id=1, source_target_pairs={{0,24},{4,28},{8,16},{12,20},{16,8},{20,12},{24,0},{28,4},{1,25},{... | collective-permute-start | bytes 1179656 | tf_op jit(solution)/shard_map/ppermute | solution.py:248
  17.1 26.0 %collective-permute-start.6 = (f32[64,1536]{1,0:T(8,128)S(1)}, f32[64,1536]{1,0:T(8,128)S(1)}, u32[]{:S(2)}, u32[]{:S(2)}) collective-permute-start(f32[64,1536]{1,0:T(8,128)S(1)} %get-tuple-element.46), channel_id=1, source_target_pairs={{0,28},{4,24},{8,20},{12,16},{16,12},{20,8},{24,4},{28,0},{1,29},{... | collective-permute-start | bytes 1179656 | tf_op jit(solution)/shard_map/ppermute | solution.py:248
  47.8 6.0 %collective-permute-start.10 = (f32[160,128]{1,0:T(8,128)S(1)}, f32[160,128]{1,0:T(8,128)S(1)}, u32[]{:S(2)}, u32[]{:S(2)}) collective-permute-start(f32[160,128]{1,0:T(8,128)S(1)} %get-tuple-element.55), channel_id=1, source_target_pairs={{0,24},{4,28},{8,16},{12,20},{16,8},{20,12},{24,0},{28,4},{1,25},{... | collective-permute-start | bytes 245768 | tf_op jit(solution)/shard_map/ppermute | solution.py:248
  55.6 7.1 %collective-permute-start.11 = (f32[160,128]{1,0:T(8,128)S(1)}, f32[160,128]{1,0:T(8,128)S(1)}, u32[]{:S(2)}, u32[]{:S(2)}) collective-permute-start(f32[160,128]{1,0:T(8,128)S(1)} %fusion), channel_id=1, source_target_pairs={{0,1},{1,0},{2,3},{3,2},{4,5},{5,4},{6,7},{7,6},{8,9},{9,8},{10,11... | collective-permute-start | bytes 245768 | tf_op jit(solution)/shard_map/ppermute | solution.py:248
  57.3 7.9 %collective-permute-start.12 = (f32[160,128]{1,0:T(8,128)S(1)}, f32[160,128]{1,0:T(8,128)S(1)}, u32[]{:S(2)}, u32[]{:S(2)}) collective-permute-start(f32[160,128]{1,0:T(8,128)S(1)} %fusion), channel_id=1, source_target_pairs={{0,2},{1,3},{2,0},{3,1},{4,6},{5,7},{6,4},{7,5},{8,10},{9,11},{10,... | collective-permute-start | bytes 245768 | tf_op jit(solution)/shard_map/ppermute | solution.py:248
  59.9 6.3 %collective-permute-start.13 = (f32[160,128]{1,0:T(8,128)S(1)}, f32[160,128]{1,0:T(8,128)S(1)}, u32[]{:S(2)}, u32[]{:S(2)}) collective-permute-start(f32[160,128]{1,0:T(8,128)S(1)} %fusion), channel_id=1, source_target_pairs={{0,3},{1,2},{2,1},{3,0},{4,7},{5,6},{6,5},{7,4},{8,11},{9,10},{10,... | collective-permute-start | bytes 245768 | tf_op jit(solution)/shard_map/ppermute | solution.py:248
  60.0 11.3 %collective-permute-start.23 = (f32[64,1536]{1,0:T(8,128)S(1)}, f32[64,1536]{1,0:T(8,128)S(1)}, u32[]{:S(2)}, u32[]{:S(2)}) collective-permute-start(f32[64,1536]{1,0:T(8,128)S(1)} %get-tuple-element.43), channel_id=1, source_target_pairs={{0,12},{4,8},{8,4},{12,0},{16,28},{20,24},{24,20},{28,16},{1,13},{... | collective-permute-start | bytes 1179656 | tf_op jit(solution)/shard_map/ppermute | solution.py:248
  60.0 15.9 %collective-permute-start.25 = (f32[64,1536]{1,0:T(8,128)S(1)}, f32[64,1536]{1,0:T(8,128)S(1)}, u32[]{:S(2)}, u32[]{:S(2)}) collective-permute-start(f32[64,1536]{1,0:T(8,128)S(1)} %get-tuple-element.41), channel_id=1, source_target_pairs={{0,20},{4,16},{8,28},{12,24},{16,4},{20,0},{24,12},{28,8},{1,21},{... | collective-permute-start | bytes 1179656 | tf_op jit(solution)/shard_map/ppermute | solution.py:248
  66.2 7.1 %collective-permute-start.15 = (f32[160,128]{1,0:T(8,128)S(1)}, f32[160,128]{1,0:T(8,128)S(1)}, u32[]{:S(2)}, u32[]{:S(2)}) collective-permute-start(f32[160,128]{1,0:T(8,128)S(1)} %add_add_fusion.refs_0_), channel_id=1, source_target_pairs={{0,8},{4,12},{8,0},{12,4},{16,24},{20,28},{24,16},{28,20},{1,9},{5... | collective-permute-start | bytes 245768 | tf_op jit(solution)/shard_map/ppermute | solution.py:248
  67.8 6.3 %collective-permute-start.17 = (f32[160,128]{1,0:T(8,128)S(1)}, f32[160,128]{1,0:T(8,128)S(1)}, u32[]{:S(2)}, u32[]{:S(2)}) collective-permute-start(f32[160,128]{1,0:T(8,128)S(1)} %add_add_fusion.refs_0_), channel_id=1, source_target_pairs={{0,16},{4,20},{8,24},{12,28},{16,0},{20,4},{24,8},{28,12},{1,17},{... | collective-permute-start | bytes 245768 | tf_op jit(solution)/shard_map/ppermute | solution.py:248
  69.4 6.4 %collective-permute-start.19 = (f32[160,128]{1,0:T(8,128)S(1)}, f32[160,128]{1,0:T(8,128)S(1)}, u32[]{:S(2)}, u32[]{:S(2)}) collective-permute-start(f32[160,128]{1,0:T(8,128)S(1)} %add_add_fusion.refs_0_), channel_id=1, source_target_pairs={{0,24},{4,28},{8,16},{12,20},{16,8},{20,12},{24,0},{28,4},{1,25},{... | collective-permute-start | bytes 245768 | tf_op jit(solution)/shard_map/ppermute | solution.py:248
  75.9 27.1 %collective-permute-start.24 = (f32[64,1536]{1,0:T(8,128)S(1)}, f32[64,1536]{1,0:T(8,128)S(1)}, u32[]{:S(2)}, u32[]{:S(2)}) collective-permute-start(f32[64,1536]{1,0:T(8,128)S(1)} %get-tuple-element.28), channel_id=1, source_target_pairs={{0,16},{4,20},{8,24},{12,28},{16,0},{20,4},{24,8},{28,12},{1,17},{... | collective-permute-start | bytes 1179656 | tf_op jit(solution)/shard_map/ppermute | solution.py:248
  77.1 26.7 %collective-permute-start.22 = (f32[64,1536]{1,0:T(8,128)S(1)}, f32[64,1536]{1,0:T(8,128)S(1)}, u32[]{:S(2)}, u32[]{:S(2)}) collective-permute-start(f32[64,1536]{1,0:T(8,128)S(1)} %get-tuple-element.27), channel_id=1, source_target_pairs={{0,8},{4,12},{8,0},{12,4},{16,24},{20,28},{24,16},{28,20},{1,9},{5... | collective-permute-start | bytes 1179656 | tf_op jit(solution)/shard_map/ppermute | solution.py:248
  78.4 26.1 %collective-permute-start.27 = (f32[64,1536]{1,0:T(8,128)S(1)}, f32[64,1536]{1,0:T(8,128)S(1)}, u32[]{:S(2)}, u32[]{:S(2)}) collective-permute-start(f32[64,1536]{1,0:T(8,128)S(1)} %get-tuple-element.30), channel_id=1, source_target_pairs={{0,28},{4,24},{8,20},{12,16},{16,12},{20,8},{24,4},{28,0},{1,29},{... | collective-permute-start | bytes 1179656 | tf_op jit(solution)/shard_map/ppermute | solution.py:248
  78.9 26.6 %collective-permute-start.26 = (f32[64,1536]{1,0:T(8,128)S(1)}, f32[64,1536]{1,0:T(8,128)S(1)}, u32[]{:S(2)}, u32[]{:S(2)}) collective-permute-start(f32[64,1536]{1,0:T(8,128)S(1)} %get-tuple-element.29), channel_id=1, source_target_pairs={{0,24},{4,28},{8,16},{12,20},{16,8},{20,12},{24,0},{28,4},{1,25},{... | collective-permute-start | bytes 1179656 | tf_op jit(solution)/shard_map/ppermute | solution.py:248
  80.4 25.1 %collective-permute-start.21 = (f32[64,1536]{1,0:T(8,128)S(1)}, f32[64,1536]{1,0:T(8,128)S(1)}, u32[]{:S(2)}, u32[]{:S(2)}) collective-permute-start(f32[64,1536]{1,0:T(8,128)S(1)} %get-tuple-element.26), channel_id=1, source_target_pairs={{0,4},{4,0},{8,12},{12,8},{16,20},{20,16},{24,28},{28,24},{1,5},{5... | collective-permute-start | bytes 1179656 | tf_op jit(solution)/shard_map/ppermute | solution.py:248
  103.0 12.0 %collective-permute-start.30 = (f32[64,1536]{1,0:T(8,128)S(1)}, f32[64,1536]{1,0:T(8,128)S(1)}, u32[]{:S(2)}, u32[]{:S(2)}) collective-permute-start(f32[64,1536]{1,0:T(8,128)S(1)} %get-tuple-element.35), channel_id=1, source_target_pairs={{0,8},{4,12},{8,0},{12,4},{16,24},{20,28},{24,16},{28,20},{1,9},{5... | collective-permute-start | bytes 1179656 | tf_op jit(solution)/shard_map/ppermute | solution.py:248
  103.8 17.8 %collective-permute-start.31 = (f32[64,1536]{1,0:T(8,128)S(1)}, f32[64,1536]{1,0:T(8,128)S(1)}, u32[]{:S(2)}, u32[]{:S(2)}) collective-permute-start(f32[64,1536]{1,0:T(8,128)S(1)} %get-tuple-element.36), channel_id=1, source_target_pairs={{0,12},{4,8},{8,4},{12,0},{16,28},{20,24},{24,20},{28,16},{1,13},{... | collective-permute-start | bytes 1179656 | tf_op jit(solution)/shard_map/ppermute | solution.py:248
  104.5 17.2 %collective-permute-start.32 = (f32[64,1536]{1,0:T(8,128)S(1)}, f32[64,1536]{1,0:T(8,128)S(1)}, u32[]{:S(2)}, u32[]{:S(2)}) collective-permute-start(f32[64,1536]{1,0:T(8,128)S(1)} %get-tuple-element.37), channel_id=1, source_target_pairs={{0,16},{4,20},{8,24},{12,28},{16,0},{20,4},{24,8},{28,12},{1,17},{... | collective-permute-start | bytes 1179656 | tf_op jit(solution)/shard_map/ppermute | solution.py:248
  109.4 15.1 %collective-permute-start.33 = (f32[64,1536]{1,0:T(8,128)S(1)}, f32[64,1536]{1,0:T(8,128)S(1)}, u32[]{:S(2)}, u32[]{:S(2)}) collective-permute-start(f32[64,1536]{1,0:T(8,128)S(1)} %get-tuple-element.38), channel_id=1, source_target_pairs={{0,20},{4,16},{8,28},{12,24},{16,4},{20,0},{24,12},{28,8},{1,21},{... | collective-permute-start | bytes 1179656 | tf_op jit(solution)/shard_map/ppermute | solution.py:248
  (11 other events, 42.8 us)

commit v2 on v1

--- a/solution.py
+++ b/solution.py
@@ -11,6 +11,8 @@
 SUB = 8
 PART = 32
 MIB = 1024 * 1024
+SHORT = pl.CostEstimate(flops=1024, bytes_accessed=1024, transcendentals=0)
+KEEP = SHORT
 
 
 def split(x):
@@ -49,7 +51,7 @@
     me = fibre_index()
     for k, part in enumerate(parts):
         at = pl.ds(pl.multiple_of((me ^ k) * rows, rows), rows)
-        high[at, :], low[at, :] = split(part[...])
+        high[at, :], low[at, :] = split(part[...] if len(part.shape) == 2 else part[0])
 
 
 def gram_kernel(scale, n, *refs):
@@ -88,9 +90,7 @@
         out_shape=[half, half, wide, wide],
         scratch_shapes=[pltpu.VMEM((size, LANES), jnp.float32)],
         compiler_params=pltpu.CompilerParams(vmem_limit_bytes=24 * MIB),
-        cost_estimate=pl.CostEstimate(
-            flops=6 * m * m * w * 3 // 4, bytes_accessed=4 * m * w, transcendentals=0
-        ),
+        cost_estimate=SHORT,
         name="gram",
     )(*parts)
 
@@ -174,9 +174,7 @@
             pltpu.VMEM((n * pieces[0].shape[0], LANES), jnp.float32),
         ],
         compiler_params=pltpu.CompilerParams(vmem_limit_bytes=24 * MIB),
-        cost_estimate=pl.CostEstimate(
-            flops=160 * m * m * m, bytes_accessed=12 * m * m, transcendentals=m
-        ),
+        cost_estimate=SHORT,
         name="factor",
     )(*pieces)
 
@@ -208,38 +206,37 @@
         out_shape=[jax.ShapeDtypeStruct((rows, width), jnp.float32)] * len(ks),
         scratch_shapes=[pltpu.VMEM((len(ks) * rows, m), jnp.bfloat16)] * 2,
         compiler_params=pltpu.CompilerParams(vmem_limit_bytes=24 * MIB),
-        cost_estimate=pl.CostEstimate(
-            flops=6 * len(ks) * rows * m * width, bytes_accessed=8 * m * width, transcendentals=0
-        ),
+        cost_estimate=SHORT,
         name="send_rows",
     )(w, high, low)
 
 
 def keep_kernel(n, w_ref, high, low, *refs):
-    parts, outs, (twin_high, twin_low), wide = refs[:n], refs[n : n + 4], refs[n + 4 : n + 6], refs[n + 6 :]
+    parts, outs, (twin_high, twin_low), wide = refs[:n], refs[n : n + 6], refs[n + 6 : n + 8], refs[n + 8 :]
     rows, width = outs[0].shape
+    half = width // 2
     rows_of(w_ref, wide, (0, 1), rows)
     place_rows(parts, twin_high, twin_low)
-    for first, (h, l) in ((0, (high, low)), (2, (twin_high, twin_low))):
-        for start in range(0, width, width // 2):
-            cols = slice(start, start + width // 2)
+    for (out, *near), h, l in ((outs[:3], high, low), (outs[3:], twin_high, twin_low)):
+        for i in range(2):
+            cols = slice(i * half, (i + 1) * half)
             solved = dot3((wide[0][...], wide[1][...]), (h[:, cols], l[:, cols]), ((1,), (0,)))
-            outs[first][:, cols] = solved[:rows]
-            outs[first + 1][:, cols] = solved[rows:]
+            out[:, cols] = solved[:rows]
+            near[i][...] = solved[rows:]
 
 
 def rows_to_keep(w, high, low, twin):
     m, width = high.shape
     n = len(twin)
     rows = m // n
+    own = jax.ShapeDtypeStruct((rows, width), jnp.float32)
+    near = jax.ShapeDtypeStruct((rows, width // 2), jnp.float32)
     return pl.pallas_call(
         functools.partial(keep_kernel, n),
-        out_shape=[jax.ShapeDtypeStruct((rows, width), jnp.float32)] * 4,
+        out_shape=[own, near, near, own, near, near],
         scratch_shapes=[pltpu.VMEM((m, width), jnp.bfloat16)] * 2 + [pltpu.VMEM((2 * rows, m), jnp.bfloat16)] * 2,
         compiler_params=pltpu.CompilerParams(vmem_limit_bytes=24 * MIB),
-        cost_estimate=pl.CostEstimate(
-            flops=24 * rows * m * width, bytes_accessed=8 * m * width, transcendentals=0
-        ),
+        cost_estimate=KEEP,
         name="keep_rows",
     )(w, high, low, *twin)
 
@@ -256,6 +253,37 @@
 
 def after(x, *earlier):
     return lax.optimization_barrier((x, *earlier))[0]
+
+
+def assemble_kernel(places, width, n_old, *refs):
+    count = len(places)
+    blocks, (out, sems) = refs[n_old : n_old + count], refs[n_old + count :]
+    me = fibre_index()
+    copies = []
+    for i, ((k, start), block) in enumerate(zip(places, blocks, strict=True)):
+        at = pl.multiple_of((me ^ k) * width, width) + start
+        place = out.at[:, pl.ds(pl.multiple_of(at, LANES), block.shape[1])]
+        copies.append(pltpu.make_async_copy(block, place, sems.at[i]))
+    for copy in copies:
+        copy.start()
+    for copy in copies:
+        copy.wait()
+
+
+def assemble(blocks, rows, width, n, old=None):
+    places = tuple(blocks)
+    olds = () if old is None else (old,)
+    return pl.pallas_call(
+        functools.partial(assemble_kernel, places, width, len(olds)),
+        out_shape=jax.ShapeDtypeStruct((rows, width * n), jnp.float32),
+        in_specs=[pl.BlockSpec(memory_space=pl.ANY)] * (len(olds) + len(places)),
+        out_specs=pl.BlockSpec(memory_space=pl.ANY),
+        scratch_shapes=[pltpu.SemaphoreType.DMA((len(places),))],
+        input_output_aliases={0: 0} if olds else {},
+        compiler_params=pltpu.CompilerParams(vmem_limit_bytes=MIB),
+        cost_estimate=SHORT,
+        name="assemble",
+    )(*olds, *blocks.values())
 
 
 def local(tensor):
@@ -270,40 +298,44 @@
     def block(x, j):
         return lax.dynamic_slice(x, (0, j * width), (rows, width))
 
-    far_first = sorted(range(1, n), key=lambda k: -k)
-    parts = [block(tensor, me)] + [None] * (n - 1)
-    for k in far_first:
-        parts[k] = permute(block(tensor, me ^ k), "fibre", k)
-    twin = [block(tensor, me ^ opposite)] + [None] * (n - 1)
-
-    def send_twin(ks, *earlier):
-        for k in ks:
-            x = block(tensor, me ^ k ^ opposite)
-            twin[k] = permute(after(x, *earlier) if earlier else x, "fibre", k)
-
-    odd = [k for k in range(3, n - 2, 2)]
-    even = [k for k in range(2, n - 2, 2)]
-    send_twin(odd)
+    far = (opposite + 1, opposite)
+    odd, even = list(range(3, n - 2, 2)), list(range(2, n - 2, 2))
+    blocks = {k: block(tensor, me ^ k) for k in far}
+    rest = after(tensor, *blocks.values())
+    blocks |= {k: block(rest, me ^ k) for k in range(n - 2)}
+    parts = [permute(blocks[k], "fibre", k) if k else blocks[0] for k in range(n)]
+    twin = [block(rest, me ^ k ^ opposite) for k in range(opposite)] + [None, None]
     mine, theirs, high, low = gram_packed(parts, 1.0 / (width * n * groups))
     mine = (mine + permute(theirs, "fibre", 1)).reshape(chips, -1, LANES)
     piece = tree_sum([mine[k] if k == 0 else permute(mine[k], "fibre", 2 * k) for k in range(chips)])
-    send_twin(even, piece)
+    for k in even:
+        twin[k] = permute(after(twin[k], piece), "fibre", k)
     piece = tree_sum([piece if k == 0 else permute(piece, "group", k) for k in range(groups)])
+    piece, *arrived = lax.optimization_barrier((piece, *[twin[k] for k in even]))
+    for k, x in zip(even, arrived, strict=True):
+        twin[k] = x
     pieces = [None] * n
     for k in range(chips):
         pieces[2 * k] = piece if k == 0 else permute(piece, "fibre", 2 * k)
         pieces[2 * k + 1] = permute(pieces[2 * k], "fibre", 1)
-    send_twin((n - 1, n - 2, 1), pieces[2])
+    own = after(jnp.stack([blocks[0], blocks[1]]), *pieces[2::2])
+    twin[opposite] = permute(own, "fibre", opposite)
+    for k in (*odd, 1):
+        twin[k] = permute(after(twin[k], *pieces[3::2]), "fibre", k)
     factor, inverse = factor_and_inverse(pieces, m)
     ks = tuple(range(2, n - 2))
     solved = rows_to_send(inverse, high, low, ks, rows)
-    out = {k: permute(x, "fibre", k) for k, x in zip(ks, solved, strict=True)}
-    out[0], near, out[opposite], twin_near = rows_to_keep(inverse, high, low, twin)
-    out[1] = permute(near, "fibre", 1)
-    out[opposite + 1] = permute(twin_near, "fibre", 1)
-    basis = jnp.zeros((rows, wide), jnp.float32)
-    for k in (0, opposite, 1, opposite + 1, *ks):
-        basis = lax.dynamic_update_slice(basis, out[k], (0, (me ^ k) * width))
+    sent = {k: permute(x, "fibre", k) for k, x in zip(ks, solved, strict=True)}
+    twin[opposite] = after(twin[opposite], solved[0])
+    twin[opposite + 1] = permute(twin[opposite][1], "fibre", 1)
+    kept = rows_to_keep(inverse, high, low, twin)
+    here = {(0, 0): kept[0], (opposite, 0): kept[3]}
+    for k, near in ((1, kept[1:3]), (opposite + 1, kept[4:])):
+        for i, x in enumerate(near):
+            here[k, i * width // 2] = permute(x, "fibre", 1)
+    basis = assemble(here | {(k, 0): sent[k] for k in even}, rows, width, n)
+    if odd:
+        basis = assemble({(k, 0): sent[k] for k in odd}, rows, width, n, basis)
     return (basis, factor)
 
 

time: 126 us -> 120 us (0.952)
  waiting for transfers between devices: 60.2 us -> 53.3 us
  Pallas kernels: 26.7 us -> 29 us
  local copies, waits for them, and re-layouts: 5.48 us -> 3.95 us
    ppermute x34 -> x36, waiting for transfers between devices: 60.2 us -> 53.3 us  [permute(): lax.ppermute(x, axis, [(i, i ^ bits) for i in range(lax.axis_size(axis))])]
    pallas_call x1 -> x3, Pallas kernels: 2.13 us -> 4.49 us  [the longest x2 2.35 us: assemble(): pl.pallas_call(functools.partial(assemble_kernel, places, width, len(olds...]
    unnamed x2 -> x0, local copies, waits for them, and re-layouts: 1.66 us -> none
    ppermute x34 -> x36, starting transfers between devices: 32.9 us -> 32.1 us  [permute(): lax.ppermute(x, axis, [(i, i ^ bits) for i in range(lax.axis_size(axis))])]
    dynamic_slice x1 -> x2, local copies, waits for them, and re-layouts: 3.34 us -> 3.9 us  [block(): return lax.dynamic_slice(x, (0, j * width), (rows, width))]
  transfers between devices with their start and end apart: 34 -> 36, of which waited for: 17 -> 23; matrix products, arithmetic and copies ran while one was open for 0% -> 2% of each run, Pallas kernels for 19% -> 21%
where the time goes in v2:
time: 120 us
  waiting for transfers between devices  53.3 us (44%)
  starting transfers between devices  32.1 us (27%)
  Pallas kernels  29 us (24%)
  local copies, waits for them, and re-layouts  3.95 us (3%)
    ppermute x36, waiting for transfers between devices, permute(): lax.ppermute(x, axis, [(i, i ^ bits) for i in range(lax.axis_size(axis))])  53.3 us
    ppermute x36, starting transfers between devices, permute(): lax.ppermute(x, axis, [(i, i ^ bits) for i in range(lax.axis_size(axis))])  32.1 us
    pallas_call x1, Pallas kernels, factor_and_inverse(): pl.pallas_call(functools.partial(factor_kernel, m, n), out_shape=[jax.Sha...  20.5 us
    dynamic_slice x2, local copies, waits for them, and re-layouts, block(): return lax.dynamic_slice(x, (0, j * width), (rows, width))  3.9 us
    pallas_call x1, Pallas kernels, gram_packed(): pl.pallas_call(functools.partial(gram_kernel, scale, n), out_shape=[half,...  2.69 us
  transfers between devices with their start and end apart: 36, of which 23 were waited for; matrix products, arithmetic and copies ran while one was open for 2% of the time, Pallas kernels for 21%

profile of v2, /device:TPU:0, one launch (start us, length us, event | category | flops | bytes accessed | tf_op | source)
XLA Modules:
  0.0 119.5 jit_solution(9063526490889781401)
XLA Ops:
  1.8 4.0 %collective-permute-start.5 = (f32[64,1536]{1,0:T(8,128)S(1)}, f32[64,1536]{1,0:T(8,128)S(1)}, u32[]{:S(2)}, u32[]{:S(2)}) collective-permute-start(f32[64,1536]{1,0:T(8,128)S(1)} %get-tuple-element.68), channel_id=1, source_target_pairs={{0,24},{4,28},{8,16},{12,20},{16,8},{20,12},{24,0},{28,4},{1,25},{... | collective-permute-start | bytes 1179656 | tf_op jit(solution)/shard_map/ppermute | solution.py:245
  5.8 2.7 %constant_dynamic-slice_fusion = (f32[64,1536]{1,0:T(8,128)S(1)}, f32[64,1536]{1,0:T(8,128)S(1)}, f32[64,1536]{1,0:T(8,128)S(1)}, f32[64,1536]{1,0:T(8,128)S(1)}...) fusion(f32[64,12288]{1,0:T(8,128)} %param.1, ...), kind=kLoop, calls=%fused_computation.5 | loop fusion | bytes 9437232 | tf_op jit(solution)/shard_map/dynamic_slice | solution.py:299
  8.5 1.7 %collective-permute-start.4 = (f32[64,1536]{1,0:T(8,128)S(1)}, f32[64,1536]{1,0:T(8,128)S(1)}, u32[]{:S(2)}, u32[]{:S(2)}) collective-permute-start(f32[64,1536]{1,0:T(8,128)S(1)} %get-tuple-element.62), channel_id=1, source_target_pairs={{0,20},{4,16},{8,28},{12,24},{16,4},{20,0},{24,12},{28,8},{1,21},{... | collective-permute-start | bytes 1179656 | tf_op jit(solution)/shard_map/ppermute | solution.py:245
  11.6 4.3 %collective-permute-done.5.refs_6_ = f32[64,1536]{1,0:T(8,128)S(1)} collective-permute-done((f32[64,1536]{1,0:T(8,128)S(1)}, f32[64,1536]{1,0:T(8,128)S(1)}, u32[]{:S(2)}, u32[]{:S(2)}) %collective-permute-start.5) | collective-permute-done | bytes 393248 | tf_op jit(solution)/shard_map/ppermute | solution.py:245
  15.8 2.0 %collective-permute-start.1 = (f32[64,1536]{1,0:T(8,128)S(1)}, f32[64,1536]{1,0:T(8,128)S(1)}, u32[]{:S(2)}, u32[]{:S(2)}) collective-permute-start(f32[64,1536]{1,0:T(8,128)S(1)} %get-tuple-element.65), channel_id=1, source_target_pairs={{0,8},{4,12},{8,0},{12,4},{16,24},{20,28},{24,16},{28,20},{1,9},{5... | collective-permute-start | bytes 1179656 | tf_op jit(solution)/shard_map/ppermute | solution.py:245
  17.8 5.9 %collective-permute-done.6.refs_7_ = f32[64,1536]{1,0:T(8,128)S(1)} collective-permute-done((f32[64,1536]{1,0:T(8,128)S(1)}, f32[64,1536]{1,0:T(8,128)S(1)}, u32[]{:S(2)}, u32[]{:S(2)}) %collective-permute-start.6) | collective-permute-done | bytes 393248 | tf_op jit(solution)/shard_map/ppermute | solution.py:245
  24.0 7.7 %collective-permute-done.4.refs_5_ = f32[64,1536]{1,0:T(8,128)S(1)} collective-permute-done((f32[64,1536]{1,0:T(8,128)S(1)}, f32[64,1536]{1,0:T(8,128)S(1)}, u32[]{:S(2)}, u32[]{:S(2)}) %collective-permute-start.4) | collective-permute-done | bytes 393248 | tf_op jit(solution)/shard_map/ppermute | solution.py:245
  31.7 8.5 %collective-permute-done.3.refs_4_ = f32[64,1536]{1,0:T(8,128)S(1)} collective-permute-done((f32[64,1536]{1,0:T(8,128)S(1)}, f32[64,1536]{1,0:T(8,128)S(1)}, u32[]{:S(2)}, u32[]{:S(2)}) %collective-permute-start.3) | collective-permute-done | bytes 393248 | tf_op jit(solution)/shard_map/ppermute | solution.py:245
  40.5 2.7 %gram.1 = (f32[640,128]{1,0:T(8,128)S(1)}, f32[640,128]{1,0:T(8,128)S(1)}, bf16[512,1536]{1,0:T(8,128)(2,1)S(1)}, bf16[512,1536]{1,0:T(8,128)(2,1)S(1)}) custom-call(f32[64,1536]{1,0:T(8,128)S(1)} %get-tuple-element.67.refs_0_, f32[64,1536]{1,0:T(8,128)S(1)} %collective-permute-done.refs_1_, f32[64,1536]{1,0:T(8,128)S(1)} %collective-permute-done.1.refs_2_, ...), custom_call_target="tpu_custom_call" | custom-call | flops 1024 | bytes 1024 | tf_op jit(solution)/shard_map/gram/pallas_call | solution.py:88
  43.2 1.6 %collective-permute-done.7 = f32[640,128]{1,0:T(8,128)S(1)} collective-permute-done((f32[640,128]{1,0:T(8,128)S(1)}, f32[640,128]{1,0:T(8,128)S(1)}, u32[]{:S(2)}, u32[]{:S(2)}) %collective-permute-start.7) | collective-permute-done | bytes 327712 | tf_op jit(solution)/shard_map/ppermute | solution.py:245
  44.9 2.4 %collective-permute-start.10 = (f32[160,128]{1,0:T(8,128)S(1)}, f32[160,128]{1,0:T(8,128)S(1)}, u32[]{:S(2)}, u32[]{:S(2)}) collective-permute-start(f32[160,128]{1,0:T(8,128)S(1)} %get-tuple-element.70), channel_id=1, source_target_pairs={{0,24},{4,28},{8,16},{12,20},{16,8},{20,12},{24,0},{28,4},{1,25},{... | collective-permute-start | bytes 245768 | tf_op jit(solution)/shard_map/ppermute | solution.py:245
  48.5 2.0 %collective-permute-done.10 = f32[160,128]{1,0:T(8,128)S(1)} collective-permute-done((f32[160,128]{1,0:T(8,128)S(1)}, f32[160,128]{1,0:T(8,128)S(1)}, u32[]{:S(2)}, u32[]{:S(2)}) %collective-permute-start.10) | collective-permute-done | bytes 81952 | tf_op jit(solution)/shard_map/ppermute | solution.py:245
  50.4 1.7 %collective-permute-done.9 = f32[160,128]{1,0:T(8,128)S(1)} collective-permute-done((f32[160,128]{1,0:T(8,128)S(1)}, f32[160,128]{1,0:T(8,128)S(1)}, u32[]{:S(2)}, u32[]{:S(2)}) %collective-permute-start.9) | collective-permute-done | bytes 81952 | tf_op jit(solution)/shard_map/ppermute | solution.py:245
  54.5 3.6 %collective-permute-start.13 = (f32[160,128]{1,0:T(8,128)S(1)}, f32[160,128]{1,0:T(8,128)S(1)}, u32[]{:S(2)}, u32[]{:S(2)}) collective-permute-start(f32[160,128]{1,0:T(8,128)S(1)} %fusion), channel_id=1, source_target_pairs={{0,3},{1,2},{2,1},{3,0},{4,7},{5,6},{6,5},{7,4},{8,11},{9,10},{10,... | collective-permute-start | bytes 245768 | tf_op jit(solution)/shard_map/ppermute | solution.py:245
  58.9 2.2 %collective-permute-done.13 = f32[160,128]{1,0:T(8,128)S(1)} collective-permute-done((f32[160,128]{1,0:T(8,128)S(1)}, f32[160,128]{1,0:T(8,128)S(1)}, u32[]{:S(2)}, u32[]{:S(2)}) %collective-permute-start.13) | collective-permute-done | bytes 81952 | tf_op jit(solution)/shard_map/ppermute | solution.py:245
  61.1 3.3 %collective-permute-done.12 = f32[160,128]{1,0:T(8,128)S(1)} collective-permute-done((f32[160,128]{1,0:T(8,128)S(1)}, f32[160,128]{1,0:T(8,128)S(1)}, u32[]{:S(2)}, u32[]{:S(2)}) %collective-permute-start.12) | collective-permute-done | bytes 81952 | tf_op jit(solution)/shard_map/ppermute | solution.py:245
  64.5 1.4 %collective-permute-start.21 = (f32[160,128]{1,0:T(8,128)S(1)}, f32[160,128]{1,0:T(8,128)S(1)}, u32[]{:S(2)}, u32[]{:S(2)}) collective-permute-start(f32[160,128]{1,0:T(8,128)S(1)} %add_add_fusion.refs_0_), channel_id=1, source_target_pairs={{0,24},{4,28},{8,16},{12,20},{16,8},{20,12},{24,0},{28,4},{1,25},{... | collective-permute-start | bytes 245768 | tf_op jit(solution)/shard_map/ppermute | solution.py:245
  68.0 2.7 %collective-permute-done.21.refs_6_ = f32[160,128]{1,0:T(8,128)S(1)} collective-permute-done((f32[160,128]{1,0:T(8,128)S(1)}, f32[160,128]{1,0:T(8,128)S(1)}, u32[]{:S(2)}, u32[]{:S(2)}) %collective-permute-start.21) | collective-permute-done | bytes 81952 | tf_op jit(solution)/shard_map/ppermute | solution.py:245
  71.8 1.5 %collective-permute-start.26 = (f32[2,64,1536]{2,1,0:T(8,128)S(1)}, f32[2,64,1536]{2,1,0:T(8,128)S(1)}, u32[]{:S(2)}, u32[]{:S(2)}) collective-permute-start(f32[2,64,1536]{2,1,0:T(8,128)S(1)} %pad_maximum_fusion), channel_id=1, source_target_pairs={{0,24},{4,28},{8,16},{12,20},{16,8},{20,12},{24,0},{28,4},{1,25},{... | collective-permute-start | bytes 2359304 | tf_op jit(solution)/shard_map/ppermute | solution.py:245
  77.0 20.5 %factor.1 = (f32[512,512]{1,0:T(8,128)}, f32[512,512]{1,0:T(8,128)S(1)}) custom-call(f32[160,128]{1,0:T(8,128)S(1)} %add_add_fusion.refs_0_, f32[160,128]{1,0:T(8,128)S(1)} %collective-permute-done.16.refs_1_, f32[160,128]{1,0:T(8,128)S(1)} %collective-permute-done.17.refs_2_, f32[160,128]{1,0:T(8,128)S(1)} %collective-permute-done.18.refs_3_, ...), custom_call_target="tpu_custom_call" | custom-call | flops 1024 | bytes 1024 | tf_op jit(solution)/shard_map/factor/pallas_call | solution.py:169
  101.4 2.1 %keep_rows.1 = (f32[64,1536]{1,0:T(8,128)S(1)}, f32[64,768]{1,0:T(8,128)S(1)}, f32[64,768]{1,0:T(8,128)S(1)}, f32[64,1536]{1,0:T(8,128)S(1)}, f32[64,768]{1,0:T(8,128)S(1)}, /*index=5*/f32[64,768]{1,0:T(8,128)S(1)}) custom-call(f32[512,512]{1,0:T(8,128)S(1)} %get-tuple-element.35.w_ref, bf16[512,1536]{1,0:T(8,128)(2,1)S(1)} %get-tuple-element.36.high, ...), custom_call_target="tpu_custom_call" | custom-call | flops 1024 | bytes 1024 | tf_op jit(solution)/shard_map/keep_rows/pallas_call | solution.py:234
  105.4 5.9 %collective-permute-done.33.refs_7_ = f32[64,1536]{1,0:T(8,128)S(1)} collective-permute-done((f32[64,1536]{1,0:T(8,128)S(1)}, f32[64,1536]{1,0:T(8,128)S(1)}, u32[]{:S(2)}, u32[]{:S(2)}) %collective-permute-start.33) | collective-permute-done | bytes 393248 | tf_op jit(solution)/shard_map/ppermute | solution.py:245
  114.0 1.5 %assemble.2.refs_0_ = f32[64,12288]{1,0:T(8,128)} custom-call(f32[64,1536]{1,0:T(8,128)S(1)} %get-tuple-element.46.refs_0_, f32[64,1536]{1,0:T(8,128)S(1)} %get-tuple-element.47.refs_1_, f32[64,768]{1,0:T(8,128)S(1)} %collective-permute-done.28.refs_2_, f32[64,768]{1,0:T(8,128)S(1)} %collective-permute-done.29.refs_3_, ...), custom_call_target="tpu_custom_call" | custom-call | flops 1024 | bytes 1024 | tf_op jit(solution)/shard_map/assemble/pallas_call | solution.py:276
  115.4 3.0 %collective-permute-done.34.refs_1_ = f32[64,1536]{1,0:T(8,128)S(1)} collective-permute-done((f32[64,1536]{1,0:T(8,128)S(1)}, f32[64,1536]{1,0:T(8,128)S(1)}, u32[]{:S(2)}, u32[]{:S(2)}) %collective-permute-start.34) | collective-permute-done | bytes 393248 | tf_op jit(solution)/shard_map/ppermute | solution.py:245
  (62 shorter events, 23.8 us)
Async XLA Ops:
  1.8 14.0 %collective-permute-start.5 = (f32[64,1536]{1,0:T(8,128)S(1)}, f32[64,1536]{1,0:T(8,128)S(1)}, u32[]{:S(2)}, u32[]{:S(2)}) collective-permute-start(f32[64,1536]{1,0:T(8,128)S(1)} %get-tuple-element.68), channel_id=1, source_target_pairs={{0,24},{4,28},{8,16},{12,20},{16,8},{20,12},{24,0},{28,4},{1,25},{... | collective-permute-start | bytes 1179656 | tf_op jit(solution)/shard_map/ppermute | solution.py:245
  5.8 18.0 %collective-permute-start.6 = (f32[64,1536]{1,0:T(8,128)S(1)}, f32[64,1536]{1,0:T(8,128)S(1)}, u32[]{:S(2)}, u32[]{:S(2)}) collective-permute-start(f32[64,1536]{1,0:T(8,128)S(1)} %get-tuple-element.69), channel_id=1, source_target_pairs={{0,28},{4,24},{8,20},{12,16},{16,12},{20,8},{24,4},{28,0},{1,29},{... | collective-permute-start | bytes 1179656 | tf_op jit(solution)/shard_map/ppermute | solution.py:245
  8.5 23.2 %collective-permute-start.4 = (f32[64,1536]{1,0:T(8,128)S(1)}, f32[64,1536]{1,0:T(8,128)S(1)}, u32[]{:S(2)}, u32[]{:S(2)}) collective-permute-start(f32[64,1536]{1,0:T(8,128)S(1)} %get-tuple-element.62), channel_id=1, source_target_pairs={{0,20},{4,16},{8,28},{12,24},{16,4},{20,0},{24,12},{28,8},{1,21},{... | collective-permute-start | bytes 1179656 | tf_op jit(solution)/shard_map/ppermute | solution.py:245
  10.2 30.0 %collective-permute-start.3 = (f32[64,1536]{1,0:T(8,128)S(1)}, f32[64,1536]{1,0:T(8,128)S(1)}, u32[]{:S(2)}, u32[]{:S(2)}) collective-permute-start(f32[64,1536]{1,0:T(8,128)S(1)} %get-tuple-element.63), channel_id=1, source_target_pairs={{0,16},{4,20},{8,24},{12,28},{16,0},{20,4},{24,8},{28,12},{1,17},{... | collective-permute-start | bytes 1179656 | tf_op jit(solution)/shard_map/ppermute | solution.py:245
  10.4 29.8 %collective-permute-start.2 = (f32[64,1536]{1,0:T(8,128)S(1)}, f32[64,1536]{1,0:T(8,128)S(1)}, u32[]{:S(2)}, u32[]{:S(2)}) collective-permute-start(f32[64,1536]{1,0:T(8,128)S(1)} %get-tuple-element.64), channel_id=1, source_target_pairs={{0,12},{4,8},{8,4},{12,0},{16,28},{20,24},{24,20},{28,16},{1,13},{... | collective-permute-start | bytes 1179656 | tf_op jit(solution)/shard_map/ppermute | solution.py:245
  15.8 24.6 %collective-permute-start.1 = (f32[64,1536]{1,0:T(8,128)S(1)}, f32[64,1536]{1,0:T(8,128)S(1)}, u32[]{:S(2)}, u32[]{:S(2)}) collective-permute-start(f32[64,1536]{1,0:T(8,128)S(1)} %get-tuple-element.65), channel_id=1, source_target_pairs={{0,8},{4,12},{8,0},{12,4},{16,24},{20,28},{24,16},{28,20},{1,9},{5... | collective-permute-start | bytes 1179656 | tf_op jit(solution)/shard_map/ppermute | solution.py:245
  23.8 16.7 %collective-permute-start = (f32[64,1536]{1,0:T(8,128)S(1)}, f32[64,1536]{1,0:T(8,128)S(1)}, u32[]{:S(2)}, u32[]{:S(2)}) collective-permute-start(f32[64,1536]{1,0:T(8,128)S(1)} %get-tuple-element.66), channel_id=1, source_target_pairs={{0,4},{4,0},{8,12},{12,8},{16,20},{20,16},{24,28},{28,24},{1,5},{5... | collective-permute-start | bytes 1179656 | tf_op jit(solution)/shard_map/ppermute | solution.py:245
  44.9 5.5 %collective-permute-start.10 = (f32[160,128]{1,0:T(8,128)S(1)}, f32[160,128]{1,0:T(8,128)S(1)}, u32[]{:S(2)}, u32[]{:S(2)}) collective-permute-start(f32[160,128]{1,0:T(8,128)S(1)} %get-tuple-element.70), channel_id=1, source_target_pairs={{0,24},{4,28},{8,16},{12,20},{16,8},{20,12},{24,0},{28,4},{1,25},{... | collective-permute-start | bytes 245768 | tf_op jit(solution)/shard_map/ppermute | solution.py:245
  52.4 12.0 %collective-permute-start.14 = (f32[64,1536]{1,0:T(8,128)S(1)}, f32[64,1536]{1,0:T(8,128)S(1)}, u32[]{:S(2)}, u32[]{:S(2)}) collective-permute-start(f32[64,1536]{1,0:T(8,128)S(1)} %get-tuple-element.32), channel_id=1, source_target_pairs={{0,8},{4,12},{8,0},{12,4},{16,24},{20,28},{24,16},{28,20},{1,9},{5... | collective-permute-start | bytes 1179656 | tf_op jit(solution)/shard_map/ppermute | solution.py:245
  53.7 10.8 %collective-permute-start.15 = (f32[64,1536]{1,0:T(8,128)S(1)}, f32[64,1536]{1,0:T(8,128)S(1)}, u32[]{:S(2)}, u32[]{:S(2)}) collective-permute-start(f32[64,1536]{1,0:T(8,128)S(1)} %get-tuple-element.33), channel_id=1, source_target_pairs={{0,16},{4,20},{8,24},{12,28},{16,0},{20,4},{24,8},{28,12},{1,17},{... | collective-permute-start | bytes 1179656 | tf_op jit(solution)/shard_map/ppermute | solution.py:245
  54.5 6.6 %collective-permute-start.13 = (f32[160,128]{1,0:T(8,128)S(1)}, f32[160,128]{1,0:T(8,128)S(1)}, u32[]{:S(2)}, u32[]{:S(2)}) collective-permute-start(f32[160,128]{1,0:T(8,128)S(1)} %fusion), channel_id=1, source_target_pairs={{0,3},{1,2},{2,1},{3,0},{4,7},{5,6},{6,5},{7,4},{8,11},{9,10},{10,... | collective-permute-start | bytes 245768 | tf_op jit(solution)/shard_map/ppermute | solution.py:245
  58.1 6.2 %collective-permute-start.12 = (f32[160,128]{1,0:T(8,128)S(1)}, f32[160,128]{1,0:T(8,128)S(1)}, u32[]{:S(2)}, u32[]{:S(2)}) collective-permute-start(f32[160,128]{1,0:T(8,128)S(1)} %fusion), channel_id=1, source_target_pairs={{0,2},{1,3},{2,0},{3,1},{4,6},{5,7},{6,4},{7,5},{8,10},{9,11},{10,... | collective-permute-start | bytes 245768 | tf_op jit(solution)/shard_map/ppermute | solution.py:245
  58.1 6.2 %collective-permute-start.11 = (f32[160,128]{1,0:T(8,128)S(1)}, f32[160,128]{1,0:T(8,128)S(1)}, u32[]{:S(2)}, u32[]{:S(2)}) collective-permute-start(f32[160,128]{1,0:T(8,128)S(1)} %fusion), channel_id=1, source_target_pairs={{0,1},{1,0},{2,3},{3,2},{4,5},{5,4},{6,7},{7,6},{8,9},{9,8},{10,11... | collective-permute-start | bytes 245768 | tf_op jit(solution)/shard_map/ppermute | solution.py:245
  64.5 6.2 %collective-permute-start.21 = (f32[160,128]{1,0:T(8,128)S(1)}, f32[160,128]{1,0:T(8,128)S(1)}, u32[]{:S(2)}, u32[]{:S(2)}) collective-permute-start(f32[160,128]{1,0:T(8,128)S(1)} %add_add_fusion.refs_0_), channel_id=1, source_target_pairs={{0,24},{4,28},{8,16},{12,20},{16,8},{20,12},{24,0},{28,4},{1,25},{... | collective-permute-start | bytes 245768 | tf_op jit(solution)/shard_map/ppermute | solution.py:245
  65.9 5.1 %collective-permute-start.19 = (f32[160,128]{1,0:T(8,128)S(1)}, f32[160,128]{1,0:T(8,128)S(1)}, u32[]{:S(2)}, u32[]{:S(2)}) collective-permute-start(f32[160,128]{1,0:T(8,128)S(1)} %add_add_fusion.refs_0_), channel_id=1, source_target_pairs={{0,16},{4,20},{8,24},{12,28},{16,0},{20,4},{24,8},{28,12},{1,17},{... | collective-permute-start | bytes 245768 | tf_op jit(solution)/shard_map/ppermute | solution.py:245
  71.8 27.0 %collective-permute-start.26 = (f32[2,64,1536]{2,1,0:T(8,128)S(1)}, f32[2,64,1536]{2,1,0:T(8,128)S(1)}, u32[]{:S(2)}, u32[]{:S(2)}) collective-permute-start(f32[2,64,1536]{2,1,0:T(8,128)S(1)} %pad_maximum_fusion), channel_id=1, source_target_pairs={{0,24},{4,28},{8,16},{12,20},{16,8},{20,12},{24,0},{28,4},{1,25},{... | collective-permute-start | bytes 2359304 | tf_op jit(solution)/shard_map/ppermute | solution.py:245
  75.1 25.1 %collective-permute-start.23 = (f32[64,1536]{1,0:T(8,128)S(1)}, f32[64,1536]{1,0:T(8,128)S(1)}, u32[]{:S(2)}, u32[]{:S(2)}) collective-permute-start(f32[64,1536]{1,0:T(8,128)S(1)} %get-tuple-element.38), channel_id=1, source_target_pairs={{0,4},{4,0},{8,12},{12,8},{16,20},{20,16},{24,28},{28,24},{1,5},{5... | collective-permute-start | bytes 1179656 | tf_op jit(solution)/shard_map/ppermute | solution.py:245
  75.3 26.1 %collective-permute-start.24 = (f32[64,1536]{1,0:T(8,128)S(1)}, f32[64,1536]{1,0:T(8,128)S(1)}, u32[]{:S(2)}, u32[]{:S(2)}) collective-permute-start(f32[64,1536]{1,0:T(8,128)S(1)} %get-tuple-element.40), channel_id=1, source_target_pairs={{0,12},{4,8},{8,4},{12,0},{16,28},{20,24},{24,20},{28,16},{1,13},{... | collective-permute-start | bytes 1179656 | tf_op jit(solution)/shard_map/ppermute | solution.py:245
  76.1 25.3 %collective-permute-start.25 = (f32[64,1536]{1,0:T(8,128)S(1)}, f32[64,1536]{1,0:T(8,128)S(1)}, u32[]{:S(2)}, u32[]{:S(2)}) collective-permute-start(f32[64,1536]{1,0:T(8,128)S(1)} %get-tuple-element.42), channel_id=1, source_target_pairs={{0,20},{4,16},{8,28},{12,24},{16,4},{20,0},{24,12},{28,8},{1,21},{... | collective-permute-start | bytes 1179656 | tf_op jit(solution)/shard_map/ppermute | solution.py:245
  99.3 12.0 %collective-permute-start.33 = (f32[64,1536]{1,0:T(8,128)S(1)}, f32[64,1536]{1,0:T(8,128)S(1)}, u32[]{:S(2)}, u32[]{:S(2)}) collective-permute-start(f32[64,1536]{1,0:T(8,128)S(1)} %get-tuple-element.52), channel_id=1, source_target_pairs={{0,16},{4,20},{8,24},{12,28},{16,0},{20,4},{24,8},{28,12},{1,17},{... | collective-permute-start | bytes 1179656 | tf_op jit(solution)/shard_map/ppermute | solution.py:245
  100.2 12.0 %collective-permute-start.32 = (f32[64,1536]{1,0:T(8,128)S(1)}, f32[64,1536]{1,0:T(8,128)S(1)}, u32[]{:S(2)}, u32[]{:S(2)}) collective-permute-start(f32[64,1536]{1,0:T(8,128)S(1)} %get-tuple-element.44), channel_id=1, source_target_pairs={{0,8},{4,12},{8,0},{12,4},{16,24},{20,28},{24,16},{28,20},{1,9},{5... | collective-permute-start | bytes 1179656 | tf_op jit(solution)/shard_map/ppermute | solution.py:245
  103.5 8.7 %collective-permute-start.28 = (f32[64,768]{1,0:T(8,128)S(1)}, f32[64,768]{1,0:T(8,128)S(1)}, u32[]{:S(2)}, u32[]{:S(2)}) collective-permute-start(f32[64,768]{1,0:T(8,128)S(1)} %get-tuple-element.48), channel_id=1, source_target_pairs={{0,4},{4,0},{8,12},{12,8},{16,20},{20,16},{24,28},{28,24},{1,5},{5... | collective-permute-start | bytes 589832 | tf_op jit(solution)/shard_map/ppermute | solution.py:245
  103.6 14.8 %collective-permute-start.34 = (f32[64,1536]{1,0:T(8,128)S(1)}, f32[64,1536]{1,0:T(8,128)S(1)}, u32[]{:S(2)}, u32[]{:S(2)}) collective-permute-start(f32[64,1536]{1,0:T(8,128)S(1)} %get-tuple-element.53), channel_id=1, source_target_pairs={{0,12},{4,8},{8,4},{12,0},{16,28},{20,24},{24,20},{28,16},{1,13},{... | collective-permute-start | bytes 1179656 | tf_op jit(solution)/shard_map/ppermute | solution.py:245
  104.6 13.8 %collective-permute-start.35 = (f32[64,1536]{1,0:T(8,128)S(1)}, f32[64,1536]{1,0:T(8,128)S(1)}, u32[]{:S(2)}, u32[]{:S(2)}) collective-permute-start(f32[64,1536]{1,0:T(8,128)S(1)} %get-tuple-element.54), channel_id=1, source_target_pairs={{0,20},{4,16},{8,28},{12,24},{16,4},{20,0},{24,12},{28,8},{1,21},{... | collective-permute-start | bytes 1179656 | tf_op jit(solution)/shard_map/ppermute | solution.py:245
  (12 other events, 29.7 us)

commit v3 on v2

--- a/solution.py
+++ b/solution.py
@@ -298,18 +298,19 @@
     def block(x, j):
         return lax.dynamic_slice(x, (0, j * width), (rows, width))
 
-    far = (opposite + 1, opposite)
+    far = opposite + 1
     odd, even = list(range(3, n - 2, 2)), list(range(2, n - 2, 2))
-    blocks = {k: block(tensor, me ^ k) for k in far}
-    rest = after(tensor, *blocks.values())
-    blocks |= {k: block(rest, me ^ k) for k in range(n - 2)}
+    blocks = {far: block(tensor, me ^ far)}
+    rest = after(tensor, blocks[far])
+    blocks |= {k: block(rest, me ^ k) for k in range(far)}
     parts = [permute(blocks[k], "fibre", k) if k else blocks[0] for k in range(n)]
     twin = [block(rest, me ^ k ^ opposite) for k in range(opposite)] + [None, None]
     mine, theirs, high, low = gram_packed(parts, 1.0 / (width * n * groups))
     mine = (mine + permute(theirs, "fibre", 1)).reshape(chips, -1, LANES)
-    piece = tree_sum([mine[k] if k == 0 else permute(mine[k], "fibre", 2 * k) for k in range(chips)])
+    terms = [mine[k] if k == 0 else permute(mine[k], "fibre", 2 * k) for k in range(chips)]
     for k in even:
-        twin[k] = permute(after(twin[k], piece), "fibre", k)
+        twin[k] = permute(after(twin[k], terms[-1]), "fibre", k)
+    piece = tree_sum(terms)
     piece = tree_sum([piece if k == 0 else permute(piece, "group", k) for k in range(groups)])
     piece, *arrived = lax.optimization_barrier((piece, *[twin[k] for k in even]))
     for k, x in zip(even, arrived, strict=True):

time: 120 us -> 119 us (level)
  waiting for transfers between devices: 53.3 us -> 48.7 us
  starting transfers between devices: 32.1 us -> 35.8 us
    ppermute x36, waiting for transfers between devices: 53.3 us -> 48.7 us  [permute(): lax.ppermute(x, axis, [(i, i ^ bits) for i in range(lax.axis_size(axis))])]
    ppermute x36, starting transfers between devices: 32.1 us -> 35.8 us  [permute(): lax.ppermute(x, axis, [(i, i ^ bits) for i in range(lax.axis_size(axis))])]
  transfers between devices with their start and end apart: 36 -> 36, of which waited for: 23 -> 20; matrix products, arithmetic and copies ran while one was open for 2% -> 2% of each run, Pallas kernels for 21% -> 22%
where the time goes in v3:
time: 119 us; the launch traced here: 118 us
  waiting for transfers between devices  48.7 us (41%)
  starting transfers between devices  35.8 us (30%)
  Pallas kernels  29 us (24%)
  local copies, waits for them, and re-layouts  3.77 us (3%)
    ppermute x36, waiting for transfers between devices, permute(): lax.ppermute(x, axis, [(i, i ^ bits) for i in range(lax.axis_size(axis))])  48.7 us
    ppermute x36, starting transfers between devices, permute(): lax.ppermute(x, axis, [(i, i ^ bits) for i in range(lax.axis_size(axis))])  35.8 us
    pallas_call x1, Pallas kernels, factor_and_inverse(): pl.pallas_call(functools.partial(factor_kernel, m, n), out_shape=[jax.Sha...  20.5 us
    dynamic_slice x2, local copies, waits for them, and re-layouts, block(): return lax.dynamic_slice(x, (0, j * width), (rows, width))  3.73 us
    pallas_call x1, Pallas kernels, gram_packed(): pl.pallas_call(functools.partial(gram_kernel, scale, n), out_shape=[half,...  2.69 us
  transfers between devices with their start and end apart: 36, of which 20 were waited for; matrix products, arithmetic and copies ran while one was open for 2% of the time, Pallas kernels for 22%

profile of v3, /device:TPU:0, one launch (start us, length us, event | category | flops | bytes accessed | tf_op | source)
XLA Modules:
  0.0 118.4 jit_solution(5229257466104461716)
XLA Ops:
  1.7 3.4 %collective-permute-start.6 = (f32[64,1536]{1,0:T(8,128)S(1)}, f32[64,1536]{1,0:T(8,128)S(1)}, u32[]{:S(2)}, u32[]{:S(2)}) collective-permute-start(f32[64,1536]{1,0:T(8,128)S(1)} %constant_dynamic-slice_fusion.12), channel_id=1, source_target_pairs={{0,28},{4,24},{8,20},{12,16},{16,12},{20,8},{24,4},{28,0},{1,29},{... | collective-permute-start | bytes 1179656 | tf_op jit(solution)/shard_map/ppermute | solution.py:245
  5.1 2.7 %constant_dynamic-slice_fusion = (f32[64,1536]{1,0:T(8,128)S(1)}, f32[64,1536]{1,0:T(8,128)S(1)}, f32[64,1536]{1,0:T(8,128)S(1)}, f32[64,1536]{1,0:T(8,128)S(1)}...) fusion(f32[64,12288]{1,0:T(8,128)} %param.1, ...), kind=kLoop, calls=%fused_computation.5 | loop fusion | bytes 9437232 | tf_op jit(solution)/shard_map/dynamic_slice | solution.py:299
  8.6 1.6 %collective-permute-start.3 = (f32[64,1536]{1,0:T(8,128)S(1)}, f32[64,1536]{1,0:T(8,128)S(1)}, u32[]{:S(2)}, u32[]{:S(2)}) collective-permute-start(f32[64,1536]{1,0:T(8,128)S(1)} %get-tuple-element.63), channel_id=1, source_target_pairs={{0,16},{4,20},{8,24},{12,28},{16,0},{20,4},{24,8},{28,12},{1,17},{... | collective-permute-start | bytes 1179656 | tf_op jit(solution)/shard_map/ppermute | solution.py:245
  11.3 3.3 %collective-permute-done.6.refs_7_ = f32[64,1536]{1,0:T(8,128)S(1)} collective-permute-done((f32[64,1536]{1,0:T(8,128)S(1)}, f32[64,1536]{1,0:T(8,128)S(1)}, u32[]{:S(2)}, u32[]{:S(2)}) %collective-permute-start.6) | collective-permute-done | bytes 393248 | tf_op jit(solution)/shard_map/ppermute | solution.py:245
  14.6 3.4 %collective-permute-start.5 = (f32[64,1536]{1,0:T(8,128)S(1)}, f32[64,1536]{1,0:T(8,128)S(1)}, u32[]{:S(2)}, u32[]{:S(2)}) collective-permute-start(f32[64,1536]{1,0:T(8,128)S(1)} %get-tuple-element.61.refs_0_), channel_id=1, source_target_pairs={{0,24},{4,28},{8,16},{12,20},{16,8},{20,12},{24,0},{28,4},{1,25},{... | collective-permute-start | bytes 1179656 | tf_op jit(solution)/shard_map/ppermute | solution.py:245
  18.0 5.1 %collective-permute-done.4.refs_5_ = f32[64,1536]{1,0:T(8,128)S(1)} collective-permute-done((f32[64,1536]{1,0:T(8,128)S(1)}, f32[64,1536]{1,0:T(8,128)S(1)}, u32[]{:S(2)}, u32[]{:S(2)}) %collective-permute-start.4) | collective-permute-done | bytes 393248 | tf_op jit(solution)/shard_map/ppermute | solution.py:245
  23.4 9.0 %collective-permute-done.3.refs_4_ = f32[64,1536]{1,0:T(8,128)S(1)} collective-permute-done((f32[64,1536]{1,0:T(8,128)S(1)}, f32[64,1536]{1,0:T(8,128)S(1)}, u32[]{:S(2)}, u32[]{:S(2)}) %collective-permute-start.3) | collective-permute-done | bytes 393248 | tf_op jit(solution)/shard_map/ppermute | solution.py:245
  32.5 7.6 %collective-permute-done.5.refs_6_ = f32[64,1536]{1,0:T(8,128)S(1)} collective-permute-done((f32[64,1536]{1,0:T(8,128)S(1)}, f32[64,1536]{1,0:T(8,128)S(1)}, u32[]{:S(2)}, u32[]{:S(2)}) %collective-permute-start.5) | collective-permute-done | bytes 393248 | tf_op jit(solution)/shard_map/ppermute | solution.py:245
  40.1 2.7 %gram.1 = (f32[640,128]{1,0:T(8,128)S(1)}, f32[640,128]{1,0:T(8,128)S(1)}, bf16[512,1536]{1,0:T(8,128)(2,1)S(1)}, bf16[512,1536]{1,0:T(8,128)(2,1)S(1)}) custom-call(f32[64,1536]{1,0:T(8,128)S(1)} %get-tuple-element.67.refs_0_, f32[64,1536]{1,0:T(8,128)S(1)} %collective-permute-done.refs_1_, f32[64,1536]{1,0:T(8,128)S(1)} %collective-permute-done.1.refs_2_, ...), custom_call_target="tpu_custom_call" | custom-call | flops 1024 | bytes 1024 | tf_op jit(solution)/shard_map/gram/pallas_call | solution.py:88
  42.8 1.6 %collective-permute-done.7 = f32[640,128]{1,0:T(8,128)S(1)} collective-permute-done((f32[640,128]{1,0:T(8,128)S(1)}, f32[640,128]{1,0:T(8,128)S(1)}, u32[]{:S(2)}, u32[]{:S(2)}) %collective-permute-start.7) | collective-permute-done | bytes 327712 | tf_op jit(solution)/shard_map/ppermute | solution.py:245
  44.5 3.3 %collective-permute-start.10 = (f32[160,128]{1,0:T(8,128)S(1)}, f32[160,128]{1,0:T(8,128)S(1)}, u32[]{:S(2)}, u32[]{:S(2)}) collective-permute-start(f32[160,128]{1,0:T(8,128)S(1)} %get-tuple-element.68), channel_id=1, source_target_pairs={{0,24},{4,28},{8,16},{12,20},{16,8},{20,12},{24,0},{28,4},{1,25},{... | collective-permute-start | bytes 245768 | tf_op jit(solution)/shard_map/ppermute | solution.py:245
  48.4 2.2 %collective-permute-done.10 = f32[160,128]{1,0:T(8,128)S(1)} collective-permute-done((f32[160,128]{1,0:T(8,128)S(1)}, f32[160,128]{1,0:T(8,128)S(1)}, u32[]{:S(2)}, u32[]{:S(2)}) %collective-permute-start.10) | collective-permute-done | bytes 81952 | tf_op jit(solution)/shard_map/ppermute | solution.py:245
  50.6 1.9 %collective-permute-start.14 = (f32[64,1536]{1,0:T(8,128)S(1)}, f32[64,1536]{1,0:T(8,128)S(1)}, u32[]{:S(2)}, u32[]{:S(2)}) collective-permute-start(f32[64,1536]{1,0:T(8,128)S(1)} %get-tuple-element.32), channel_id=1, source_target_pairs={{0,8},{4,12},{8,0},{12,4},{16,24},{20,28},{24,16},{28,20},{1,9},{5... | collective-permute-start | bytes 1179656 | tf_op jit(solution)/shard_map/ppermute | solution.py:245
  52.5 2.0 %collective-permute-start.15 = (f32[64,1536]{1,0:T(8,128)S(1)}, f32[64,1536]{1,0:T(8,128)S(1)}, u32[]{:S(2)}, u32[]{:S(2)}) collective-permute-start(f32[64,1536]{1,0:T(8,128)S(1)} %get-tuple-element.33), channel_id=1, source_target_pairs={{0,16},{4,20},{8,24},{12,28},{16,0},{20,4},{24,8},{28,12},{1,17},{... | collective-permute-start | bytes 1179656 | tf_op jit(solution)/shard_map/ppermute | solution.py:245
  54.6 3.7 %collective-permute-start.13 = (f32[160,128]{1,0:T(8,128)S(1)}, f32[160,128]{1,0:T(8,128)S(1)}, u32[]{:S(2)}, u32[]{:S(2)}) collective-permute-start(f32[160,128]{1,0:T(8,128)S(1)} %fusion), channel_id=1, source_target_pairs={{0,3},{1,2},{2,1},{3,0},{4,7},{5,6},{6,5},{7,4},{8,11},{9,10},{10,... | collective-permute-start | bytes 245768 | tf_op jit(solution)/shard_map/ppermute | solution.py:245
  59.1 2.2 %collective-permute-done.13 = f32[160,128]{1,0:T(8,128)S(1)} collective-permute-done((f32[160,128]{1,0:T(8,128)S(1)}, f32[160,128]{1,0:T(8,128)S(1)}, u32[]{:S(2)}, u32[]{:S(2)}) %collective-permute-start.13) | collective-permute-done | bytes 81952 | tf_op jit(solution)/shard_map/ppermute | solution.py:245
  61.3 2.4 %collective-permute-done.12 = f32[160,128]{1,0:T(8,128)S(1)} collective-permute-done((f32[160,128]{1,0:T(8,128)S(1)}, f32[160,128]{1,0:T(8,128)S(1)}, u32[]{:S(2)}, u32[]{:S(2)}) %collective-permute-start.12) | collective-permute-done | bytes 81952 | tf_op jit(solution)/shard_map/ppermute | solution.py:245
  64.3 2.0 %collective-permute-start.19 = (f32[160,128]{1,0:T(8,128)S(1)}, f32[160,128]{1,0:T(8,128)S(1)}, u32[]{:S(2)}, u32[]{:S(2)}) collective-permute-start(f32[160,128]{1,0:T(8,128)S(1)} %add_add_fusion.refs_0_), channel_id=1, source_target_pairs={{0,16},{4,20},{8,24},{12,28},{16,0},{20,4},{24,8},{28,12},{1,17},{... | collective-permute-start | bytes 245768 | tf_op jit(solution)/shard_map/ppermute | solution.py:245
  67.4 2.3 %collective-permute-done.21.refs_6_ = f32[160,128]{1,0:T(8,128)S(1)} collective-permute-done((f32[160,128]{1,0:T(8,128)S(1)}, f32[160,128]{1,0:T(8,128)S(1)}, u32[]{:S(2)}, u32[]{:S(2)}) %collective-permute-start.21) | collective-permute-done | bytes 81952 | tf_op jit(solution)/shard_map/ppermute | solution.py:245
  70.7 1.5 %collective-permute-start.26 = (f32[2,64,1536]{2,1,0:T(8,128)S(1)}, f32[2,64,1536]{2,1,0:T(8,128)S(1)}, u32[]{:S(2)}, u32[]{:S(2)}) collective-permute-start(f32[2,64,1536]{2,1,0:T(8,128)S(1)} %pad_maximum_fusion), channel_id=1, source_target_pairs={{0,24},{4,28},{8,16},{12,20},{16,8},{20,12},{24,0},{28,4},{1,25},{... | collective-permute-start | bytes 2359304 | tf_op jit(solution)/shard_map/ppermute | solution.py:245
  75.9 20.5 %factor.1 = (f32[512,512]{1,0:T(8,128)}, f32[512,512]{1,0:T(8,128)S(1)}) custom-call(f32[160,128]{1,0:T(8,128)S(1)} %add_add_fusion.refs_0_, f32[160,128]{1,0:T(8,128)S(1)} %collective-permute-done.16.refs_1_, f32[160,128]{1,0:T(8,128)S(1)} %collective-permute-done.17.refs_2_, f32[160,128]{1,0:T(8,128)S(1)} %collective-permute-done.18.refs_3_, ...), custom_call_target="tpu_custom_call" | custom-call | flops 1024 | bytes 1024 | tf_op jit(solution)/shard_map/factor/pallas_call | solution.py:169
  100.3 2.1 %keep_rows.1 = (f32[64,1536]{1,0:T(8,128)S(1)}, f32[64,768]{1,0:T(8,128)S(1)}, f32[64,768]{1,0:T(8,128)S(1)}, f32[64,1536]{1,0:T(8,128)S(1)}, f32[64,768]{1,0:T(8,128)S(1)}, /*index=5*/f32[64,768]{1,0:T(8,128)S(1)}) custom-call(f32[512,512]{1,0:T(8,128)S(1)} %get-tuple-element.35.w_ref, bf16[512,1536]{1,0:T(8,128)(2,1)S(1)} %get-tuple-element.36.high, ...), custom_call_target="tpu_custom_call" | custom-call | flops 1024 | bytes 1024 | tf_op jit(solution)/shard_map/keep_rows/pallas_call | solution.py:234
  104.3 5.9 %collective-permute-done.33.refs_7_ = f32[64,1536]{1,0:T(8,128)S(1)} collective-permute-done((f32[64,1536]{1,0:T(8,128)S(1)}, f32[64,1536]{1,0:T(8,128)S(1)}, u32[]{:S(2)}, u32[]{:S(2)}) %collective-permute-start.33) | collective-permute-done | bytes 393248 | tf_op jit(solution)/shard_map/ppermute | solution.py:245
  114.3 3.0 %collective-permute-done.34.refs_1_ = f32[64,1536]{1,0:T(8,128)S(1)} collective-permute-done((f32[64,1536]{1,0:T(8,128)S(1)}, f32[64,1536]{1,0:T(8,128)S(1)}, u32[]{:S(2)}, u32[]{:S(2)}) %collective-permute-start.34) | collective-permute-done | bytes 393248 | tf_op jit(solution)/shard_map/ppermute | solution.py:245
  (62 shorter events, 22.1 us)
Async XLA Ops:
  1.7 12.9 %collective-permute-start.6 = (f32[64,1536]{1,0:T(8,128)S(1)}, f32[64,1536]{1,0:T(8,128)S(1)}, u32[]{:S(2)}, u32[]{:S(2)}) collective-permute-start(f32[64,1536]{1,0:T(8,128)S(1)} %constant_dynamic-slice_fusion.12), channel_id=1, source_target_pairs={{0,28},{4,24},{8,20},{12,16},{16,12},{20,8},{24,4},{28,0},{1,29},{... | collective-permute-start | bytes 1179656 | tf_op jit(solution)/shard_map/ppermute | solution.py:245
  7.8 15.3 %collective-permute-start.4 = (f32[64,1536]{1,0:T(8,128)S(1)}, f32[64,1536]{1,0:T(8,128)S(1)}, u32[]{:S(2)}, u32[]{:S(2)}) collective-permute-start(f32[64,1536]{1,0:T(8,128)S(1)} %get-tuple-element.62), channel_id=1, source_target_pairs={{0,20},{4,16},{8,28},{12,24},{16,4},{20,0},{24,12},{28,8},{1,21},{... | collective-permute-start | bytes 1179656 | tf_op jit(solution)/shard_map/ppermute | solution.py:245
  8.6 23.8 %collective-permute-start.3 = (f32[64,1536]{1,0:T(8,128)S(1)}, f32[64,1536]{1,0:T(8,128)S(1)}, u32[]{:S(2)}, u32[]{:S(2)}) collective-permute-start(f32[64,1536]{1,0:T(8,128)S(1)} %get-tuple-element.63), channel_id=1, source_target_pairs={{0,16},{4,20},{8,24},{12,28},{16,0},{20,4},{24,8},{28,12},{1,17},{... | collective-permute-start | bytes 1179656 | tf_op jit(solution)/shard_map/ppermute | solution.py:245
  10.2 22.2 %collective-permute-start.2 = (f32[64,1536]{1,0:T(8,128)S(1)}, f32[64,1536]{1,0:T(8,128)S(1)}, u32[]{:S(2)}, u32[]{:S(2)}) collective-permute-start(f32[64,1536]{1,0:T(8,128)S(1)} %get-tuple-element.64), channel_id=1, source_target_pairs={{0,12},{4,8},{8,4},{12,0},{16,28},{20,24},{24,20},{28,16},{1,13},{... | collective-permute-start | bytes 1179656 | tf_op jit(solution)/shard_map/ppermute | solution.py:245
  10.2 22.3 %collective-permute-start.1 = (f32[64,1536]{1,0:T(8,128)S(1)}, f32[64,1536]{1,0:T(8,128)S(1)}, u32[]{:S(2)}, u32[]{:S(2)}) collective-permute-start(f32[64,1536]{1,0:T(8,128)S(1)} %get-tuple-element.65), channel_id=1, source_target_pairs={{0,8},{4,12},{8,0},{12,4},{16,24},{20,28},{24,16},{28,20},{1,9},{5... | collective-permute-start | bytes 1179656 | tf_op jit(solution)/shard_map/ppermute | solution.py:245
  14.6 25.4 %collective-permute-start.5 = (f32[64,1536]{1,0:T(8,128)S(1)}, f32[64,1536]{1,0:T(8,128)S(1)}, u32[]{:S(2)}, u32[]{:S(2)}) collective-permute-start(f32[64,1536]{1,0:T(8,128)S(1)} %get-tuple-element.61.refs_0_), channel_id=1, source_target_pairs={{0,24},{4,28},{8,16},{12,20},{16,8},{20,12},{24,0},{28,4},{1,25},{... | collective-permute-start | bytes 1179656 | tf_op jit(solution)/shard_map/ppermute | solution.py:245
  23.1 17.0 %collective-permute-start = (f32[64,1536]{1,0:T(8,128)S(1)}, f32[64,1536]{1,0:T(8,128)S(1)}, u32[]{:S(2)}, u32[]{:S(2)}) collective-permute-start(f32[64,1536]{1,0:T(8,128)S(1)} %get-tuple-element.66), channel_id=1, source_target_pairs={{0,4},{4,0},{8,12},{12,8},{16,20},{20,16},{24,28},{28,24},{1,5},{5... | collective-permute-start | bytes 1179656 | tf_op jit(solution)/shard_map/ppermute | solution.py:245
  44.5 6.1 %collective-permute-start.10 = (f32[160,128]{1,0:T(8,128)S(1)}, f32[160,128]{1,0:T(8,128)S(1)}, u32[]{:S(2)}, u32[]{:S(2)}) collective-permute-start(f32[160,128]{1,0:T(8,128)S(1)} %get-tuple-element.68), channel_id=1, source_target_pairs={{0,24},{4,28},{8,16},{12,20},{16,8},{20,12},{24,0},{28,4},{1,25},{... | collective-permute-start | bytes 245768 | tf_op jit(solution)/shard_map/ppermute | solution.py:245
  47.8 6.8 %collective-permute-start.9 = (f32[160,128]{1,0:T(8,128)S(1)}, f32[160,128]{1,0:T(8,128)S(1)}, u32[]{:S(2)}, u32[]{:S(2)}) collective-permute-start(f32[160,128]{1,0:T(8,128)S(1)} %get-tuple-element.69), channel_id=1, source_target_pairs={{0,16},{4,20},{8,24},{12,28},{16,0},{20,4},{24,8},{28,12},{1,17},{... | collective-permute-start | bytes 245768 | tf_op jit(solution)/shard_map/ppermute | solution.py:245
  48.3 6.3 %collective-permute-start.8 = (f32[160,128]{1,0:T(8,128)S(1)}, f32[160,128]{1,0:T(8,128)S(1)}, u32[]{:S(2)}, u32[]{:S(2)}) collective-permute-start(f32[160,128]{1,0:T(8,128)S(1)} %get-tuple-element.70), channel_id=1, source_target_pairs={{0,8},{4,12},{8,0},{12,4},{16,24},{20,28},{24,16},{28,20},{1,9},{5... | collective-permute-start | bytes 245768 | tf_op jit(solution)/shard_map/ppermute | solution.py:245
  50.6 13.1 %collective-permute-start.14 = (f32[64,1536]{1,0:T(8,128)S(1)}, f32[64,1536]{1,0:T(8,128)S(1)}, u32[]{:S(2)}, u32[]{:S(2)}) collective-permute-start(f32[64,1536]{1,0:T(8,128)S(1)} %get-tuple-element.32), channel_id=1, source_target_pairs={{0,8},{4,12},{8,0},{12,4},{16,24},{20,28},{24,16},{28,20},{1,9},{5... | collective-permute-start | bytes 1179656 | tf_op jit(solution)/shard_map/ppermute | solution.py:245
  52.5 11.2 %collective-permute-start.15 = (f32[64,1536]{1,0:T(8,128)S(1)}, f32[64,1536]{1,0:T(8,128)S(1)}, u32[]{:S(2)}, u32[]{:S(2)}) collective-permute-start(f32[64,1536]{1,0:T(8,128)S(1)} %get-tuple-element.33), channel_id=1, source_target_pairs={{0,16},{4,20},{8,24},{12,28},{16,0},{20,4},{24,8},{28,12},{1,17},{... | collective-permute-start | bytes 1179656 | tf_op jit(solution)/shard_map/ppermute | solution.py:245
  54.6 6.7 %collective-permute-start.13 = (f32[160,128]{1,0:T(8,128)S(1)}, f32[160,128]{1,0:T(8,128)S(1)}, u32[]{:S(2)}, u32[]{:S(2)}) collective-permute-start(f32[160,128]{1,0:T(8,128)S(1)} %fusion), channel_id=1, source_target_pairs={{0,3},{1,2},{2,1},{3,0},{4,7},{5,6},{6,5},{7,4},{8,11},{9,10},{10,... | collective-permute-start | bytes 245768 | tf_op jit(solution)/shard_map/ppermute | solution.py:245
  63.7 5.9 %collective-permute-start.21 = (f32[160,128]{1,0:T(8,128)S(1)}, f32[160,128]{1,0:T(8,128)S(1)}, u32[]{:S(2)}, u32[]{:S(2)}) collective-permute-start(f32[160,128]{1,0:T(8,128)S(1)} %add_add_fusion.refs_0_), channel_id=1, source_target_pairs={{0,24},{4,28},{8,16},{12,20},{16,8},{20,12},{24,0},{28,4},{1,25},{... | collective-permute-start | bytes 245768 | tf_op jit(solution)/shard_map/ppermute | solution.py:245
  64.3 5.4 %collective-permute-start.19 = (f32[160,128]{1,0:T(8,128)S(1)}, f32[160,128]{1,0:T(8,128)S(1)}, u32[]{:S(2)}, u32[]{:S(2)}) collective-permute-start(f32[160,128]{1,0:T(8,128)S(1)} %add_add_fusion.refs_0_), channel_id=1, source_target_pairs={{0,16},{4,20},{8,24},{12,28},{16,0},{20,4},{24,8},{28,12},{1,17},{... | collective-permute-start | bytes 245768 | tf_op jit(solution)/shard_map/ppermute | solution.py:245
  70.7 27.0 %collective-permute-start.26 = (f32[2,64,1536]{2,1,0:T(8,128)S(1)}, f32[2,64,1536]{2,1,0:T(8,128)S(1)}, u32[]{:S(2)}, u32[]{:S(2)}) collective-permute-start(f32[2,64,1536]{2,1,0:T(8,128)S(1)} %pad_maximum_fusion), channel_id=1, source_target_pairs={{0,24},{4,28},{8,16},{12,20},{16,8},{20,12},{24,0},{28,4},{1,25},{... | collective-permute-start | bytes 2359304 | tf_op jit(solution)/shard_map/ppermute | solution.py:245
  74.0 25.1 %collective-permute-start.23 = (f32[64,1536]{1,0:T(8,128)S(1)}, f32[64,1536]{1,0:T(8,128)S(1)}, u32[]{:S(2)}, u32[]{:S(2)}) collective-permute-start(f32[64,1536]{1,0:T(8,128)S(1)} %get-tuple-element.38), channel_id=1, source_target_pairs={{0,4},{4,0},{8,12},{12,8},{16,20},{20,16},{24,28},{28,24},{1,5},{5... | collective-permute-start | bytes 1179656 | tf_op jit(solution)/shard_map/ppermute | solution.py:245
  74.2 26.1 %collective-permute-start.24 = (f32[64,1536]{1,0:T(8,128)S(1)}, f32[64,1536]{1,0:T(8,128)S(1)}, u32[]{:S(2)}, u32[]{:S(2)}) collective-permute-start(f32[64,1536]{1,0:T(8,128)S(1)} %get-tuple-element.40), channel_id=1, source_target_pairs={{0,12},{4,8},{8,4},{12,0},{16,28},{20,24},{24,20},{28,16},{1,13},{... | collective-permute-start | bytes 1179656 | tf_op jit(solution)/shard_map/ppermute | solution.py:245
  75.0 25.3 %collective-permute-start.25 = (f32[64,1536]{1,0:T(8,128)S(1)}, f32[64,1536]{1,0:T(8,128)S(1)}, u32[]{:S(2)}, u32[]{:S(2)}) collective-permute-start(f32[64,1536]{1,0:T(8,128)S(1)} %get-tuple-element.42), channel_id=1, source_target_pairs={{0,20},{4,16},{8,28},{12,24},{16,4},{20,0},{24,12},{28,8},{1,21},{... | collective-permute-start | bytes 1179656 | tf_op jit(solution)/shard_map/ppermute | solution.py:245
  98.2 12.0 %collective-permute-start.33 = (f32[64,1536]{1,0:T(8,128)S(1)}, f32[64,1536]{1,0:T(8,128)S(1)}, u32[]{:S(2)}, u32[]{:S(2)}) collective-permute-start(f32[64,1536]{1,0:T(8,128)S(1)} %get-tuple-element.52), channel_id=1, source_target_pairs={{0,16},{4,20},{8,24},{12,28},{16,0},{20,4},{24,8},{28,12},{1,17},{... | collective-permute-start | bytes 1179656 | tf_op jit(solution)/shard_map/ppermute | solution.py:245
  99.2 12.0 %collective-permute-start.32 = (f32[64,1536]{1,0:T(8,128)S(1)}, f32[64,1536]{1,0:T(8,128)S(1)}, u32[]{:S(2)}, u32[]{:S(2)}) collective-permute-start(f32[64,1536]{1,0:T(8,128)S(1)} %get-tuple-element.44), channel_id=1, source_target_pairs={{0,8},{4,12},{8,0},{12,4},{16,24},{20,28},{24,16},{28,20},{1,9},{5... | collective-permute-start | bytes 1179656 | tf_op jit(solution)/shard_map/ppermute | solution.py:245
  102.4 8.7 %collective-permute-start.28 = (f32[64,768]{1,0:T(8,128)S(1)}, f32[64,768]{1,0:T(8,128)S(1)}, u32[]{:S(2)}, u32[]{:S(2)}) collective-permute-start(f32[64,768]{1,0:T(8,128)S(1)} %get-tuple-element.48), channel_id=1, source_target_pairs={{0,4},{4,0},{8,12},{12,8},{16,20},{20,16},{24,28},{28,24},{1,5},{5... | collective-permute-start | bytes 589832 | tf_op jit(solution)/shard_map/ppermute | solution.py:245
  102.5 14.8 %collective-permute-start.34 = (f32[64,1536]{1,0:T(8,128)S(1)}, f32[64,1536]{1,0:T(8,128)S(1)}, u32[]{:S(2)}, u32[]{:S(2)}) collective-permute-start(f32[64,1536]{1,0:T(8,128)S(1)} %get-tuple-element.53), channel_id=1, source_target_pairs={{0,12},{4,8},{8,4},{12,0},{16,28},{20,24},{24,20},{28,16},{1,13},{... | collective-permute-start | bytes 1179656 | tf_op jit(solution)/shard_map/ppermute | solution.py:245
  103.5 13.8 %collective-permute-start.35 = (f32[64,1536]{1,0:T(8,128)S(1)}, f32[64,1536]{1,0:T(8,128)S(1)}, u32[]{:S(2)}, u32[]{:S(2)}) collective-permute-start(f32[64,1536]{1,0:T(8,128)S(1)} %get-tuple-element.54), channel_id=1, source_target_pairs={{0,20},{4,16},{8,28},{12,24},{16,4},{20,0},{24,12},{28,8},{1,21},{... | collective-permute-start | bytes 1179656 | tf_op jit(solution)/shard_map/ppermute | solution.py:245
  (12 other events, 31.3 us)

commit v4 on v3

--- a/solution.py
+++ b/solution.py
@@ -99,42 +99,61 @@
     return jnp.broadcast_to(v[:, j : j + 1], (SUB, LANES))
 
 
-def along_sublanes(v, s):
-    return jnp.broadcast_to(v[s : s + 1, :], (SUB, LANES))
-
-
-def factor_block(x, z):
+def along_sublanes(ref, s):
+    return jnp.broadcast_to(ref[s : s + 1, :], (SUB, LANES))
+
+
+def factor_block(x, z, x_ref, z_ref, c_ref):
     sub = lax.broadcasted_iota(jnp.int32, (SUB, LANES), 0)
+    eight = range(SUB)
     for g in range(len(x)):
-        cols = [along_lanes(x[g], SUB * g + t) for t in range(SUB)]
-        x_rows, z_rows, inverses, r = [], [], [], {}
-        xg, zg = x[g], z[g]
-        for t in range(SUB):
-            inverse = lax.rsqrt(along_sublanes(cols[t], t))
-            m = jnp.where(sub > t, cols[t] * inverse, 0.0)
-            x_row, z_row = along_sublanes(xg, t) * inverse, along_sublanes(zg, t) * inverse
-            xg = jnp.where(sub == t, x_row, xg - m * x_row)
-            zg = jnp.where(sub == t, z_row, zg - m * z_row)
+        at = SUB * g
+        x_ref[at : at + SUB, :], z_ref[at : at + SUB, :] = x[g], z[g]
+        for t in eight:
+            c_ref[SUB * (at + t) : SUB * (at + t + 1), :] = along_lanes(x[g], at + t)
+        d = {(t, u): along_sublanes(c_ref, SUB * (at + u) + t) for u in eight for t in range(u + 1)}
+        x_rows = [along_sublanes(x_ref, at + t) for t in eight]
+        z_rows = [along_sublanes(z_ref, at + t) for t in eight]
+        scale, r = [], {}
+        for t in eight:
+            scale.append(lax.rsqrt(d[t, t]))
+            inverse = scale[t] * scale[t]
+            x_rows[t], z_rows[t] = x_rows[t] * scale[t], z_rows[t] * scale[t]
             for u in range(t + 1, SUB):
-                r[t, u] = along_sublanes(cols[u], t) * inverse
-                cols[u] = cols[u] - m * r[t, u]
-            x_rows.append(x_row)
-            z_rows.append(z_row)
-            inverses.append(inverse)
-        x[g], z[g] = xg, zg
-        for h in range(g + 1, len(x)):
-            cols = [along_lanes(x[h], SUB * g + t) for t in range(SUB)]
-            for t in range(SUB):
-                cols[t] = cols[t] * inverses[t]
+                for v in range(t + 1, u + 1):
+                    d[v, u] = d[v, u] - (d[t, v] * d[t, u]) * inverse
+                r[t, u] = d[t, u] * scale[t]
+                x_rows[u] = x_rows[u] - r[t, u] * x_rows[t]
+                z_rows[u] = z_rows[u] - r[t, u] * z_rows[t]
+        x[g], z[g] = x_rows[0], z_rows[0]
+        for t in range(1, SUB):
+            x[g], z[g] = jnp.where(sub == t, x_rows[t], x[g]), jnp.where(sub == t, z_rows[t], z[g])
+        if g + 1 < len(x):
+            cols = [along_lanes(x[g + 1], at + t) for t in eight]
+            for t in eight:
+                cols[t] = cols[t] * scale[t]
                 for u in range(t + 1, SUB):
                     cols[u] = cols[u] - cols[t] * r[t, u]
-                x[h] = x[h] - cols[t] * x_rows[t]
-                z[h] = z[h] - cols[t] * z_rows[t]
+                x[g + 1] = x[g + 1] - cols[t] * x_rows[t]
+                z[g + 1] = z[g + 1] - cols[t] * z_rows[t]
+        for t in reversed(eight):
+            for u in range(t + 1, SUB):
+                x_rows[t] = x_rows[t] - r[t, u] * x_rows[u]
+                z_rows[t] = z_rows[t] - r[t, u] * z_rows[u]
+            x_rows[t], z_rows[t] = x_rows[t] * scale[t], z_rows[t] * scale[t]
+        for h in range(g + 2, len(x)):
+            for t in eight:
+                col = along_lanes(x[h], at + t)
+                if t == 0:
+                    x_sum, z_sum = col * x_rows[t], col * z_rows[t]
+                else:
+                    x_sum, z_sum = x_sum + col * x_rows[t], z_sum + col * z_rows[t]
+            x[h], z[h] = x[h] - x_sum, z[h] - z_sum
     return jnp.concatenate(x, 0), jnp.concatenate(z, 0)
 
 
 def factor_kernel(m, n, *refs):
-    pieces, (l_ref, w_ref, a_ref, packed) = refs[:n], refs[n:]
+    pieces, (l_ref, w_ref, a_ref, packed, *spare) = refs[:n], refs[n:]
     piece = pieces[0].shape[0]
     me = fibre_index()
     for k, part in enumerate(pieces):
@@ -150,7 +169,7 @@
         ks = slice(k, k + LANES)
         x = [a_ref[k + s : k + s + SUB, ks] for s in groups]
         z = [(lane[s : s + SUB] == row[s : s + SUB]).astype(jnp.float32) for s in groups]
-        upper, inverse = factor_block(x, z)
+        upper, inverse = factor_block(x, z, *spare)
         l_ref[ks, ks] = jnp.where(row >= lane, upper.T, 0.0)
         w_ref[ks, ks] = inverse
         if k + LANES < m:
@@ -172,6 +191,9 @@
         scratch_shapes=[
             pltpu.VMEM((m, m), jnp.float32),
             pltpu.VMEM((n * pieces[0].shape[0], LANES), jnp.float32),
+            pltpu.VMEM((LANES, LANES), jnp.float32),
+            pltpu.VMEM((LANES, LANES), jnp.float32),
+            pltpu.VMEM((LANES * SUB, LANES), jnp.float32),
         ],
         compiler_params=pltpu.CompilerParams(vmem_limit_bytes=24 * MIB),
         cost_estimate=SHORT,

time: 119 us -> 116 us (0.975)
  Pallas kernels: 29 us -> 26.1 us
    pallas_call x1, Pallas kernels: 20.5 us -> 17.5 us  [factor_and_inverse(): pl.pallas_call(functools.partial(factor_kernel, m, n), out_shape=[jax.Sha...]
  transfers between devices with their start and end apart: 36 -> 36, of which waited for: 20 -> 23; matrix products, arithmetic and copies ran while one was open for 2% -> 2% of each run, Pallas kernels for 22% -> 19%
where the time goes in v4:
time: 116 us
  waiting for transfers between devices  49.2 us (42%)
  starting transfers between devices  35.9 us (31%)
  Pallas kernels  26.1 us (22%)
  local copies, waits for them, and re-layouts  3.77 us (3%)
    ppermute x36, waiting for transfers between devices, permute(): lax.ppermute(x, axis, [(i, i ^ bits) for i in range(lax.axis_size(axis))])  49.2 us
    ppermute x36, starting transfers between devices, permute(): lax.ppermute(x, axis, [(i, i ^ bits) for i in range(lax.axis_size(axis))])  35.9 us
    pallas_call x1, Pallas kernels, factor_and_inverse(): pl.pallas_call(functools.partial(factor_kernel, m, n), out_shape=[jax.Sha...  17.5 us
    dynamic_slice x2, local copies, waits for them, and re-layouts, block(): return lax.dynamic_slice(x, (0, j * width), (rows, width))  3.73 us
    pallas_call x1, Pallas kernels, gram_packed(): pl.pallas_call(functools.partial(gram_kernel, scale, n), out_shape=[half,...  2.69 us
    pallas_call x2, Pallas kernels, assemble(): pl.pallas_call(functools.partial(assemble_kernel, places, width, len(olds...  2.35 us
  transfers between devices with their start and end apart: 36, of which 23 were waited for; matrix products, arithmetic and copies ran while one was open for 2% of the time, Pallas kernels for 19%

profile of v4, /device:TPU:0, one launch (start us, length us, event | category | flops | bytes accessed | tf_op | source)
XLA Modules:
  0.0 116.0 jit_solution(1706796866918723398)
XLA Ops:
  1.7 3.4 %collective-permute-start.6 = (f32[64,1536]{1,0:T(8,128)S(1)}, f32[64,1536]{1,0:T(8,128)S(1)}, u32[]{:S(2)}, u32[]{:S(2)}) collective-permute-start(f32[64,1536]{1,0:T(8,128)S(1)} %constant_dynamic-slice_fusion.12), channel_id=1, source_target_pairs={{0,28},{4,24},{8,20},{12,16},{16,12},{20,8},{24,4},{28,0},{1,29},{... | collective-permute-start | bytes 1179656 | tf_op jit(solution)/shard_map/ppermute | solution.py:267
  5.1 2.7 %constant_dynamic-slice_fusion = (f32[64,1536]{1,0:T(8,128)S(1)}, f32[64,1536]{1,0:T(8,128)S(1)}, f32[64,1536]{1,0:T(8,128)S(1)}, f32[64,1536]{1,0:T(8,128)S(1)}...) fusion(f32[64,12288]{1,0:T(8,128)} %param.1, ...), kind=kLoop, calls=%fused_computation.5 | loop fusion | bytes 9437232 | tf_op jit(solution)/shard_map/dynamic_slice | solution.py:321
  8.6 1.6 %collective-permute-start.3 = (f32[64,1536]{1,0:T(8,128)S(1)}, f32[64,1536]{1,0:T(8,128)S(1)}, u32[]{:S(2)}, u32[]{:S(2)}) collective-permute-start(f32[64,1536]{1,0:T(8,128)S(1)} %get-tuple-element.63), channel_id=1, source_target_pairs={{0,16},{4,20},{8,24},{12,28},{16,0},{20,4},{24,8},{28,12},{1,17},{... | collective-permute-start | bytes 1179656 | tf_op jit(solution)/shard_map/ppermute | solution.py:267
  11.3 3.3 %collective-permute-done.6.refs_7_ = f32[64,1536]{1,0:T(8,128)S(1)} collective-permute-done((f32[64,1536]{1,0:T(8,128)S(1)}, f32[64,1536]{1,0:T(8,128)S(1)}, u32[]{:S(2)}, u32[]{:S(2)}) %collective-permute-start.6) | collective-permute-done | bytes 393248 | tf_op jit(solution)/shard_map/ppermute | solution.py:267
  14.6 3.4 %collective-permute-start.5 = (f32[64,1536]{1,0:T(8,128)S(1)}, f32[64,1536]{1,0:T(8,128)S(1)}, u32[]{:S(2)}, u32[]{:S(2)}) collective-permute-start(f32[64,1536]{1,0:T(8,128)S(1)} %get-tuple-element.61.refs_0_), channel_id=1, source_target_pairs={{0,24},{4,28},{8,16},{12,20},{16,8},{20,12},{24,0},{28,4},{1,25},{... | collective-permute-start | bytes 1179656 | tf_op jit(solution)/shard_map/ppermute | solution.py:267
  18.0 5.1 %collective-permute-done.4.refs_5_ = f32[64,1536]{1,0:T(8,128)S(1)} collective-permute-done((f32[64,1536]{1,0:T(8,128)S(1)}, f32[64,1536]{1,0:T(8,128)S(1)}, u32[]{:S(2)}, u32[]{:S(2)}) %collective-permute-start.4) | collective-permute-done | bytes 393248 | tf_op jit(solution)/shard_map/ppermute | solution.py:267
  23.4 9.0 %collective-permute-done.3.refs_4_ = f32[64,1536]{1,0:T(8,128)S(1)} collective-permute-done((f32[64,1536]{1,0:T(8,128)S(1)}, f32[64,1536]{1,0:T(8,128)S(1)}, u32[]{:S(2)}, u32[]{:S(2)}) %collective-permute-start.3) | collective-permute-done | bytes 393248 | tf_op jit(solution)/shard_map/ppermute | solution.py:267
  32.5 7.6 %collective-permute-done.5.refs_6_ = f32[64,1536]{1,0:T(8,128)S(1)} collective-permute-done((f32[64,1536]{1,0:T(8,128)S(1)}, f32[64,1536]{1,0:T(8,128)S(1)}, u32[]{:S(2)}, u32[]{:S(2)}) %collective-permute-start.5) | collective-permute-done | bytes 393248 | tf_op jit(solution)/shard_map/ppermute | solution.py:267
  40.1 2.7 %gram.1 = (f32[640,128]{1,0:T(8,128)S(1)}, f32[640,128]{1,0:T(8,128)S(1)}, bf16[512,1536]{1,0:T(8,128)(2,1)S(1)}, bf16[512,1536]{1,0:T(8,128)(2,1)S(1)}) custom-call(f32[64,1536]{1,0:T(8,128)S(1)} %get-tuple-element.67.refs_0_, f32[64,1536]{1,0:T(8,128)S(1)} %collective-permute-done.refs_1_, f32[64,1536]{1,0:T(8,128)S(1)} %collective-permute-done.1.refs_2_, ...), custom_call_target="tpu_custom_call" | custom-call | flops 1024 | bytes 1024 | tf_op jit(solution)/shard_map/gram/pallas_call | solution.py:88
  42.8 1.6 %collective-permute-done.7 = f32[640,128]{1,0:T(8,128)S(1)} collective-permute-done((f32[640,128]{1,0:T(8,128)S(1)}, f32[640,128]{1,0:T(8,128)S(1)}, u32[]{:S(2)}, u32[]{:S(2)}) %collective-permute-start.7) | collective-permute-done | bytes 327712 | tf_op jit(solution)/shard_map/ppermute | solution.py:267
  44.5 3.3 %collective-permute-start.10 = (f32[160,128]{1,0:T(8,128)S(1)}, f32[160,128]{1,0:T(8,128)S(1)}, u32[]{:S(2)}, u32[]{:S(2)}) collective-permute-start(f32[160,128]{1,0:T(8,128)S(1)} %get-tuple-element.68), channel_id=1, source_target_pairs={{0,24},{4,28},{8,16},{12,20},{16,8},{20,12},{24,0},{28,4},{1,25},{... | collective-permute-start | bytes 245768 | tf_op jit(solution)/shard_map/ppermute | solution.py:267
  48.4 2.2 %collective-permute-done.10 = f32[160,128]{1,0:T(8,128)S(1)} collective-permute-done((f32[160,128]{1,0:T(8,128)S(1)}, f32[160,128]{1,0:T(8,128)S(1)}, u32[]{:S(2)}, u32[]{:S(2)}) %collective-permute-start.10) | collective-permute-done | bytes 81952 | tf_op jit(solution)/shard_map/ppermute | solution.py:267
  50.6 1.9 %collective-permute-start.14 = (f32[64,1536]{1,0:T(8,128)S(1)}, f32[64,1536]{1,0:T(8,128)S(1)}, u32[]{:S(2)}, u32[]{:S(2)}) collective-permute-start(f32[64,1536]{1,0:T(8,128)S(1)} %get-tuple-element.32), channel_id=1, source_target_pairs={{0,8},{4,12},{8,0},{12,4},{16,24},{20,28},{24,16},{28,20},{1,9},{5... | collective-permute-start | bytes 1179656 | tf_op jit(solution)/shard_map/ppermute | solution.py:267
  52.5 2.0 %collective-permute-start.15 = (f32[64,1536]{1,0:T(8,128)S(1)}, f32[64,1536]{1,0:T(8,128)S(1)}, u32[]{:S(2)}, u32[]{:S(2)}) collective-permute-start(f32[64,1536]{1,0:T(8,128)S(1)} %get-tuple-element.33), channel_id=1, source_target_pairs={{0,16},{4,20},{8,24},{12,28},{16,0},{20,4},{24,8},{28,12},{1,17},{... | collective-permute-start | bytes 1179656 | tf_op jit(solution)/shard_map/ppermute | solution.py:267
  54.6 3.7 %collective-permute-start.13 = (f32[160,128]{1,0:T(8,128)S(1)}, f32[160,128]{1,0:T(8,128)S(1)}, u32[]{:S(2)}, u32[]{:S(2)}) collective-permute-start(f32[160,128]{1,0:T(8,128)S(1)} %fusion), channel_id=1, source_target_pairs={{0,3},{1,2},{2,1},{3,0},{4,7},{5,6},{6,5},{7,4},{8,11},{9,10},{10,... | collective-permute-start | bytes 245768 | tf_op jit(solution)/shard_map/ppermute | solution.py:267
  59.1 2.2 %collective-permute-done.13 = f32[160,128]{1,0:T(8,128)S(1)} collective-permute-done((f32[160,128]{1,0:T(8,128)S(1)}, f32[160,128]{1,0:T(8,128)S(1)}, u32[]{:S(2)}, u32[]{:S(2)}) %collective-permute-start.13) | collective-permute-done | bytes 81952 | tf_op jit(solution)/shard_map/ppermute | solution.py:267
  61.3 2.4 %collective-permute-done.12 = f32[160,128]{1,0:T(8,128)S(1)} collective-permute-done((f32[160,128]{1,0:T(8,128)S(1)}, f32[160,128]{1,0:T(8,128)S(1)}, u32[]{:S(2)}, u32[]{:S(2)}) %collective-permute-start.12) | collective-permute-done | bytes 81952 | tf_op jit(solution)/shard_map/ppermute | solution.py:267
  64.3 2.0 %collective-permute-start.19 = (f32[160,128]{1,0:T(8,128)S(1)}, f32[160,128]{1,0:T(8,128)S(1)}, u32[]{:S(2)}, u32[]{:S(2)}) collective-permute-start(f32[160,128]{1,0:T(8,128)S(1)} %add_add_fusion.refs_0_), channel_id=1, source_target_pairs={{0,16},{4,20},{8,24},{12,28},{16,0},{20,4},{24,8},{28,12},{1,17},{... | collective-permute-start | bytes 245768 | tf_op jit(solution)/shard_map/ppermute | solution.py:267
  67.4 2.3 %collective-permute-done.21.refs_6_ = f32[160,128]{1,0:T(8,128)S(1)} collective-permute-done((f32[160,128]{1,0:T(8,128)S(1)}, f32[160,128]{1,0:T(8,128)S(1)}, u32[]{:S(2)}, u32[]{:S(2)}) %collective-permute-start.21) | collective-permute-done | bytes 81952 | tf_op jit(solution)/shard_map/ppermute | solution.py:267
  75.9 17.5 %factor.1 = (f32[512,512]{1,0:T(8,128)}, f32[512,512]{1,0:T(8,128)S(1)}) custom-call(f32[160,128]{1,0:T(8,128)S(1)} %add_add_fusion.refs_0_, f32[160,128]{1,0:T(8,128)S(1)} %collective-permute-done.16.refs_1_, f32[160,128]{1,0:T(8,128)S(1)} %collective-permute-done.17.refs_2_, f32[160,128]{1,0:T(8,128)S(1)} %collective-permute-done.18.refs_3_, ...), custom_call_target="tpu_custom_call" | custom-call | flops 1024 | bytes 1024 | tf_op jit(solution)/shard_map/factor/pallas_call | solution.py:188
  98.5 2.1 %keep_rows.1 = (f32[64,1536]{1,0:T(8,128)S(1)}, f32[64,768]{1,0:T(8,128)S(1)}, f32[64,768]{1,0:T(8,128)S(1)}, f32[64,1536]{1,0:T(8,128)S(1)}, f32[64,768]{1,0:T(8,128)S(1)}, /*index=5*/f32[64,768]{1,0:T(8,128)S(1)}) custom-call(f32[512,512]{1,0:T(8,128)S(1)} %get-tuple-element.35.w_ref, bf16[512,1536]{1,0:T(8,128)(2,1)S(1)} %get-tuple-element.36.high, ...), custom_call_target="tpu_custom_call" | custom-call | flops 1024 | bytes 1024 | tf_op jit(solution)/shard_map/keep_rows/pallas_call | solution.py:256
  100.8 1.5 %collective-permute-start.34 = (f32[64,1536]{1,0:T(8,128)S(1)}, f32[64,1536]{1,0:T(8,128)S(1)}, u32[]{:S(2)}, u32[]{:S(2)}) collective-permute-start(f32[64,1536]{1,0:T(8,128)S(1)} %get-tuple-element.53), channel_id=1, source_target_pairs={{0,12},{4,8},{8,4},{12,0},{16,28},{20,24},{24,20},{28,16},{1,13},{... | collective-permute-start | bytes 1179656 | tf_op jit(solution)/shard_map/ppermute | solution.py:267
  102.5 4.8 %collective-permute-done.33.refs_7_ = f32[64,1536]{1,0:T(8,128)S(1)} collective-permute-done((f32[64,1536]{1,0:T(8,128)S(1)}, f32[64,1536]{1,0:T(8,128)S(1)}, u32[]{:S(2)}, u32[]{:S(2)}) %collective-permute-start.33) | collective-permute-done | bytes 393248 | tf_op jit(solution)/shard_map/ppermute | solution.py:267
  111.4 3.0 %collective-permute-done.34.refs_1_ = f32[64,1536]{1,0:T(8,128)S(1)} collective-permute-done((f32[64,1536]{1,0:T(8,128)S(1)}, f32[64,1536]{1,0:T(8,128)S(1)}, u32[]{:S(2)}, u32[]{:S(2)}) %collective-permute-start.34) | collective-permute-done | bytes 393248 | tf_op jit(solution)/shard_map/ppermute | solution.py:267
  (62 shorter events, 23.7 us)
Async XLA Ops:
  1.7 12.9 %collective-permute-start.6 = (f32[64,1536]{1,0:T(8,128)S(1)}, f32[64,1536]{1,0:T(8,128)S(1)}, u32[]{:S(2)}, u32[]{:S(2)}) collective-permute-start(f32[64,1536]{1,0:T(8,128)S(1)} %constant_dynamic-slice_fusion.12), channel_id=1, source_target_pairs={{0,28},{4,24},{8,20},{12,16},{16,12},{20,8},{24,4},{28,0},{1,29},{... | collective-permute-start | bytes 1179656 | tf_op jit(solution)/shard_map/ppermute | solution.py:267
  7.8 15.3 %collective-permute-start.4 = (f32[64,1536]{1,0:T(8,128)S(1)}, f32[64,1536]{1,0:T(8,128)S(1)}, u32[]{:S(2)}, u32[]{:S(2)}) collective-permute-start(f32[64,1536]{1,0:T(8,128)S(1)} %get-tuple-element.62), channel_id=1, source_target_pairs={{0,20},{4,16},{8,28},{12,24},{16,4},{20,0},{24,12},{28,8},{1,21},{... | collective-permute-start | bytes 1179656 | tf_op jit(solution)/shard_map/ppermute | solution.py:267
  8.6 23.8 %collective-permute-start.3 = (f32[64,1536]{1,0:T(8,128)S(1)}, f32[64,1536]{1,0:T(8,128)S(1)}, u32[]{:S(2)}, u32[]{:S(2)}) collective-permute-start(f32[64,1536]{1,0:T(8,128)S(1)} %get-tuple-element.63), channel_id=1, source_target_pairs={{0,16},{4,20},{8,24},{12,28},{16,0},{20,4},{24,8},{28,12},{1,17},{... | collective-permute-start | bytes 1179656 | tf_op jit(solution)/shard_map/ppermute | solution.py:267
  10.2 22.2 %collective-permute-start.2 = (f32[64,1536]{1,0:T(8,128)S(1)}, f32[64,1536]{1,0:T(8,128)S(1)}, u32[]{:S(2)}, u32[]{:S(2)}) collective-permute-start(f32[64,1536]{1,0:T(8,128)S(1)} %get-tuple-element.64), channel_id=1, source_target_pairs={{0,12},{4,8},{8,4},{12,0},{16,28},{20,24},{24,20},{28,16},{1,13},{... | collective-permute-start | bytes 1179656 | tf_op jit(solution)/shard_map/ppermute | solution.py:267
  10.2 22.3 %collective-permute-start.1 = (f32[64,1536]{1,0:T(8,128)S(1)}, f32[64,1536]{1,0:T(8,128)S(1)}, u32[]{:S(2)}, u32[]{:S(2)}) collective-permute-start(f32[64,1536]{1,0:T(8,128)S(1)} %get-tuple-element.65), channel_id=1, source_target_pairs={{0,8},{4,12},{8,0},{12,4},{16,24},{20,28},{24,16},{28,20},{1,9},{5... | collective-permute-start | bytes 1179656 | tf_op jit(solution)/shard_map/ppermute | solution.py:267
  14.6 25.4 %collective-permute-start.5 = (f32[64,1536]{1,0:T(8,128)S(1)}, f32[64,1536]{1,0:T(8,128)S(1)}, u32[]{:S(2)}, u32[]{:S(2)}) collective-permute-start(f32[64,1536]{1,0:T(8,128)S(1)} %get-tuple-element.61.refs_0_), channel_id=1, source_target_pairs={{0,24},{4,28},{8,16},{12,20},{16,8},{20,12},{24,0},{28,4},{1,25},{... | collective-permute-start | bytes 1179656 | tf_op jit(solution)/shard_map/ppermute | solution.py:267
  23.1 17.0 %collective-permute-start = (f32[64,1536]{1,0:T(8,128)S(1)}, f32[64,1536]{1,0:T(8,128)S(1)}, u32[]{:S(2)}, u32[]{:S(2)}) collective-permute-start(f32[64,1536]{1,0:T(8,128)S(1)} %get-tuple-element.66), channel_id=1, source_target_pairs={{0,4},{4,0},{8,12},{12,8},{16,20},{20,16},{24,28},{28,24},{1,5},{5... | collective-permute-start | bytes 1179656 | tf_op jit(solution)/shard_map/ppermute | solution.py:267
  44.5 6.1 %collective-permute-start.10 = (f32[160,128]{1,0:T(8,128)S(1)}, f32[160,128]{1,0:T(8,128)S(1)}, u32[]{:S(2)}, u32[]{:S(2)}) collective-permute-start(f32[160,128]{1,0:T(8,128)S(1)} %get-tuple-element.68), channel_id=1, source_target_pairs={{0,24},{4,28},{8,16},{12,20},{16,8},{20,12},{24,0},{28,4},{1,25},{... | collective-permute-start | bytes 245768 | tf_op jit(solution)/shard_map/ppermute | solution.py:267
  47.8 6.8 %collective-permute-start.9 = (f32[160,128]{1,0:T(8,128)S(1)}, f32[160,128]{1,0:T(8,128)S(1)}, u32[]{:S(2)}, u32[]{:S(2)}) collective-permute-start(f32[160,128]{1,0:T(8,128)S(1)} %get-tuple-element.69), channel_id=1, source_target_pairs={{0,16},{4,20},{8,24},{12,28},{16,0},{20,4},{24,8},{28,12},{1,17},{... | collective-permute-start | bytes 245768 | tf_op jit(solution)/shard_map/ppermute | solution.py:267
  48.3 6.3 %collective-permute-start.8 = (f32[160,128]{1,0:T(8,128)S(1)}, f32[160,128]{1,0:T(8,128)S(1)}, u32[]{:S(2)}, u32[]{:S(2)}) collective-permute-start(f32[160,128]{1,0:T(8,128)S(1)} %get-tuple-element.70), channel_id=1, source_target_pairs={{0,8},{4,12},{8,0},{12,4},{16,24},{20,28},{24,16},{28,20},{1,9},{5... | collective-permute-start | bytes 245768 | tf_op jit(solution)/shard_map/ppermute | solution.py:267
  50.6 13.1 %collective-permute-start.14 = (f32[64,1536]{1,0:T(8,128)S(1)}, f32[64,1536]{1,0:T(8,128)S(1)}, u32[]{:S(2)}, u32[]{:S(2)}) collective-permute-start(f32[64,1536]{1,0:T(8,128)S(1)} %get-tuple-element.32), channel_id=1, source_target_pairs={{0,8},{4,12},{8,0},{12,4},{16,24},{20,28},{24,16},{28,20},{1,9},{5... | collective-permute-start | bytes 1179656 | tf_op jit(solution)/shard_map/ppermute | solution.py:267
  52.5 11.2 %collective-permute-start.15 = (f32[64,1536]{1,0:T(8,128)S(1)}, f32[64,1536]{1,0:T(8,128)S(1)}, u32[]{:S(2)}, u32[]{:S(2)}) collective-permute-start(f32[64,1536]{1,0:T(8,128)S(1)} %get-tuple-element.33), channel_id=1, source_target_pairs={{0,16},{4,20},{8,24},{12,28},{16,0},{20,4},{24,8},{28,12},{1,17},{... | collective-permute-start | bytes 1179656 | tf_op jit(solution)/shard_map/ppermute | solution.py:267
  54.6 6.7 %collective-permute-start.13 = (f32[160,128]{1,0:T(8,128)S(1)}, f32[160,128]{1,0:T(8,128)S(1)}, u32[]{:S(2)}, u32[]{:S(2)}) collective-permute-start(f32[160,128]{1,0:T(8,128)S(1)} %fusion), channel_id=1, source_target_pairs={{0,3},{1,2},{2,1},{3,0},{4,7},{5,6},{6,5},{7,4},{8,11},{9,10},{10,... | collective-permute-start | bytes 245768 | tf_op jit(solution)/shard_map/ppermute | solution.py:267
  63.7 5.9 %collective-permute-start.21 = (f32[160,128]{1,0:T(8,128)S(1)}, f32[160,128]{1,0:T(8,128)S(1)}, u32[]{:S(2)}, u32[]{:S(2)}) collective-permute-start(f32[160,128]{1,0:T(8,128)S(1)} %add_add_fusion.refs_0_), channel_id=1, source_target_pairs={{0,24},{4,28},{8,16},{12,20},{16,8},{20,12},{24,0},{28,4},{1,25},{... | collective-permute-start | bytes 245768 | tf_op jit(solution)/shard_map/ppermute | solution.py:267
  64.3 5.4 %collective-permute-start.19 = (f32[160,128]{1,0:T(8,128)S(1)}, f32[160,128]{1,0:T(8,128)S(1)}, u32[]{:S(2)}, u32[]{:S(2)}) collective-permute-start(f32[160,128]{1,0:T(8,128)S(1)} %add_add_fusion.refs_0_), channel_id=1, source_target_pairs={{0,16},{4,20},{8,24},{12,28},{16,0},{20,4},{24,8},{28,12},{1,17},{... | collective-permute-start | bytes 245768 | tf_op jit(solution)/shard_map/ppermute | solution.py:267
  70.7 24.1 %collective-permute-start.26 = (f32[2,64,1536]{2,1,0:T(8,128)S(1)}, f32[2,64,1536]{2,1,0:T(8,128)S(1)}, u32[]{:S(2)}, u32[]{:S(2)}) collective-permute-start(f32[2,64,1536]{2,1,0:T(8,128)S(1)} %pad_maximum_fusion), channel_id=1, source_target_pairs={{0,24},{4,28},{8,16},{12,20},{16,8},{20,12},{24,0},{28,4},{1,25},{... | collective-permute-start | bytes 2359304 | tf_op jit(solution)/shard_map/ppermute | solution.py:267
  74.0 22.2 %collective-permute-start.23 = (f32[64,1536]{1,0:T(8,128)S(1)}, f32[64,1536]{1,0:T(8,128)S(1)}, u32[]{:S(2)}, u32[]{:S(2)}) collective-permute-start(f32[64,1536]{1,0:T(8,128)S(1)} %get-tuple-element.38), channel_id=1, source_target_pairs={{0,4},{4,0},{8,12},{12,8},{16,20},{20,16},{24,28},{28,24},{1,5},{5... | collective-permute-start | bytes 1179656 | tf_op jit(solution)/shard_map/ppermute | solution.py:267
  74.2 23.2 %collective-permute-start.24 = (f32[64,1536]{1,0:T(8,128)S(1)}, f32[64,1536]{1,0:T(8,128)S(1)}, u32[]{:S(2)}, u32[]{:S(2)}) collective-permute-start(f32[64,1536]{1,0:T(8,128)S(1)} %get-tuple-element.40), channel_id=1, source_target_pairs={{0,12},{4,8},{8,4},{12,0},{16,28},{20,24},{24,20},{28,16},{1,13},{... | collective-permute-start | bytes 1179656 | tf_op jit(solution)/shard_map/ppermute | solution.py:267
  75.0 23.4 %collective-permute-start.25 = (f32[64,1536]{1,0:T(8,128)S(1)}, f32[64,1536]{1,0:T(8,128)S(1)}, u32[]{:S(2)}, u32[]{:S(2)}) collective-permute-start(f32[64,1536]{1,0:T(8,128)S(1)} %get-tuple-element.42), channel_id=1, source_target_pairs={{0,20},{4,16},{8,28},{12,24},{16,4},{20,0},{24,12},{28,8},{1,21},{... | collective-permute-start | bytes 1179656 | tf_op jit(solution)/shard_map/ppermute | solution.py:267
  95.3 12.1 %collective-permute-start.33 = (f32[64,1536]{1,0:T(8,128)S(1)}, f32[64,1536]{1,0:T(8,128)S(1)}, u32[]{:S(2)}, u32[]{:S(2)}) collective-permute-start(f32[64,1536]{1,0:T(8,128)S(1)} %get-tuple-element.52), channel_id=1, source_target_pairs={{0,16},{4,20},{8,24},{12,28},{16,0},{20,4},{24,8},{28,12},{1,17},{... | collective-permute-start | bytes 1179656 | tf_op jit(solution)/shard_map/ppermute | solution.py:267
  96.2 12.0 %collective-permute-start.32 = (f32[64,1536]{1,0:T(8,128)S(1)}, f32[64,1536]{1,0:T(8,128)S(1)}, u32[]{:S(2)}, u32[]{:S(2)}) collective-permute-start(f32[64,1536]{1,0:T(8,128)S(1)} %get-tuple-element.44), channel_id=1, source_target_pairs={{0,8},{4,12},{8,0},{12,4},{16,24},{20,28},{24,16},{28,20},{1,9},{5... | collective-permute-start | bytes 1179656 | tf_op jit(solution)/shard_map/ppermute | solution.py:267
  100.6 7.6 %collective-permute-start.28 = (f32[64,768]{1,0:T(8,128)S(1)}, f32[64,768]{1,0:T(8,128)S(1)}, u32[]{:S(2)}, u32[]{:S(2)}) collective-permute-start(f32[64,768]{1,0:T(8,128)S(1)} %get-tuple-element.48), channel_id=1, source_target_pairs={{0,4},{4,0},{8,12},{12,8},{16,20},{20,16},{24,28},{28,24},{1,5},{5... | collective-permute-start | bytes 589832 | tf_op jit(solution)/shard_map/ppermute | solution.py:267
  100.8 13.6 %collective-permute-start.34 = (f32[64,1536]{1,0:T(8,128)S(1)}, f32[64,1536]{1,0:T(8,128)S(1)}, u32[]{:S(2)}, u32[]{:S(2)}) collective-permute-start(f32[64,1536]{1,0:T(8,128)S(1)} %get-tuple-element.53), channel_id=1, source_target_pairs={{0,12},{4,8},{8,4},{12,0},{16,28},{20,24},{24,20},{28,16},{1,13},{... | collective-permute-start | bytes 1179656 | tf_op jit(solution)/shard_map/ppermute | solution.py:267
  102.3 12.6 %collective-permute-start.35 = (f32[64,1536]{1,0:T(8,128)S(1)}, f32[64,1536]{1,0:T(8,128)S(1)}, u32[]{:S(2)}, u32[]{:S(2)}) collective-permute-start(f32[64,1536]{1,0:T(8,128)S(1)} %get-tuple-element.54), channel_id=1, source_target_pairs={{0,20},{4,16},{8,28},{12,24},{16,4},{20,0},{24,12},{28,8},{1,21},{... | collective-permute-start | bytes 1179656 | tf_op jit(solution)/shard_map/ppermute | solution.py:267
  (12 other events, 32.4 us)

commit v5 on v4

--- a/solution.py
+++ b/solution.py
@@ -54,11 +54,35 @@
         high[at, :], low[at, :] = split(part[...] if len(part.shape) == 2 else part[0])
 
 
-def gram_kernel(scale, n, *refs):
-    parts, (mine, theirs, high, low, packed) = refs[:n], refs[n:]
+def split_kernel(*refs):
+    parts, (high, low) = refs[:-2], refs[-2:]
+    rows = parts[0].shape[0]
+    for i, part in enumerate(parts):
+        at = slice(i * rows, (i + 1) * rows)
+        high[at, :], low[at, :] = split(part[...])
+
+
+def split_early(parts):
+    rows, w = parts[0].shape
+    return pl.pallas_call(
+        split_kernel,
+        out_shape=[jax.ShapeDtypeStruct((rows * len(parts), w), jnp.bfloat16)] * 2,
+        compiler_params=pltpu.CompilerParams(vmem_limit_bytes=24 * MIB),
+        cost_estimate=SHORT,
+        name="split_early",
+    )(*parts)
+
+
+def gram_kernel(scale, n, ks, early_high, early_low, last, mine, theirs, high, low, packed):
+    rows = last.shape[0]
+    me = fibre_index()
+    for i, k in enumerate(ks):
+        at, piece = pl.ds(pl.multiple_of((me ^ k) * rows, rows), rows), slice(i * rows, (i + 1) * rows)
+        high[at, :], low[at, :] = early_high[piece, :], early_low[piece, :]
+    at = pl.ds(pl.multiple_of((me ^ (n - 2)) * rows, rows), rows)
+    high[at, :], low[at, :] = split(last[...])
     m = high.shape[0]
     half = m // 2
-    place_rows(parts, high, low)
     blocks = packed_blocks(m)
     for start in (0, half):
         rows, upto = slice(start, start + half), slice(0, start + half)
@@ -82,17 +106,20 @@
     rows, w = parts[0].shape
     n = len(parts)
     m = rows * n
+    ks = [k for k in range(n) if k != n - 2]
+    early = split_early([parts[k] for k in ks])
+    last = after(parts[n - 2], *early)
     size = len(packed_blocks(m)) * PART
     half = jax.ShapeDtypeStruct((size // 2, LANES), jnp.float32)
     wide = jax.ShapeDtypeStruct((m, w), jnp.bfloat16)
     return pl.pallas_call(
-        functools.partial(gram_kernel, scale, n),
+        functools.partial(gram_kernel, scale, n, ks),
         out_shape=[half, half, wide, wide],
         scratch_shapes=[pltpu.VMEM((size, LANES), jnp.float32)],
         compiler_params=pltpu.CompilerParams(vmem_limit_bytes=24 * MIB),
         cost_estimate=SHORT,
         name="gram",
-    )(*parts)
+    )(*early, last)
 
 
 def along_lanes(v, j):
@@ -165,22 +192,25 @@
     row = lax.broadcasted_iota(jnp.int32, (LANES, LANES), 0)
     lane = lax.broadcasted_iota(jnp.int32, (LANES, LANES), 1)
     groups = range(0, LANES, SUB)
+    nt, nn = ((1,), (1,)), ((1,), (0,))
     for k in range(0, m, LANES):
-        ks = slice(k, k + LANES)
-        x = [a_ref[k + s : k + s + SUB, ks] for s in groups]
+        ks, before, rest = slice(k, k + LANES), slice(0, k), slice(k + LANES, m)
+        block = a_ref[ks, ks]
+        if k:
+            block = block - dot_full(l_ref[ks, before], l_ref[ks, before], nt)
+        below = a_ref[rest, ks] if k + LANES < m else None
+        if k and below is not None:
+            below = below - dot_full(l_ref[rest, before], l_ref[ks, before], nt)
+        solved = dot_full(l_ref[ks, before], w_ref[before, before], nn) if k else None
+        x = [block[s : s + SUB] for s in groups]
         z = [(lane[s : s + SUB] == row[s : s + SUB]).astype(jnp.float32) for s in groups]
         upper, inverse = factor_block(x, z, *spare)
         l_ref[ks, ks] = jnp.where(row >= lane, upper.T, 0.0)
         w_ref[ks, ks] = inverse
-        if k + LANES < m:
-            rest = slice(k + LANES, m)
-            panel = dot_full(a_ref[rest, ks], inverse, ((1,), (1,)))
-            l_ref[rest, ks] = panel
-            a_ref[rest, rest] = a_ref[rest, rest] - dot_full(panel, panel, ((1,), (1,)))
-    for i in range(LANES, m, LANES):
-        rows = slice(i, i + LANES)
-        acc = dot_full(l_ref[rows, 0:i], w_ref[0:i, 0:i], ((1,), (0,)))
-        w_ref[rows, 0:i] = -dot_full(w_ref[rows, rows], acc, ((1,), (0,)))
+        if below is not None:
+            l_ref[rest, ks] = dot_full(below, inverse, nt)
+        if k:
+            w_ref[ks, before] = -dot_full(inverse, solved, nn)
 
 
 def factor_and_inverse(pieces, m):
@@ -328,6 +358,8 @@
     parts = [permute(blocks[k], "fibre", k) if k else blocks[0] for k in range(n)]
     twin = [block(rest, me ^ k ^ opposite) for k in range(opposite)] + [None, None]
     mine, theirs, high, low = gram_packed(parts, 1.0 / (width * n * groups))
+    twin[1] = permute(after(twin[1], parts[far]), "fibre", 1)
+    theirs, twin[1] = lax.optimization_barrier((theirs, twin[1]))
     mine = (mine + permute(theirs, "fibre", 1)).reshape(chips, -1, LANES)
     terms = [mine[k] if k == 0 else permute(mine[k], "fibre", 2 * k) for k in range(chips)]
     for k in even:
@@ -343,7 +375,7 @@
         pieces[2 * k + 1] = permute(pieces[2 * k], "fibre", 1)
     own = after(jnp.stack([blocks[0], blocks[1]]), *pieces[2::2])
     twin[opposite] = permute(own, "fibre", opposite)
-    for k in (*odd, 1):
+    for k in odd:
         twin[k] = permute(after(twin[k], *pieces[3::2]), "fibre", k)
     factor, inverse = factor_and_inverse(pieces, m)
     ks = tuple(range(2, n - 2))

time: 116 us -> 116 us (level)
    pallas_call x1 -> x2, Pallas kernels: 2.69 us -> 2.75 us  [the longest x1 2.28 us: gram_packed(): pl.pallas_call(functools.partial(gram_kernel, scale, n, ks), out_shape=[h...]
  transfers between devices with their start and end apart: 36 -> 36, of which waited for: 23 -> 24; matrix products, arithmetic and copies ran while one was open for 2% -> 2% of each run, Pallas kernels for 19% -> 22%
where the time goes in v5:
time: 116 us
  waiting for transfers between devices  48.9 us (42%)
  starting transfers between devices  36.3 us (31%)
  Pallas kernels  25.8 us (22%)
  local copies, waits for them, and re-layouts  3.82 us (3%)
    ppermute x36, waiting for transfers between devices, permute(): lax.ppermute(x, axis, [(i, i ^ bits) for i in range(lax.axis_size(axis))])  48.9 us
    ppermute x36, starting transfers between devices, permute(): lax.ppermute(x, axis, [(i, i ^ bits) for i in range(lax.axis_size(axis))])  36.3 us
    pallas_call x1, Pallas kernels, factor_and_inverse(): pl.pallas_call(functools.partial(factor_kernel, m, n), out_shape=[jax.Sha...  17.2 us
    dynamic_slice x2, local copies, waits for them, and re-layouts, block(): return lax.dynamic_slice(x, (0, j * width), (rows, width))  3.77 us
    pallas_call x2, Pallas kernels, assemble(): pl.pallas_call(functools.partial(assemble_kernel, places, width, len(olds...  2.35 us
  transfers between devices with their start and end apart: 36, of which 24 were waited for; matrix products, arithmetic and copies ran while one was open for 2% of the time, Pallas kernels for 22%

profile of v5, /device:TPU:0, one launch (start us, length us, event | category | flops | bytes accessed | tf_op | source)
XLA Modules:
  0.0 115.9 jit_solution(16626446514451250119)
XLA Ops:
  1.7 3.4 %collective-permute-start.5 = (f32[64,1536]{1,0:T(8,128)S(1)}, f32[64,1536]{1,0:T(8,128)S(1)}, u32[]{:S(2)}, u32[]{:S(2)}) collective-permute-start(f32[64,1536]{1,0:T(8,128)S(1)} %constant_dynamic-slice_fusion.12), channel_id=1, source_target_pairs={{0,28},{4,24},{8,20},{12,16},{16,12},{20,8},{24,4},{28,0},{1,29},{... | collective-permute-start | bytes 1179656 | tf_op jit(solution)/shard_map/ppermute | solution.py:297
  5.1 2.7 %constant_dynamic-slice_fusion = (f32[64,1536]{1,0:T(8,128)S(1)}, f32[64,1536]{1,0:T(8,128)S(1)}, f32[64,1536]{1,0:T(8,128)S(1)}, f32[64,1536]{1,0:T(8,128)S(1)}...) fusion(f32[64,12288]{1,0:T(8,128)} %param.1, ...), kind=kLoop, calls=%fused_computation.5 | loop fusion | bytes 9437232 | tf_op jit(solution)/shard_map/dynamic_slice | solution.py:351
  8.6 1.6 %collective-permute-start.3 = (f32[64,1536]{1,0:T(8,128)S(1)}, f32[64,1536]{1,0:T(8,128)S(1)}, u32[]{:S(2)}, u32[]{:S(2)}) collective-permute-start(f32[64,1536]{1,0:T(8,128)S(1)} %get-tuple-element.73), channel_id=1, source_target_pairs={{0,16},{4,20},{8,24},{12,28},{16,0},{20,4},{24,8},{28,12},{1,17},{... | collective-permute-start | bytes 1179656 | tf_op jit(solution)/shard_map/ppermute | solution.py:297
  11.4 3.2 %collective-permute-done.5.refs_6_ = f32[64,1536]{1,0:T(8,128)S(1)} collective-permute-done((f32[64,1536]{1,0:T(8,128)S(1)}, f32[64,1536]{1,0:T(8,128)S(1)}, u32[]{:S(2)}, u32[]{:S(2)}) %collective-permute-start.5) | collective-permute-done | bytes 393248 | tf_op jit(solution)/shard_map/ppermute | solution.py:297
  15.4 7.7 %collective-permute-done.4.refs_5_ = f32[64,1536]{1,0:T(8,128)S(1)} collective-permute-done((f32[64,1536]{1,0:T(8,128)S(1)}, f32[64,1536]{1,0:T(8,128)S(1)}, u32[]{:S(2)}, u32[]{:S(2)}) %collective-permute-start.4) | collective-permute-done | bytes 393248 | tf_op jit(solution)/shard_map/ppermute | solution.py:297
  23.1 3.3 %collective-permute-start.6 = (f32[64,1536]{1,0:T(8,128)S(1)}, f32[64,1536]{1,0:T(8,128)S(1)}, u32[]{:S(2)}, u32[]{:S(2)}) collective-permute-start(f32[64,1536]{1,0:T(8,128)S(1)} %get-tuple-element.71.refs_0_), channel_id=1, source_target_pairs={{0,24},{4,28},{8,16},{12,20},{16,8},{20,12},{24,0},{28,4},{1,25},{... | collective-permute-start | bytes 1179656 | tf_op jit(solution)/shard_map/ppermute | solution.py:297
  26.4 6.0 %collective-permute-done.3.refs_4_ = f32[64,1536]{1,0:T(8,128)S(1)} collective-permute-done((f32[64,1536]{1,0:T(8,128)S(1)}, f32[64,1536]{1,0:T(8,128)S(1)}, u32[]{:S(2)}, u32[]{:S(2)}) %collective-permute-start.3) | collective-permute-done | bytes 393248 | tf_op jit(solution)/shard_map/ppermute | solution.py:297
  32.9 7.1 %collective-permute-done.6.last = f32[64,1536]{1,0:T(8,128)S(1)} collective-permute-done((f32[64,1536]{1,0:T(8,128)S(1)}, f32[64,1536]{1,0:T(8,128)S(1)}, u32[]{:S(2)}, u32[]{:S(2)}) %collective-permute-start.6) | collective-permute-done | bytes 393248 | tf_op jit(solution)/shard_map/ppermute | solution.py:297
  40.1 2.3 %gram.1 = (f32[640,128]{1,0:T(8,128)S(1)}, f32[640,128]{1,0:T(8,128)S(1)}, bf16[512,1536]{1,0:T(8,128)(2,1)S(1)}, bf16[512,1536]{1,0:T(8,128)(2,1)S(1)}) custom-call(bf16[448,1536]{1,0:T(8,128)(2,1)S(1)} %get-tuple-element.35.early_high, bf16[448,1536]{1,0:T(8,128)(2,1)S(1)} %get-tuple-element.36.early_low, f32[64,1536]{1,0:T(8,128)S(1)} %collective-permute-done.6.last), custom_call_target="tpu_custom_call" | custom-call | flops 1024 | bytes 1024 | tf_op jit(solution)/shard_map/gram/pallas_call | solution.py:115
  42.4 1.6 %collective-permute-done.8 = f32[640,128]{1,0:T(8,128)S(1)} collective-permute-done((f32[640,128]{1,0:T(8,128)S(1)}, f32[640,128]{1,0:T(8,128)S(1)}, u32[]{:S(2)}, u32[]{:S(2)}) %collective-permute-start.8) | collective-permute-done | bytes 327712 | tf_op jit(solution)/shard_map/ppermute | solution.py:297
  44.1 3.3 %collective-permute-start.11 = (f32[160,128]{1,0:T(8,128)S(1)}, f32[160,128]{1,0:T(8,128)S(1)}, u32[]{:S(2)}, u32[]{:S(2)}) collective-permute-start(f32[160,128]{1,0:T(8,128)S(1)} %get-tuple-element.78), channel_id=1, source_target_pairs={{0,24},{4,28},{8,16},{12,20},{16,8},{20,12},{24,0},{28,4},{1,25},{... | collective-permute-start | bytes 245768 | tf_op jit(solution)/shard_map/ppermute | solution.py:297
  48.0 2.2 %collective-permute-done.11 = f32[160,128]{1,0:T(8,128)S(1)} collective-permute-done((f32[160,128]{1,0:T(8,128)S(1)}, f32[160,128]{1,0:T(8,128)S(1)}, u32[]{:S(2)}, u32[]{:S(2)}) %collective-permute-start.11) | collective-permute-done | bytes 81952 | tf_op jit(solution)/shard_map/ppermute | solution.py:297
  50.2 1.9 %collective-permute-start.15 = (f32[64,1536]{1,0:T(8,128)S(1)}, f32[64,1536]{1,0:T(8,128)S(1)}, u32[]{:S(2)}, u32[]{:S(2)}) collective-permute-start(f32[64,1536]{1,0:T(8,128)S(1)} %get-tuple-element.42), channel_id=1, source_target_pairs={{0,8},{4,12},{8,0},{12,4},{16,24},{20,28},{24,16},{28,20},{1,9},{5... | collective-permute-start | bytes 1179656 | tf_op jit(solution)/shard_map/ppermute | solution.py:297
  52.1 2.0 %collective-permute-start.16 = (f32[64,1536]{1,0:T(8,128)S(1)}, f32[64,1536]{1,0:T(8,128)S(1)}, u32[]{:S(2)}, u32[]{:S(2)}) collective-permute-start(f32[64,1536]{1,0:T(8,128)S(1)} %get-tuple-element.43), channel_id=1, source_target_pairs={{0,16},{4,20},{8,24},{12,28},{16,0},{20,4},{24,8},{28,12},{1,17},{... | collective-permute-start | bytes 1179656 | tf_op jit(solution)/shard_map/ppermute | solution.py:297
  54.2 3.7 %collective-permute-start.14 = (f32[160,128]{1,0:T(8,128)S(1)}, f32[160,128]{1,0:T(8,128)S(1)}, u32[]{:S(2)}, u32[]{:S(2)}) collective-permute-start(f32[160,128]{1,0:T(8,128)S(1)} %fusion), channel_id=1, source_target_pairs={{0,3},{1,2},{2,1},{3,0},{4,7},{5,6},{6,5},{7,4},{8,11},{9,10},{10,... | collective-permute-start | bytes 245768 | tf_op jit(solution)/shard_map/ppermute | solution.py:297
  58.7 2.2 %collective-permute-done.14 = f32[160,128]{1,0:T(8,128)S(1)} collective-permute-done((f32[160,128]{1,0:T(8,128)S(1)}, f32[160,128]{1,0:T(8,128)S(1)}, u32[]{:S(2)}, u32[]{:S(2)}) %collective-permute-start.14) | collective-permute-done | bytes 81952 | tf_op jit(solution)/shard_map/ppermute | solution.py:297
  60.9 2.4 %collective-permute-done.13 = f32[160,128]{1,0:T(8,128)S(1)} collective-permute-done((f32[160,128]{1,0:T(8,128)S(1)}, f32[160,128]{1,0:T(8,128)S(1)}, u32[]{:S(2)}, u32[]{:S(2)}) %collective-permute-start.13) | collective-permute-done | bytes 81952 | tf_op jit(solution)/shard_map/ppermute | solution.py:297
  63.9 2.0 %collective-permute-start.20 = (f32[160,128]{1,0:T(8,128)S(1)}, f32[160,128]{1,0:T(8,128)S(1)}, u32[]{:S(2)}, u32[]{:S(2)}) collective-permute-start(f32[160,128]{1,0:T(8,128)S(1)} %add_add_fusion.refs_0_), channel_id=1, source_target_pairs={{0,16},{4,20},{8,24},{12,28},{16,0},{20,4},{24,8},{28,12},{1,17},{... | collective-permute-start | bytes 245768 | tf_op jit(solution)/shard_map/ppermute | solution.py:297
  67.0 2.3 %collective-permute-done.22.refs_6_ = f32[160,128]{1,0:T(8,128)S(1)} collective-permute-done((f32[160,128]{1,0:T(8,128)S(1)}, f32[160,128]{1,0:T(8,128)S(1)}, u32[]{:S(2)}, u32[]{:S(2)}) %collective-permute-start.22) | collective-permute-done | bytes 81952 | tf_op jit(solution)/shard_map/ppermute | solution.py:297
  70.3 1.5 %collective-permute-start.26 = (f32[2,64,1536]{2,1,0:T(8,128)S(1)}, f32[2,64,1536]{2,1,0:T(8,128)S(1)}, u32[]{:S(2)}, u32[]{:S(2)}) collective-permute-start(f32[2,64,1536]{2,1,0:T(8,128)S(1)} %pad_maximum_fusion), channel_id=1, source_target_pairs={{0,24},{4,28},{8,16},{12,20},{16,8},{20,12},{24,0},{28,4},{1,25},{... | collective-permute-start | bytes 2359304 | tf_op jit(solution)/shard_map/ppermute | solution.py:297
  75.3 17.2 %factor.1 = (f32[512,512]{1,0:T(8,128)}, f32[512,512]{1,0:T(8,128)S(1)}) custom-call(f32[160,128]{1,0:T(8,128)S(1)} %add_add_fusion.refs_0_, f32[160,128]{1,0:T(8,128)S(1)} %collective-permute-done.17.refs_1_, f32[160,128]{1,0:T(8,128)S(1)} %collective-permute-done.18.refs_2_, f32[160,128]{1,0:T(8,128)S(1)} %collective-permute-done.19.refs_3_, ...), custom_call_target="tpu_custom_call" | custom-call | flops 1024 | bytes 1024 | tf_op jit(solution)/shard_map/factor/pallas_call | solution.py:218
  98.0 2.1 %keep_rows.1 = (f32[64,1536]{1,0:T(8,128)S(1)}, f32[64,768]{1,0:T(8,128)S(1)}, f32[64,768]{1,0:T(8,128)S(1)}, f32[64,1536]{1,0:T(8,128)S(1)}, f32[64,768]{1,0:T(8,128)S(1)}, /*index=5*/f32[64,768]{1,0:T(8,128)S(1)}) custom-call(f32[512,512]{1,0:T(8,128)S(1)} %get-tuple-element.45.w_ref, bf16[512,1536]{1,0:T(8,128)(2,1)S(1)} %get-tuple-element.46.high, ...), custom_call_target="tpu_custom_call" | custom-call | flops 1024 | bytes 1024 | tf_op jit(solution)/shard_map/keep_rows/pallas_call | solution.py:286
  102.5 4.1 %collective-permute-done.33.refs_7_ = f32[64,1536]{1,0:T(8,128)S(1)} collective-permute-done((f32[64,1536]{1,0:T(8,128)S(1)}, f32[64,1536]{1,0:T(8,128)S(1)}, u32[]{:S(2)}, u32[]{:S(2)}) %collective-permute-start.33) | collective-permute-done | bytes 393248 | tf_op jit(solution)/shard_map/ppermute | solution.py:297
  110.3 4.2 %collective-permute-done.34.refs_1_ = f32[64,1536]{1,0:T(8,128)S(1)} collective-permute-done((f32[64,1536]{1,0:T(8,128)S(1)}, f32[64,1536]{1,0:T(8,128)S(1)}, u32[]{:S(2)}, u32[]{:S(2)}) %collective-permute-start.34) | collective-permute-done | bytes 393248 | tf_op jit(solution)/shard_map/ppermute | solution.py:297
  (63 shorter events, 24.9 us)
Async XLA Ops:
  1.7 12.9 %collective-permute-start.5 = (f32[64,1536]{1,0:T(8,128)S(1)}, f32[64,1536]{1,0:T(8,128)S(1)}, u32[]{:S(2)}, u32[]{:S(2)}) collective-permute-start(f32[64,1536]{1,0:T(8,128)S(1)} %constant_dynamic-slice_fusion.12), channel_id=1, source_target_pairs={{0,28},{4,24},{8,20},{12,16},{16,12},{20,8},{24,4},{28,0},{1,29},{... | collective-permute-start | bytes 1179656 | tf_op jit(solution)/shard_map/ppermute | solution.py:297
  7.8 15.3 %collective-permute-start.4 = (f32[64,1536]{1,0:T(8,128)S(1)}, f32[64,1536]{1,0:T(8,128)S(1)}, u32[]{:S(2)}, u32[]{:S(2)}) collective-permute-start(f32[64,1536]{1,0:T(8,128)S(1)} %get-tuple-element.72), channel_id=1, source_target_pairs={{0,20},{4,16},{8,28},{12,24},{16,4},{20,0},{24,12},{28,8},{1,21},{... | collective-permute-start | bytes 1179656 | tf_op jit(solution)/shard_map/ppermute | solution.py:297
  8.6 23.8 %collective-permute-start.3 = (f32[64,1536]{1,0:T(8,128)S(1)}, f32[64,1536]{1,0:T(8,128)S(1)}, u32[]{:S(2)}, u32[]{:S(2)}) collective-permute-start(f32[64,1536]{1,0:T(8,128)S(1)} %get-tuple-element.73), channel_id=1, source_target_pairs={{0,16},{4,20},{8,24},{12,28},{16,0},{20,4},{24,8},{28,12},{1,17},{... | collective-permute-start | bytes 1179656 | tf_op jit(solution)/shard_map/ppermute | solution.py:297
  10.2 22.2 %collective-permute-start.2 = (f32[64,1536]{1,0:T(8,128)S(1)}, f32[64,1536]{1,0:T(8,128)S(1)}, u32[]{:S(2)}, u32[]{:S(2)}) collective-permute-start(f32[64,1536]{1,0:T(8,128)S(1)} %get-tuple-element.74), channel_id=1, source_target_pairs={{0,12},{4,8},{8,4},{12,0},{16,28},{20,24},{24,20},{28,16},{1,13},{... | collective-permute-start | bytes 1179656 | tf_op jit(solution)/shard_map/ppermute | solution.py:297
  10.2 22.3 %collective-permute-start.1 = (f32[64,1536]{1,0:T(8,128)S(1)}, f32[64,1536]{1,0:T(8,128)S(1)}, u32[]{:S(2)}, u32[]{:S(2)}) collective-permute-start(f32[64,1536]{1,0:T(8,128)S(1)} %get-tuple-element.75), channel_id=1, source_target_pairs={{0,8},{4,12},{8,0},{12,4},{16,24},{20,28},{24,16},{28,20},{1,9},{5... | collective-permute-start | bytes 1179656 | tf_op jit(solution)/shard_map/ppermute | solution.py:297
  14.6 17.8 %collective-permute-start = (f32[64,1536]{1,0:T(8,128)S(1)}, f32[64,1536]{1,0:T(8,128)S(1)}, u32[]{:S(2)}, u32[]{:S(2)}) collective-permute-start(f32[64,1536]{1,0:T(8,128)S(1)} %get-tuple-element.76), channel_id=1, source_target_pairs={{0,4},{4,0},{8,12},{12,8},{16,20},{20,16},{24,28},{28,24},{1,5},{5... | collective-permute-start | bytes 1179656 | tf_op jit(solution)/shard_map/ppermute | solution.py:297
  23.1 17.0 %collective-permute-start.6 = (f32[64,1536]{1,0:T(8,128)S(1)}, f32[64,1536]{1,0:T(8,128)S(1)}, u32[]{:S(2)}, u32[]{:S(2)}) collective-permute-start(f32[64,1536]{1,0:T(8,128)S(1)} %get-tuple-element.71.refs_0_), channel_id=1, source_target_pairs={{0,24},{4,28},{8,16},{12,20},{16,8},{20,12},{24,0},{28,4},{1,25},{... | collective-permute-start | bytes 1179656 | tf_op jit(solution)/shard_map/ppermute | solution.py:297
  32.4 10.0 %collective-permute-start.7 = (f32[64,1536]{1,0:T(8,128)S(1)}, f32[64,1536]{1,0:T(8,128)S(1)}, u32[]{:S(2)}, u32[]{:S(2)}) collective-permute-start(f32[64,1536]{1,0:T(8,128)S(1)} %get-tuple-element.40), channel_id=1, source_target_pairs={{0,4},{4,0},{8,12},{12,8},{16,20},{20,16},{24,28},{28,24},{1,5},{5... | collective-permute-start | bytes 1179656 | tf_op jit(solution)/shard_map/ppermute | solution.py:297
  44.1 6.1 %collective-permute-start.11 = (f32[160,128]{1,0:T(8,128)S(1)}, f32[160,128]{1,0:T(8,128)S(1)}, u32[]{:S(2)}, u32[]{:S(2)}) collective-permute-start(f32[160,128]{1,0:T(8,128)S(1)} %get-tuple-element.78), channel_id=1, source_target_pairs={{0,24},{4,28},{8,16},{12,20},{16,8},{20,12},{24,0},{28,4},{1,25},{... | collective-permute-start | bytes 245768 | tf_op jit(solution)/shard_map/ppermute | solution.py:297
  47.4 6.8 %collective-permute-start.10 = (f32[160,128]{1,0:T(8,128)S(1)}, f32[160,128]{1,0:T(8,128)S(1)}, u32[]{:S(2)}, u32[]{:S(2)}) collective-permute-start(f32[160,128]{1,0:T(8,128)S(1)} %get-tuple-element.79), channel_id=1, source_target_pairs={{0,16},{4,20},{8,24},{12,28},{16,0},{20,4},{24,8},{28,12},{1,17},{... | collective-permute-start | bytes 245768 | tf_op jit(solution)/shard_map/ppermute | solution.py:297
  47.9 6.3 %collective-permute-start.9 = (f32[160,128]{1,0:T(8,128)S(1)}, f32[160,128]{1,0:T(8,128)S(1)}, u32[]{:S(2)}, u32[]{:S(2)}) collective-permute-start(f32[160,128]{1,0:T(8,128)S(1)} %get-tuple-element.80), channel_id=1, source_target_pairs={{0,8},{4,12},{8,0},{12,4},{16,24},{20,28},{24,16},{28,20},{1,9},{5... | collective-permute-start | bytes 245768 | tf_op jit(solution)/shard_map/ppermute | solution.py:297
  50.2 13.1 %collective-permute-start.15 = (f32[64,1536]{1,0:T(8,128)S(1)}, f32[64,1536]{1,0:T(8,128)S(1)}, u32[]{:S(2)}, u32[]{:S(2)}) collective-permute-start(f32[64,1536]{1,0:T(8,128)S(1)} %get-tuple-element.42), channel_id=1, source_target_pairs={{0,8},{4,12},{8,0},{12,4},{16,24},{20,28},{24,16},{28,20},{1,9},{5... | collective-permute-start | bytes 1179656 | tf_op jit(solution)/shard_map/ppermute | solution.py:297
  52.1 11.2 %collective-permute-start.16 = (f32[64,1536]{1,0:T(8,128)S(1)}, f32[64,1536]{1,0:T(8,128)S(1)}, u32[]{:S(2)}, u32[]{:S(2)}) collective-permute-start(f32[64,1536]{1,0:T(8,128)S(1)} %get-tuple-element.43), channel_id=1, source_target_pairs={{0,16},{4,20},{8,24},{12,28},{16,0},{20,4},{24,8},{28,12},{1,17},{... | collective-permute-start | bytes 1179656 | tf_op jit(solution)/shard_map/ppermute | solution.py:297
  54.2 6.7 %collective-permute-start.14 = (f32[160,128]{1,0:T(8,128)S(1)}, f32[160,128]{1,0:T(8,128)S(1)}, u32[]{:S(2)}, u32[]{:S(2)}) collective-permute-start(f32[160,128]{1,0:T(8,128)S(1)} %fusion), channel_id=1, source_target_pairs={{0,3},{1,2},{2,1},{3,0},{4,7},{5,6},{6,5},{7,4},{8,11},{9,10},{10,... | collective-permute-start | bytes 245768 | tf_op jit(solution)/shard_map/ppermute | solution.py:297
  63.3 5.9 %collective-permute-start.22 = (f32[160,128]{1,0:T(8,128)S(1)}, f32[160,128]{1,0:T(8,128)S(1)}, u32[]{:S(2)}, u32[]{:S(2)}) collective-permute-start(f32[160,128]{1,0:T(8,128)S(1)} %add_add_fusion.refs_0_), channel_id=1, source_target_pairs={{0,24},{4,28},{8,16},{12,20},{16,8},{20,12},{24,0},{28,4},{1,25},{... | collective-permute-start | bytes 245768 | tf_op jit(solution)/shard_map/ppermute | solution.py:297
  63.9 5.4 %collective-permute-start.20 = (f32[160,128]{1,0:T(8,128)S(1)}, f32[160,128]{1,0:T(8,128)S(1)}, u32[]{:S(2)}, u32[]{:S(2)}) collective-permute-start(f32[160,128]{1,0:T(8,128)S(1)} %add_add_fusion.refs_0_), channel_id=1, source_target_pairs={{0,16},{4,20},{8,24},{12,28},{16,0},{20,4},{24,8},{28,12},{1,17},{... | collective-permute-start | bytes 245768 | tf_op jit(solution)/shard_map/ppermute | solution.py:297
  70.3 23.6 %collective-permute-start.26 = (f32[2,64,1536]{2,1,0:T(8,128)S(1)}, f32[2,64,1536]{2,1,0:T(8,128)S(1)}, u32[]{:S(2)}, u32[]{:S(2)}) collective-permute-start(f32[2,64,1536]{2,1,0:T(8,128)S(1)} %pad_maximum_fusion), channel_id=1, source_target_pairs={{0,24},{4,28},{8,16},{12,20},{16,8},{20,12},{24,0},{28,4},{1,25},{... | collective-permute-start | bytes 2359304 | tf_op jit(solution)/shard_map/ppermute | solution.py:297
  73.6 23.2 %collective-permute-start.24 = (f32[64,1536]{1,0:T(8,128)S(1)}, f32[64,1536]{1,0:T(8,128)S(1)}, u32[]{:S(2)}, u32[]{:S(2)}) collective-permute-start(f32[64,1536]{1,0:T(8,128)S(1)} %get-tuple-element.50), channel_id=1, source_target_pairs={{0,12},{4,8},{8,4},{12,0},{16,28},{20,24},{24,20},{28,16},{1,13},{... | collective-permute-start | bytes 1179656 | tf_op jit(solution)/shard_map/ppermute | solution.py:297
  74.3 23.8 %collective-permute-start.25 = (f32[64,1536]{1,0:T(8,128)S(1)}, f32[64,1536]{1,0:T(8,128)S(1)}, u32[]{:S(2)}, u32[]{:S(2)}) collective-permute-start(f32[64,1536]{1,0:T(8,128)S(1)} %get-tuple-element.52), channel_id=1, source_target_pairs={{0,20},{4,16},{8,28},{12,24},{16,4},{20,0},{24,12},{28,8},{1,21},{... | collective-permute-start | bytes 1179656 | tf_op jit(solution)/shard_map/ppermute | solution.py:297
  94.2 12.3 %collective-permute-start.33 = (f32[64,1536]{1,0:T(8,128)S(1)}, f32[64,1536]{1,0:T(8,128)S(1)}, u32[]{:S(2)}, u32[]{:S(2)}) collective-permute-start(f32[64,1536]{1,0:T(8,128)S(1)} %get-tuple-element.62), channel_id=1, source_target_pairs={{0,16},{4,20},{8,24},{12,28},{16,0},{20,4},{24,8},{28,12},{1,17},{... | collective-permute-start | bytes 1179656 | tf_op jit(solution)/shard_map/ppermute | solution.py:297
  95.1 12.0 %collective-permute-start.32 = (f32[64,1536]{1,0:T(8,128)S(1)}, f32[64,1536]{1,0:T(8,128)S(1)}, u32[]{:S(2)}, u32[]{:S(2)}) collective-permute-start(f32[64,1536]{1,0:T(8,128)S(1)} %get-tuple-element.54), channel_id=1, source_target_pairs={{0,8},{4,12},{8,0},{12,4},{16,24},{20,28},{24,16},{28,20},{1,9},{5... | collective-permute-start | bytes 1179656 | tf_op jit(solution)/shard_map/ppermute | solution.py:297
  100.2 6.9 %collective-permute-start.28 = (f32[64,768]{1,0:T(8,128)S(1)}, f32[64,768]{1,0:T(8,128)S(1)}, u32[]{:S(2)}, u32[]{:S(2)}) collective-permute-start(f32[64,768]{1,0:T(8,128)S(1)} %get-tuple-element.58), channel_id=1, source_target_pairs={{0,4},{4,0},{8,12},{12,8},{16,20},{20,16},{24,28},{28,24},{1,5},{5... | collective-permute-start | bytes 589832 | tf_op jit(solution)/shard_map/ppermute | solution.py:297
  100.8 13.7 %collective-permute-start.34 = (f32[64,1536]{1,0:T(8,128)S(1)}, f32[64,1536]{1,0:T(8,128)S(1)}, u32[]{:S(2)}, u32[]{:S(2)}) collective-permute-start(f32[64,1536]{1,0:T(8,128)S(1)} %get-tuple-element.63), channel_id=1, source_target_pairs={{0,12},{4,8},{8,4},{12,0},{16,28},{20,24},{24,20},{28,16},{1,13},{... | collective-permute-start | bytes 1179656 | tf_op jit(solution)/shard_map/ppermute | solution.py:297
  101.9 13.0 %collective-permute-start.35 = (f32[64,1536]{1,0:T(8,128)S(1)}, f32[64,1536]{1,0:T(8,128)S(1)}, u32[]{:S(2)}, u32[]{:S(2)}) collective-permute-start(f32[64,1536]{1,0:T(8,128)S(1)} %get-tuple-element.64), channel_id=1, source_target_pairs={{0,20},{4,16},{8,28},{12,24},{16,4},{20,0},{24,12},{28,8},{1,21},{... | collective-permute-start | bytes 1179656 | tf_op jit(solution)/shard_map/ppermute | solution.py:297
  (12 other events, 32.6 us)
